TPU v7x, 32 devices: a whole 2x2x4 slice. The times are simulated.
32 devices in a mesh: dp: 8 (over y, x, core), mp: 4 (over z).
Axes of the slice: x: 2, y: 2, z: 4, core: 2. Of those that a mesh axis runs over, the one named last changes fastest.
Arguments:
- tokens: bfloat16 [16, 1024, 1024], P('dp'), may hold values from -6 to 6
- memory: bfloat16 [16, 1024, 1024], P('dp'), may hold values from -6 to 6
- target_lengths: int32 [16], P('dp'), may hold values from 128 to 1024, as said below
- source_lengths: int32 [16], P('dp'), may hold values from 128 to 1024, as said below
- cotangent: bfloat16 [16, 1024, 1024], P('dp'), may hold values from -6 to 6
- norm_gain: bfloat16 [3, 1024], replicated, may hold values from 0.5 to 1.5
- norm_bias: bfloat16 [3, 1024], replicated, may hold values from -1 to 1
- self_in: bfloat16 [3, 1024, 1024], P(None, None, 'mp'), may hold values from -0.1875 to 0.1875
- self_in_bias: bfloat16 [2, 1024], P(None, 'mp'), may hold values from -1 to 1
- self_out: bfloat16 [1024, 1024], P('mp'), may hold values from -1.5 to 1.5
- cross_query: bfloat16 [1024, 1024], P(None, 'mp'), may hold values from -0.1875 to 0.1875
- cross_kv: bfloat16 [2, 1024, 1024], P(None, None, 'mp'), may hold values from -0.1875 to 0.1875
- cross_bias: bfloat16 [2, 1024], P(None, 'mp'), may hold values from -1 to 1
- cross_out: bfloat16 [1024, 1024], P('mp'), may hold values from -1.5 to 1.5
- out_bias: bfloat16 [3, 1024], replicated, may hold values from -1 to 1
- ffn_up: bfloat16 [1024, 4096], P(None, 'mp'), may hold values from -0.1875 to 0.1875
- ffn_up_bias: bfloat16 [4096], P('mp'), may hold values from -1 to 1
- ffn_down: bfloat16 [4096, 1024], P('mp'), may hold values from -0.09375 to 0.09375
Outputs:
- output: bfloat16 [16, 1024, 1024], P('dp')
- tokens_grad: float32 [16, 1024, 1024], P('dp')
- memory_grad: float32 [16, 1024, 1024], P('dp')
- norm_gain_grad: float32 [3, 1024], replicated
- norm_bias_grad: float32 [3, 1024], replicated
- self_in_grad: float32 [3, 1024, 1024], P(None, None, 'mp')
- self_in_bias_grad: float32 [2, 1024], P(None, 'mp')
- self_out_grad: float32 [1024, 1024], P('mp')
- cross_query_grad: float32 [1024, 1024], P(None, 'mp')
- cross_kv_grad: float32 [2, 1024, 1024], P(None, None, 'mp')
- cross_bias_grad: float32 [2, 1024], P(None, 'mp')
- cross_out_grad: float32 [1024, 1024], P('mp')
- out_bias_grad: float32 [3, 1024], replicated
- ffn_up_grad: float32 [1024, 4096], P(None, 'mp')
- ffn_up_bias_grad: float32 [4096], P('mp')
- ffn_down_grad: float32 [4096, 1024], P('mp')
Inputs may be any that keep to these rules, and one draw needn't show every extreme that they name: `target_lengths`: one row has exactly 1024. `source_lengths`: one row has exactly 1024.
All inputs are finite; a program needn't handle non-finite values.
Results may differ from a plain program's by a relative error of at most 0.024.
Values may be sent and summed in bfloat16 or wider, within the bound.
No kernel may reach another device: no remote copies, remote signals or barrier semaphores. Data moves between devices by JAX's collectives and lax.ppermute only.
A program may use at most 320 MiB of HBM per device.

v0:
```python
import jax
import jax.numpy as jnp
from jax import lax
from jax.sharding import PartitionSpec as P

HEAD_DIM = 64


neg_fill = -1000000000.0
eps_norm = 1e-05


def to_low(value):
    return value.astype(jnp.bfloat16)


def norm_layer(values, gain, shift):
    centre = jnp.mean(values, axis=-1, keepdims=True)
    offset = values - centre
    spread = jnp.mean(offset * offset, axis=-1, keepdims=True)
    return offset * lax.rsqrt(spread + eps_norm) * gain + shift


def activation(values):
    return jax.nn.gelu(values, approximate=True)


def project(inputs, weight):
    return jnp.einsum("bld,de->ble", inputs, weight, preferred_element_type=jnp.float32)


def project_back(grads, weight):
    return jnp.einsum("ble,de->bld", grads, weight, preferred_element_type=jnp.float32)


def outer_sum(inputs, grads):
    return jnp.einsum("bld,ble->de", inputs, grads, preferred_element_type=jnp.float32)


def split_heads(values):
    return values.reshape(values.shape[0], values.shape[1], -1, HEAD_DIM)


def join_heads(values):
    return values.reshape(values.shape[0], values.shape[1], -1)


def row_total(values):
    return jnp.sum(values, axis=(0, 1), dtype=jnp.float32)


def score_block(query, keys, allowed):
    scores = jnp.einsum(
        "bqhe,bkhe->bhqk", query, keys, preferred_element_type=jnp.float32
    ) * HEAD_DIM ** (-0.5)
    return jnp.where(allowed[:, None], scores, neg_fill)


def attend_forward(query, keys, values, allowed):
    scores = score_block(query, keys, allowed)
    highest = jnp.max(scores, axis=-1, keepdims=True)
    weights = jnp.exp(scores - highest)
    total = jnp.sum(weights, axis=-1, keepdims=True)
    mixed = jnp.einsum(
        "bhqk,bkhe->bqhe", to_low(weights / total), values, preferred_element_type=jnp.float32
    )
    return (to_low(join_heads(mixed)), highest + jnp.log(total))


def attend_backward(query, keys, values, allowed, log_total, grad_mixed):
    probs = jnp.exp(score_block(query, keys, allowed) - log_total)
    grad_probs = jnp.einsum(
        "bqhe,bkhe->bhqk", grad_mixed, values, preferred_element_type=jnp.float32
    )
    centre = jnp.sum(grad_probs * probs, axis=-1, keepdims=True)
    grad_scores = to_low(probs * (grad_probs - centre))
    factor = HEAD_DIM ** (-0.5)
    grad_query = (
        jnp.einsum("bhqk,bkhe->bqhe", grad_scores, keys, preferred_element_type=jnp.float32)
        * factor
    )
    grad_keys = (
        jnp.einsum("bhqk,bqhe->bkhe", grad_scores, query, preferred_element_type=jnp.float32)
        * factor
    )
    grad_values = jnp.einsum(
        "bhqk,bqhe->bkhe", to_low(probs), grad_mixed, preferred_element_type=jnp.float32
    )
    return (
        to_low(join_heads(grad_query)),
        to_low(join_heads(grad_keys)),
        to_low(join_heads(grad_values)),
    )


def branch_input(resid, gain, shift):
    normed, pullback = jax.vjp(
        norm_layer, resid, gain.astype(jnp.float32), shift.astype(jnp.float32)
    )
    low_normed = to_low(normed)
    return (low_normed, pullback)


def branch_output(partial_value, shift):
    return lax.psum(partial_value, "mp") + shift.astype(jnp.float32)


def grad_entry(grad_resid):
    low_grad = to_low(grad_resid)
    bias_grad = row_total(low_grad)
    return (low_grad, bias_grad)


def grad_norm_input(partial_value):
    return lax.psum(partial_value.astype(jnp.bfloat16), "mp").astype(jnp.float32)


def finish_small(gain_grad, shift_grad, bias_grad):
    return (gain_grad, shift_grad, bias_grad)


def shards(
    tokens,
    memory,
    target_lengths,
    source_lengths,
    cotangent,
    norm_gain,
    norm_bias,
    self_in,
    self_in_bias,
    self_out,
    cross_query,
    cross_kv,
    cross_bias,
    cross_out,
    out_bias,
    ffn_up,
    ffn_up_bias,
    ffn_down,
):
    batch, length, width = tokens.shape
    source = memory.shape[1]
    resid = tokens.astype(jnp.float32)
    grad_out = cotangent.astype(jnp.float32)
    places = jnp.arange(length, dtype=jnp.int32)
    source_places = jnp.arange(source, dtype=jnp.int32)
    causal = (places[None, None, :] <= places[None, :, None]) & (
        places[None, None, :] < target_lengths[:, None, None]
    )
    crossing = jnp.broadcast_to(
        source_places[None, None, :] < source_lengths[:, None, None], (batch, length, source)
    )
    normed_one, pull_one = branch_input(resid, norm_gain[0], norm_bias[0])
    query_one = split_heads(to_low(project(normed_one, self_in[0]) + self_in_bias[0]))
    keys_one = split_heads(to_low(project(normed_one, self_in[1])))
    values_one = split_heads(to_low(project(normed_one, self_in[2]) + self_in_bias[1]))
    mixed_one, total_one = attend_forward(query_one, keys_one, values_one, causal)
    first = resid + branch_output(project(mixed_one, self_out), out_bias[0])
    normed_two, pull_two = branch_input(first, norm_gain[1], norm_bias[1])
    query_two = split_heads(to_low(project(normed_two, cross_query) + cross_bias[0]))
    keys_two = split_heads(to_low(project(memory, cross_kv[0])))
    values_two = split_heads(to_low(project(memory, cross_kv[1]) + cross_bias[1]))
    mixed_two, total_two = attend_forward(query_two, keys_two, values_two, crossing)
    second = first + branch_output(project(mixed_two, cross_out), out_bias[1])
    normed_three, pull_three = branch_input(second, norm_gain[2], norm_bias[2])
    hidden_pre = project(normed_three, ffn_up) + ffn_up_bias
    hidden, pull_gelu = jax.vjp(activation, hidden_pre)
    hidden_low = to_low(hidden)
    final = second + branch_output(project(hidden_low, ffn_down), out_bias[2])
    entry_three, bias_three = grad_entry(grad_out)
    ffn_down_grad = outer_sum(hidden_low, entry_three)
    grad_pre = to_low(pull_gelu(project_back(entry_three, ffn_down))[0])
    ffn_up_grad = outer_sum(normed_three, grad_pre)
    ffn_up_bias_grad = row_total(grad_pre)
    grad_normed = grad_norm_input(project_back(grad_pre, ffn_up))
    grad_second, gain_three, shift_three = pull_three(grad_normed)
    grad_second = grad_second + grad_out
    gain_three, shift_three, bias_three = finish_small(gain_three, shift_three, bias_three)
    entry_two, bias_two = grad_entry(grad_second)
    cross_out_grad = outer_sum(mixed_two, entry_two)
    grad_mixed = split_heads(to_low(project_back(entry_two, cross_out)))
    grad_query, grad_keys, grad_values = attend_backward(
        query_two, keys_two, values_two, crossing, total_two, grad_mixed
    )
    cross_bias_grad = jnp.stack([row_total(grad_query), row_total(grad_values)])
    cross_query_grad = outer_sum(normed_two, grad_query)
    cross_kv_grad = jnp.stack([outer_sum(memory, grad_keys), outer_sum(memory, grad_values)])
    memory_part = project_back(grad_keys, cross_kv[0]) + project_back(grad_values, cross_kv[1])
    memory_grad = lax.psum(memory_part.astype(jnp.bfloat16), "mp").astype(jnp.float32)
    grad_normed = grad_norm_input(project_back(grad_query, cross_query))
    grad_first, gain_two, shift_two = pull_two(grad_normed)
    grad_first = grad_first + grad_second
    gain_two, shift_two, bias_two = finish_small(gain_two, shift_two, bias_two)
    entry_one, bias_one = grad_entry(grad_first)
    self_out_grad = outer_sum(mixed_one, entry_one)
    grad_mixed = split_heads(to_low(project_back(entry_one, self_out)))
    grad_query, grad_keys, grad_values = attend_backward(
        query_one, keys_one, values_one, causal, total_one, grad_mixed
    )
    self_in_bias_grad = jnp.stack([row_total(grad_query), row_total(grad_values)])
    self_in_grad = jnp.stack(
        [
            outer_sum(normed_one, grad_query),
            outer_sum(normed_one, grad_keys),
            outer_sum(normed_one, grad_values),
        ]
    )
    input_part = (
        project_back(grad_query, self_in[0])
        + project_back(grad_keys, self_in[1])
        + project_back(grad_values, self_in[2])
    )
    grad_normed = grad_norm_input(input_part)
    tokens_grad, gain_one, shift_one = pull_one(grad_normed)
    tokens_grad = tokens_grad + grad_first
    gain_one, shift_one, bias_one = finish_small(gain_one, shift_one, bias_one)
    (
        self_in_grad,
        self_in_bias_grad,
        self_out_grad,
        cross_query_grad,
        cross_kv_grad,
        cross_bias_grad,
        cross_out_grad,
        ffn_up_grad,
        ffn_up_bias_grad,
        ffn_down_grad,
        gain_one,
        gain_two,
        gain_three,
        shift_one,
        shift_two,
        shift_three,
        bias_one,
        bias_two,
        bias_three,
    ) = (
        lax.psum(self_in_grad.astype(jnp.bfloat16), "dp").astype(jnp.float32),
        lax.psum(self_in_bias_grad.astype(jnp.bfloat16), "dp").astype(jnp.float32),
        lax.psum(self_out_grad.astype(jnp.bfloat16), "dp").astype(jnp.float32),
        lax.psum(cross_query_grad.astype(jnp.bfloat16), "dp").astype(jnp.float32),
        lax.psum(cross_kv_grad.astype(jnp.bfloat16), "dp").astype(jnp.float32),
        lax.psum(cross_bias_grad.astype(jnp.bfloat16), "dp").astype(jnp.float32),
        lax.psum(cross_out_grad.astype(jnp.bfloat16), "dp").astype(jnp.float32),
        lax.psum(ffn_up_grad.astype(jnp.bfloat16), "dp").astype(jnp.float32),
        lax.psum(ffn_up_bias_grad.astype(jnp.bfloat16), "dp").astype(jnp.float32),
        lax.psum(ffn_down_grad.astype(jnp.bfloat16), "dp").astype(jnp.float32),
        lax.psum(gain_one.astype(jnp.bfloat16), "dp").astype(jnp.float32),
        lax.psum(gain_two.astype(jnp.bfloat16), "dp").astype(jnp.float32),
        lax.psum(gain_three.astype(jnp.bfloat16), "dp").astype(jnp.float32),
        lax.psum(shift_one.astype(jnp.bfloat16), "dp").astype(jnp.float32),
        lax.psum(shift_two.astype(jnp.bfloat16), "dp").astype(jnp.float32),
        lax.psum(shift_three.astype(jnp.bfloat16), "dp").astype(jnp.float32),
        lax.psum(bias_one.astype(jnp.bfloat16), "dp").astype(jnp.float32),
        lax.psum(bias_two.astype(jnp.bfloat16), "dp").astype(jnp.float32),
        lax.psum(bias_three.astype(jnp.bfloat16), "dp").astype(jnp.float32),
    )
    return (
        to_low(final),
        tokens_grad,
        memory_grad,
        jnp.stack([gain_one, gain_two, gain_three]),
        jnp.stack([shift_one, shift_two, shift_three]),
        self_in_grad,
        self_in_bias_grad,
        self_out_grad,
        cross_query_grad,
        cross_kv_grad,
        cross_bias_grad,
        cross_out_grad,
        jnp.stack([bias_one, bias_two, bias_three]),
        ffn_up_grad,
        ffn_up_bias_grad,
        ffn_down_grad,
    )


def solution(mesh):
    placed = (
        P("dp", None, None),
        P("dp", None, None),
        P("dp"),
        P("dp"),
        P("dp", None, None),
        P(),
        P(),
        P(None, None, "mp"),
        P(None, "mp"),
        P("mp", None),
        P(None, "mp"),
        P(None, None, "mp"),
        P(None, "mp"),
        P("mp", None),
        P(),
        P(None, "mp"),
        P("mp"),
        P("mp", None),
    )
    return jax.shard_map(
        shards,
        mesh=mesh,
        in_specs=placed,
        out_specs=(
            P("dp", None, None),
            P("dp", None, None),
            P("dp", None, None),
            P(),
            P(),
            P(None, None, "mp"),
            P(None, "mp"),
            P("mp", None),
            P(None, "mp"),
            P(None, None, "mp"),
            P(None, "mp"),
            P("mp", None),
            P(),
            P(None, "mp"),
            P("mp"),
            P("mp", None),
        ),
        check_vma=False,
    )
```

profile of v0, /device:TPU:0, one launch (start us, length us, event | category | flops | bytes accessed | tf_op | source)
XLA Modules:
  0.0 2059.2 jit_solution(15494911709358077210)
XLA Ops:
  25.9 13.8 fusion.115
  39.7 13.1 fusion
  52.8 13.9 fusion.54
  81.8 284.3 %all-reduce.11.cloned.1.call-done = f32[2,1024,1024]{2,1,0:T(8,128)} async-done(((f32[2,1024,1024]{2,1,0:T(8,128)}), f32[2,1024,1024]{2,1,0:T(8,128)}) %all-reduce.11.cloned.1.call-update) | async-done | bytes 8388624 | tf_op jit(solution)/shard_map/psum | solution.py:105
  375.6 13.8 fusion.116
  389.5 13.1 fusion.1
  402.6 13.7 fusion.53
  422.1 289.9 %all-reduce.13.cloned.1.call-done = f32[2,1024,1024]{2,1,0:T(8,128)} async-done(((f32[2,1024,1024]{2,1,0:T(8,128)}), f32[2,1024,1024]{2,1,0:T(8,128)}) %all-reduce.13.cloned.1.call-update) | async-done | bytes 8388624 | tf_op jit(solution)/shard_map/psum | solution.py:105
  722.2 14.6 multiply_reduce_fusion.2
  762.5 12.3 fusion.42
  797.7 118.9 %all-reduce.17.cloned.1.call-done = bf16[2,1024,1024]{2,1,0:T(8,128)(2,1)} async-done(((bf16[2,1024,1024]{2,1,0:T(8,128)(2,1)}), bf16[2,1024,1024]{2,1,0:T(8,128)(2,1)}) %all-reduce.17.cloned.1.call-update) | async-done | bytes 4194320 | tf_op jit(solution)/shard_map/psum | solution.py:115
  922.2 286.7 %all-reduce.15.cloned.1.call-done = f32[2,1024,1024]{2,1,0:T(8,128)} async-done(((f32[2,1024,1024]{2,1,0:T(8,128)}), f32[2,1024,1024]{2,1,0:T(8,128)}) %all-reduce.15.cloned.1.call-update) | async-done | bytes 8388624 | tf_op jit(solution)/shard_map/psum | solution.py:105
  1208.9 11.7 fusion.26
  1230.8 22.1 %multiply_reduce_fusion.1 = (f32[2,4,1024]{2,1,0:T(4,128)S(1)}, f32[2,4,1024,1024]{2,3,1,0:T(8,128)}) fusion(f32[2,4,1024,1024]{2,3,1,0:T(8,128)} %get-tuple-element.87, f32[2,4,1024]{2,1,0:T(4,128)S(1)} %bitcast.273, bf16[2,1024,4,64]{1,3,2,0:T(8,128)(2,1)S(1)} %bitcast.256, bf16[2,1024,4,64]{1,3,2,0:T(8,128)(2,1)S(1)} %bitcast.279), kind=kOutput, calls=%fused_computation.3 | convolution fusion | flops 1098899456 | bytes 69271552 | tf_op jit(solution)/shard_map/bqhe,bkhe->bhqk/dot_general | solution.py:72
  1252.9 28.1 %multiply_convert_fusion.1 = bf16[2,4,1024,1024]{2,3,1,0:T(8,128)(2,1)} fusion(f32[2,4,1024,1024]{2,3,1,0:T(8,128)} %get-tuple-element.89, f32[2,4,1024,1024]{2,3,1,0:T(8,128)} %get-tuple-element.87, f32[2,4,1024]{2,1,0:T(4,128)S(1)} %get-tuple-element.88, f32[2,4,1024]{2,1,0:T(4,128)S(1)} %bitcast.274), kind=kLoop, calls=%fused_computation.2 | loop fusion | flops 33554432 | bytes 83951616 | tf_op jit(solution)/shard_map/convert_element_type | solution.py:14
  1293.9 15.5 bitcast_reduce_fusion
  1337.6 110.3 %all-reduce.19.cloned.1.call-done = bf16[2,1024,1024]{2,1,0:T(8,128)(2,1)} async-done(((bf16[2,1024,1024]{2,1,0:T(8,128)(2,1)}), bf16[2,1024,1024]{2,1,0:T(8,128)(2,1)}) %all-reduce.19.cloned.1.call-update) | async-done | bytes 4194320 | tf_op jit(solution)/shard_map/psum | solution.py:115
  1476.6 14.5 bitcast_reduce_fusion.1
  1491.1 22.0 %multiply_reduce_fusion = (f32[2,4,1024]{2,1,0:T(4,128)S(1)}, f32[2,4,1024,1024]{2,3,1,0:T(8,128)}) fusion(f32[2,4,1024,1024]{2,3,1,0:T(8,128)} %get-tuple-element.85, f32[2,4,1024]{2,1,0:T(4,128)S(1)} %bitcast.271, bf16[2,1024,4,64]{1,3,2,0:T(8,128)(2,1)S(1)} %bitcast.245, bf16[2,1024,4,64]{1,3,2,0:T(8,128)(2,1)S(1)} %bitcast.277), kind=kOutput, calls=%fused_computation.1 | convolution fusion | flops 1098899456 | bytes 69271552 | tf_op jit(solution)/shard_map/bqhe,bkhe->bhqk/dot_general | solution.py:72
  1513.1 28.3 %multiply_convert_fusion = bf16[2,4,1024,1024]{2,3,1,0:T(8,128)(2,1)} fusion(f32[2,4,1024,1024]{2,3,1,0:T(8,128)} %get-tuple-element.91, f32[2,4,1024,1024]{2,3,1,0:T(8,128)} %get-tuple-element.85, f32[2,4,1024]{2,1,0:T(4,128)S(1)} %get-tuple-element.90, f32[2,4,1024]{2,1,0:T(4,128)S(1)} %bitcast.272), kind=kLoop, calls=%fused_computation | loop fusion | flops 33554432 | bytes 83951616 | tf_op jit(solution)/shard_map/convert_element_type | solution.py:14
  1541.4 12.0 multiply_convert_fusion.4
  1585.3 114.9 %all-reduce.21.cloned.1.call-done = (bf16[2,1024,256]{1,2,0:T(8,128)(2,1)}, bf16[3,1024,256]{2,1,0:T(8,128)(2,1)}, bf16[256,1024]{1,0:T(8,128)(2,1)}, bf16[1024,...) async-done(((bf16[2,1024,256]{1,2,0:T(8,128)(2,1)}, bf16[3,1024,256]{2,1,0:T(8,128)(2,1)}, ...) | async-done | bytes 8388624 | tf_op jit(solution)/shard_map/psum | solution.py:243
  1718.0 277.5 %all-reduce.23.cloned.1.call-done = (bf16[2,1024,1024]{2,1,0:T(8,128)(2,1)}, bf16[2,1024,1024]{2,1,0:T(8,128)(2,1)}) async-done(((bf16[2,1024,1024]{2,1,0:T(8,128)(2,1)}, bf16[2,1024,1024]{2,1,0:T(8,128)(2,1)}), (bf16[2,1024,1024]{2,1,0:T(8,128)(2,1)}, bf16[2,1024,1024]{2,1,0:T(8,128)(2,1)})) %all-reduce.23.cloned.1.call-update) | async-done | bytes 8388624 | tf_op jit(solution)/shard_map/psum | solution.py:115
  2010.2 24.4 %all-reduce = (bf16[1,1024]{1,0:T(2,128)(2,1)S(1)}, bf16[1,1024]{1,0:T(2,128)(2,1)S(1)}, bf16[1,1024]{1,0:T(2,128)(2,1)S(1)}, bf16[1,1024]{1,0:T(2,128)(2,1)S(1)...) all-reduce(bf16[1,1024]{1,0:T(2,128)(2,1)S(1)} %stack.108, ...), channel_id=1, replica_groups=mesh['dp'=8,'mp'=4] {'dp'}, use_global_device_ids=true, to_apply=%region_30.31 | all-reduce | flops 11264 | bytes 45056 | tf_op jit(solution)/shard_map/psum | solution.py:251
  (297 shorter events, 273.9 us)
Async XLA Ops:
  7.2 736.3 %copy-start = (bf16[1024,1024]{1,0:T(8,128)(2,1)S(1)}, bf16[1024,1024]{1,0:T(8,128)(2,1)}, u32[]{:S(2)}) copy-start(bf16[1024,1024]{1,0:T(8,128)(2,1)} %param.35) | copy-start | bytes 6291460
  7.2 358.9 %all-reduce.11.cloned.1.call-start = ((), (), s32[]{:S(2)}) async-start(), calls=%async_computation | async-start | bytes 16777216 | tf_op jit(solution)/shard_map/psum | solution.py:105
  16.3 356.8 %copy-start.61 = (f32[1,1024]{1,0:T(1,128)}, f32[1,1024]{1,0:T(1,128)S(1)}, u32[]{:S(2)}) copy-start(f32[1,1024]{1,0:T(1,128)S(1)} %get-tuple-element.76) | copy-start | bytes 12292
  17.0 356.2 %copy-start.75 = (f32[1,1024]{1,0:T(1,128)}, f32[1,1024]{1,0:T(1,128)S(1)}, u32[]{:S(2)}) copy-start(f32[1,1024]{1,0:T(1,128)S(1)} %get-tuple-element.79) | copy-start | bytes 12292
  24.7 28.1 %copy-start.38 = (bf16[2,1024,256]{1,2,0:T(8,128)(2,1)}, bf16[2,1024,256]{1,2,0:T(8,128)(2,1)S(1)}, u32[]{:S(2)}) copy-start(bf16[2,1024,256]{1,2,0:T(8,128)(2,1)S(1)} %add_convert_fusion.8) | copy-start | bytes 3145732
  52.8 14.9 copy-start.34
  72.5 639.6 %all-reduce.13.cloned.1.call-start = ((), (), s32[]{:S(2)}) async-start(), calls=%async_computation.1 | async-start | bytes 16777216 | tf_op jit(solution)/shard_map/psum | solution.py:105
  76.9 298.8 %copy-start.15 = (bf16[2,1024,256]{1,2,0:T(8,128)(2,1)}, bf16[2,1024,256]{1,2,0:T(8,128)(2,1)S(1)}, u32[]{:S(2)}) copy-start(bf16[2,1024,256]{1,2,0:T(8,128)(2,1)S(1)} %convolution_convert_fusion.4) | copy-start | bytes 3145732
  373.1 16.3 copy-start.59
  373.1 16.3 copy-start.53
  402.6 14.7 copy-start.44
  422.1 494.5 %all-reduce.17.cloned.1.call-start = ((), (), s32[]{:S(2)}) async-start(), calls=%async_computation.3 | async-start | bytes 8388608 | tf_op jit(solution)/shard_map/psum | solution.py:115
  722.2 14.6 copy-start.77
  762.4 446.5 %all-reduce.15.cloned.1.call-start = ((), (), s32[]{:S(2)}) async-start(), calls=%async_computation.2 | async-start | bytes 16777216 | tf_op jit(solution)/shard_map/psum | solution.py:105
  774.8 673.2 %all-reduce.19.cloned.1.call-start = ((), (), s32[]{:S(2)}) async-start(), calls=%async_computation.4 | async-start | bytes 8388608 | tf_op jit(solution)/shard_map/psum | solution.py:115
  797.7 411.3 %copy-start.68 = (f32[1,1024]{1,0:T(1,128)S(1)}, f32[1,1024]{1,0:T(1,128)}, u32[]{:S(2)}) copy-start(f32[1,1024]{1,0:T(1,128)} %get-tuple-element.71) | copy-start | bytes 12292
  1252.8 28.1 %copy-start.16 = (bf16[2,1024,256]{1,2,0:T(8,128)(2,1)S(1)}, bf16[2,1024,256]{1,2,0:T(8,128)(2,1)}, u32[]{:S(2)}) copy-start(bf16[2,1024,256]{1,2,0:T(8,128)(2,1)} %copy-done.15) | copy-start | bytes 3145732
  1293.8 20.1 copy-start.14
  1293.8 406.4 %all-reduce.21.cloned.1.call-start = ((), (), s32[]{:S(2)}) async-start(), calls=%async_computation.5 | async-start | bytes 16777216 | tf_op jit(solution)/shard_map/psum | solution.py:243
  1337.6 116.3 %copy-start.60 = (f32[2,1024]{1,0:T(2,128)S(1)}, f32[2,1024]{1,0:T(2,128)}, u32[]{:S(2)}) copy-start(f32[2,1024]{1,0:T(2,128)} %copy-done.59) | copy-start | bytes 24580
  1513.1 28.3 %copy-start.20 = (bf16[2,1024,256]{1,2,0:T(8,128)(2,1)S(1)}, bf16[2,1024,256]{1,2,0:T(8,128)(2,1)}, u32[]{:S(2)}) copy-start(bf16[2,1024,256]{1,2,0:T(8,128)(2,1)} %copy-done.19) | copy-start | bytes 3145732
  1572.1 423.4 %all-reduce.23.cloned.1.call-start = ((), (), s32[]{:S(2)}) async-start(), calls=%async_computation.6 | async-start | bytes 16777216 | tf_op jit(solution)/shard_map/psum | solution.py:115
  1715.5 287.3 %copy-start.56 = (f32[2,1024]{1,0:T(2,128)S(1)}, f32[2,1024]{1,0:T(2,128)}, u32[]{:S(2)}) copy-start(f32[2,1024]{1,0:T(2,128)} %copy-done.55) | copy-start | bytes 24580
  2036.4 15.4 copy-start.1
  (73 other events, 535.1 us)
Sparse Core Ops, SparseCore 0:
  72.6 293.5 all-reduce.10
  422.2 289.8 all-reduce.12
  762.6 153.9 all-reduce.16
  919.1 289.8 all-reduce.14
  1293.9 153.9 all-reduce.18
  1572.2 127.9 all-reduce.20
  1703.6 291.8 all-reduce.22
where the time goes:
time: 2070 us; the launch traced here: 2060 us
  waiting for transfers between devices  1480 us (71%)
  matrix products  300 us (14%)
  other arithmetic  224 us (11%)
  blocking collectives  24.4 us (1%)
    psum x3, waiting for transfers between devices, branch_output(): return lax.psum(partial_value, 'mp') + shift.astype(jnp.float32)  861 us
    psum x3, waiting for transfers between devices, grad_norm_input(): lax.psum(partial_value.astype(jnp.bfloat16), 'mp').astype(jnp.float32)  507 us
    psum x1, waiting for transfers between devices, shards(): lax.psum(cross_kv_grad.astype(jnp.bfloat16), 'dp').astype(jnp.float32)  115 us
    convert_element_type x2, other arithmetic, to_low(): return value.astype(jnp.bfloat16)  56.3 us
    dot_general x10, matrix products, outer_sum(): jnp.einsum('bld,ble->de', inputs, grads, preferred_element_type=jnp.float32)  47.9 us
    dot_general x10, matrix products, project(): jnp.einsum('bld,de->ble', inputs, weight, preferred_element_type=jnp.floa...  46.8 us
    reduce_sum x7, other arithmetic, norm_layer(): return offset * lax.rsqrt(spread + eps_norm) * gain + shift  45.5 us
    dot_general x2, matrix products, attend_backward(): jnp.einsum('bqhe,bkhe->bhqk', grad_mixed, values, preferred_element_type=...  44.1 us
  transfers between devices with their start and end apart: 7, of which 7 were waited for; matrix products, arithmetic and copies ran while one was open for 6% of the time, Pallas kernels for 0%

commit v1 on v0

v1 whole, which is shorter than its diff:
```python
import functools

import jax
import jax.numpy as jnp
from jax import lax
from jax.experimental import pallas as pl
from jax.experimental.pallas import tpu as pltpu
from jax.sharding import PartitionSpec as P

neg_fill = -1000000000.0
open_cap = 3e38
eps_norm = 1e-05
PAIR = 128
HALF = 64
QUERY_SCALE = 0.125
f32 = jnp.float32
bf16 = jnp.bfloat16


def low(value):
    return value.astype(bf16)


def nn(left, right):
    return lax.dot_general(left, right, (((1,), (0,)), ((), ())), preferred_element_type=f32)


def nt(left, right):
    return lax.dot_general(left, right, (((1,), (1,)), ((), ())), preferred_element_type=f32)


def tn(left, right):
    return lax.dot_general(left, right, (((0,), (0,)), ((), ())), preferred_element_type=f32)


def after(value, *others):
    return lax.optimization_barrier((value,) + others)[0]


def norm_stats(values):
    centre = jnp.mean(values, axis=-1, keepdims=True)
    offset = values - centre
    spread = jnp.mean(offset * offset, axis=-1, keepdims=True)
    scale = lax.rsqrt(spread + eps_norm)
    return offset * scale, scale


def norm_forward(values, gain, shift):
    hat, scale = norm_stats(values)
    return low(hat * gain + shift)


def norm_backward(values, gain, grad):
    hat, scale = norm_stats(values)
    scaled = grad * gain
    mean_one = jnp.mean(scaled, axis=-1, keepdims=True)
    mean_two = jnp.mean(scaled * hat, axis=-1, keepdims=True)
    back = scale * (scaled - mean_one - hat * mean_two)
    return back, jnp.sum(grad * hat, axis=0), jnp.sum(grad, axis=0)


def head_halves(both):
    lane = lax.broadcasted_iota(jnp.int32, both.shape, 1)
    zero = jnp.zeros_like(both)
    return jnp.where(lane < HALF, both, zero), jnp.where(lane < HALF, zero, both)


def fill_caps(info, cap_ref, block, causal):
    length = cap_ref.shape[0]
    for t in range(2):
        keys = lax.broadcasted_iota(jnp.int32, (length, block), 0)
        allowed = keys < info[0]
        if causal:
            places = lax.broadcasted_iota(jnp.int32, (length, block), 1) + info[1 + t] * block
            allowed = allowed & (keys <= places)
        cap_ref[:, t * block : (t + 1) * block] = jnp.where(allowed, open_cap, neg_fill)


def forward_kernel(info, q_ref, k_ref, v_ref, o_ref, lse_ref, cap_ref, s_ref, *, block, causal, chunk):
    length = k_ref.shape[0]

    @pl.when(pl.program_id(0) == 0)
    def _():
        fill_caps(info, cap_ref, block, causal)

    for t in (1, 0):
        rows = slice(t * block, (t + 1) * block)
        span = length // 2 if (causal and t == 0) else length
        queries = jnp.concatenate(head_halves(q_ref[rows, :] * bf16(QUERY_SCALE)), axis=0)
        most = jnp.full((8, 2 * block), -open_cap, f32)
        for c in range(0, span, chunk):
            keys = slice(c, c + chunk)
            cap = cap_ref[keys, rows]
            scores = jnp.minimum(nt(k_ref[keys, :], queries), jnp.concatenate([cap, cap], axis=1))
            s_ref[t, keys, :] = scores
            most = jnp.maximum(most, jnp.max(scores.reshape(chunk // 8, 8, 2 * block), axis=0))
        most = jnp.max(most, axis=0, keepdims=True)
        total = jnp.zeros((8, 2 * block), f32)
        mixed = jnp.zeros((PAIR, 2 * block), f32)
        for c in range(0, span, chunk):
            keys = slice(c, c + chunk)
            weights = jnp.exp(s_ref[t, keys, :] - most)
            total = total + jnp.sum(weights.reshape(chunk // 8, 8, 2 * block), axis=0)
            mixed = mixed + tn(v_ref[keys, :], low(weights))
        total = jnp.sum(total, axis=0, keepdims=True)
        mixed = mixed / total
        sub = lax.broadcasted_iota(jnp.int32, (PAIR, block), 0)
        o_ref[rows, :] = low(jnp.where(sub < HALF, mixed[:, :block], mixed[:, block:]).T)
        lse = most + jnp.log(total)
        lse_ref[0, 0:1, rows] = lse[:, :block]
        lse_ref[0, 1:2, rows] = lse[:, block:]


def backward_kernel(
    info, q_ref, k_ref, v_ref, o_ref, g_ref, lse_ref, dq_ref, dk_ref, dv_ref, cap_ref, dk_acc, dv_acc,
    *, block, causal, chunk
):
    length = k_ref.shape[0]

    @pl.when(pl.program_id(0) == 0)
    def _():
        fill_caps(info, cap_ref, block, causal)

    for t in (1, 0):
        rows = slice(t * block, (t + 1) * block)
        span = length // 2 if (causal and t == 0) else length
        grads = g_ref[rows, :]
        prod = (grads.astype(f32) * o_ref[rows, :].astype(f32)).T
        centre = jnp.concatenate(
            [jnp.sum(prod[:HALF], axis=0, keepdims=True), jnp.sum(prod[HALF:], axis=0, keepdims=True)], axis=1
        )
        lse = jnp.concatenate([lse_ref[0, 0:1, rows], lse_ref[0, 1:2, rows]], axis=1)
        queries = jnp.concatenate(head_halves(q_ref[rows, :] * bf16(QUERY_SCALE)), axis=0)
        grads = jnp.concatenate(head_halves(grads), axis=0)
        dq = jnp.zeros((PAIR, 2 * block), f32)
        for c in range(0, span, chunk):
            keys = slice(c, c + chunk)
            k, v = k_ref[keys, :], v_ref[keys, :]
            cap = cap_ref[keys, rows]
            scores = jnp.minimum(nt(k, queries), jnp.concatenate([cap, cap], axis=1))
            probs = jnp.exp(scores - lse)
            grad_scores = low(probs * (nt(v, grads) - centre))
            dv = nn(low(probs), grads)
            dk = nn(grad_scores, queries)
            dq = dq + tn(k, grad_scores)
            if t == 1:
                dk_acc[keys, :] = dk
                dv_acc[keys, :] = dv
            else:
                dk_acc[keys, :] += dk
                dv_acc[keys, :] += dv
        sub = lax.broadcasted_iota(jnp.int32, (PAIR, block), 0)
        dq = jnp.where(sub < HALF, dq[:, :block], dq[:, block:]) * QUERY_SCALE
        dq_ref[rows, :] = low(dq.T)
    dk_ref[...] = low(dk_acc[...])
    dv_ref[...] = low(dv_acc[...])


def attention_specs(queries, length):
    one = pl.BlockSpec((queries, PAIR), lambda i, *_: (0, i))
    key = pl.BlockSpec((length, PAIR), lambda i, *_: (0, i))
    lse = pl.BlockSpec((1, 8, queries), lambda i, *_: (i, 0, 0))
    return one, key, lse


def attend_forward(info, query, keys, values, causal):
    queries, width = query.shape
    length = keys.shape[0]
    one, key, lse = attention_specs(queries, length)
    pairs = width // PAIR
    return pl.pallas_call(
        functools.partial(forward_kernel, block=queries // 2, causal=causal, chunk=min(256, length // 2)),
        out_shape=(
            jax.ShapeDtypeStruct((queries, width), bf16),
            jax.ShapeDtypeStruct((pairs, 8, queries), f32),
        ),
        grid_spec=pltpu.PrefetchScalarGridSpec(
            num_scalar_prefetch=1,
            grid=(pairs,),
            in_specs=[one, key, key],
            out_specs=[one, lse],
            scratch_shapes=[pltpu.VMEM((length, queries), f32), pltpu.VMEM((2, length, queries), f32)],
        ),
        compiler_params=pltpu.CompilerParams(vmem_limit_bytes=40 << 20),
        cost_estimate=pl.CostEstimate(
            flops=12 * queries * length * width, bytes_accessed=4 * (queries + length) * width, transcendentals=0
        ),
    )(info, query, keys, values)


def attend_backward(info, query, keys, values, mixed, grad, lse_rows, causal):
    queries, width = query.shape
    length = keys.shape[0]
    one, key, lse = attention_specs(queries, length)
    return pl.pallas_call(
        functools.partial(backward_kernel, block=queries // 2, causal=causal, chunk=min(256, length // 2)),
        out_shape=(
            jax.ShapeDtypeStruct((queries, width), bf16),
            jax.ShapeDtypeStruct((length, width), bf16),
            jax.ShapeDtypeStruct((length, width), bf16),
        ),
        grid_spec=pltpu.PrefetchScalarGridSpec(
            num_scalar_prefetch=1,
            grid=(width // PAIR,),
            in_specs=[one, key, key, one, one, lse],
            out_specs=[one, key, key],
            scratch_shapes=[
                pltpu.VMEM((length, queries), f32),
                pltpu.VMEM((length, PAIR), f32),
                pltpu.VMEM((length, PAIR), f32),
            ],
        ),
        compiler_params=pltpu.CompilerParams(vmem_limit_bytes=40 << 20),
        cost_estimate=pl.CostEstimate(
            flops=20 * queries * length * width, bytes_accessed=4 * (queries + length) * width, transcendentals=0
        ),
    )(info, query, keys, values, mixed, grad, lse_rows)


def place_kernel(where, *refs, count, pieces):
    out_ref = refs[-1]
    step = pl.program_id(0)
    for k in range(count):

        @pl.when(step // pieces == k)
        def _(k=k):
            out_ref[...] = refs[k][...].astype(out_ref.dtype)


def place(where, slots, kind):
    count, pieces = len(slots), where.shape[0] // len(slots)
    rows, width = slots[0].shape
    block = rows // pieces
    return pl.pallas_call(
        functools.partial(place_kernel, count=count, pieces=pieces),
        out_shape=jax.ShapeDtypeStruct((rows * count, width), kind),
        grid_spec=pltpu.PrefetchScalarGridSpec(
            num_scalar_prefetch=1,
            grid=(count * pieces,),
            in_specs=[
                pl.BlockSpec(
                    (block, width),
                    lambda i, where, k=k: (jnp.clip(i - k * pieces, 0, pieces - 1), 0),
                )
                for k in range(count)
            ],
            out_specs=pl.BlockSpec((block, width), lambda i, where: (where[i], 0)),
        ),
        compiler_params=pltpu.CompilerParams(vmem_limit_bytes=40 << 20),
        cost_estimate=pl.CostEstimate(flops=0, bytes_accessed=6 * rows * count * width, transcendentals=0),
    )(where, *slots)


def build(dp_size, mp_size):
    ring = [(i, (i + 1) % mp_size) for i in range(mp_size)]
    back_ring = [(i, (i - 1) % mp_size) for i in range(mp_size)]
    dp_bits = dp_size.bit_length() - 1

    def flip(axis, size, bit):
        return lambda value: lax.ppermute(value, axis, [(i, i ^ (1 << bit)) for i in range(size)])

    def gather_slots(share):
        slots = [share]
        for _ in range(mp_size - 1):
            slots.append(lax.ppermute(slots[-1], "mp", ring))
        return slots

    def reduce_slots(slots):
        total = slots[mp_size - 1]
        for k in range(mp_size - 2, -1, -1):
            total = lax.ppermute(total, "mp", back_ring) + slots[k]
        return total

    def shards(
        tokens,
        memory,
        target_lengths,
        source_lengths,
        cotangent,
        norm_gain,
        norm_bias,
        self_in,
        self_in_bias,
        self_out,
        cross_query,
        cross_kv,
        cross_bias,
        cross_out,
        out_bias,
        ffn_up,
        ffn_up_bias,
        ffn_down,
    ):
        rows, length, width = tokens.shape
        source = memory.shape[1]
        d = lax.axis_index("dp")
        z = lax.axis_index("mp")
        group = mp_size // rows
        row = z // group
        part = z % group
        block = length // (2 * group)
        share = width // dp_size
        own_starts = (part * block, (2 * group - 1 - part) * block)

        def own(values):
            return jnp.concatenate([lax.dynamic_slice_in_dim(values, s, block, 0) for s in own_starts])

        def take_row(values):
            return lax.dynamic_index_in_dim(values, row, 0, keepdims=False)

        def rows_of(weight):
            return lax.dynamic_slice_in_dim(weight, d * share, share, 0)

        def cols_of(weight):
            return lax.dynamic_slice_in_dim(weight, d * share, share, 1).T

        def with_bias(piece, bias):
            extra = jnp.zeros((16, piece.shape[1]), bf16)
            if bias is not None:
                extra = lax.dynamic_update_slice(extra, bias[None], (0, 0))
            return jnp.concatenate([piece, extra])

        def group_slots(pieces, *held):
            cat = jnp.concatenate([with_bias(p, b) for p, b in pieces], axis=1)
            if held:
                cat = after(cat, *held)
            return gather_slots(cat)

        def gather_group(slots, wides, *held):
            starts = [0]
            for w in wides:
                starts.append(starts[-1] + w)
            both = jnp.concatenate(
                [s[:, a:b] for a, b in zip(starts[:-1], starts[1:]) for s in slots], axis=1
            )
            part_to_send = both[:share]
            if held:
                part_to_send = after(part_to_send, *held)
            full = lax.all_gather(part_to_send, "dp", axis=0, tiled=True)
            bias = both[share].astype(f32)
            found = []
            for a, b in zip(starts[:-1], starts[1:]):
                cols = slice(a * mp_size, b * mp_size)
                found.append((full[:, cols], bias[cols]))
            return found

        per = width // mp_size
        hid = ffn_up.shape[1]
        slots_a = group_slots(
            [
                (rows_of(self_in[0]), self_in_bias[0]),
                (rows_of(self_in[1]), None),
                (rows_of(self_in[2]), self_in_bias[1]),
            ]
        )
        slots_b = group_slots(
            [
                (cols_of(self_out), None),
                (rows_of(cross_query), cross_bias[0]),
                (rows_of(cross_kv[0]), None),
                (rows_of(cross_kv[1]), cross_bias[1]),
            ],
            slots_a[-1],
        )
        slots_c = group_slots(
            [(cols_of(cross_out), None), (rows_of(ffn_up), ffn_up_bias), (cols_of(ffn_down), None)],
            slots_b[-1],
        )
        (w_q1, b_q1), (w_k1, _), (w_v1, b_v1) = gather_group(slots_a, [per, per, per])
        (w_o1, _), (w_q2, b_q2), (w_k2, _), (w_v2, b_v2) = gather_group(slots_b, [per, per, per, per])
        (w_o2, _), (w_up, b_up), (w_down, _) = gather_group(slots_c, [per, hid, hid])
        gains, shifts = norm_gain.astype(f32), norm_bias.astype(f32)
        biases = out_bias.astype(f32)

        ends = jnp.stack([part, 2 * group - 1 - part]).astype(jnp.int32)
        target_info = jnp.concatenate([target_lengths[row][None], ends])
        source_info = jnp.concatenate([source_lengths[row][None], ends])
        full_row = take_row(tokens).astype(f32)
        mem_row = take_row(memory)
        resid = own(full_row)
        grad_out_low = own(take_row(cotangent))
        grad_out = grad_out_low.astype(f32)
        h1_row = norm_forward(full_row, gains[0], shifts[0])
        h1 = own(h1_row)
        q1 = low(nn(h1, w_q1) + b_q1)
        k1 = low(nn(h1_row, w_k1))
        v1 = low(nn(h1_row, w_v1) + b_v1)
        o1, lse1 = attend_forward(target_info, q1, k1, v1, True)
        first = resid + nt(o1, w_o1) + biases[0]
        h2 = norm_forward(first, gains[1], shifts[1])
        q2 = low(nn(h2, w_q2) + b_q2)
        k2 = low(nn(mem_row, w_k2))
        v2 = low(nn(mem_row, w_v2) + b_v2)
        o2, lse2 = attend_forward(source_info, q2, k2, v2, False)
        second = first + nt(o2, w_o2) + biases[1]
        h3 = norm_forward(second, gains[2], shifts[2])
        pre = nn(h3, w_up) + b_up
        hidden, pull_gelu = jax.vjp(lambda u: jax.nn.gelu(u, approximate=True), pre)
        hidden = low(hidden)
        final = low(second + nt(hidden, w_down) + biases[2])

        def slot_places():
            found = []
            for k in range(mp_size):
                other = lax.rem(z - k + mp_size, mp_size)
                base = (other // group) * (2 * group)
                found += [base + other % group, base + 2 * group - 1 - other % group]
            return jnp.stack(found).astype(jnp.int32)

        causal_places = slot_places()
        memory_places = jnp.stack([lax.rem(z - k + mp_size, mp_size) for k in range(mp_size)]).astype(jnp.int32)

        bias_three = jnp.sum(grad_out, axis=0)
        grad_down = low(tn(grad_out_low, hidden))
        grad_pre = low(pull_gelu(nn(grad_out_low, w_down))[0])
        grad_up = low(tn(h3, grad_pre))
        up_bias_grad = jnp.sum(grad_pre.astype(f32), axis=0)
        back, gain_three, shift_three = norm_backward(second, gains[2], nt(grad_pre, w_up))
        grad_second = grad_out + back
        e2 = low(grad_second)
        output_slots = gather_slots(final)

        def scatter(grad):
            return lax.psum_scatter(grad, "dp", scatter_dimension=0, tiled=True)

        down_share = scatter(grad_down)
        up_share = scatter(grad_up)

        def bit_of(b):
            return lax.rem(lax.shift_right_logical(d, b), 2)

        def halves_of(act):
            wide = act.reshape(act.shape[0], dp_size // 2, 2, share)
            core = bit_of(0)
            send = lax.dynamic_index_in_dim(wide, 1 - core, 2, keepdims=False)
            keep = lax.dynamic_index_in_dim(wide, core, 2, keepdims=False)
            return send.reshape(act.shape[0], -1), keep.reshape(act.shape[0], -1)

        def halving_sum(pairs):
            split = [(halves_of(act), grad) for act, grad in pairs]
            sent = jnp.concatenate([low(tn(send, grad)) for (send, _), grad in split], axis=1)
            got = flip("dp", dp_size, 0)(sent)
            kept = jnp.concatenate([tn(keep, grad) for (_, keep), grad in split], axis=1)
            kept = low(kept + got.astype(f32))
            cols = kept.shape[1]
            bits = list(range(1, dp_bits))
            sides = []
            for order, side in ((bits, slice(0, cols // 2)), (bits[::-1], slice(cols // 2, cols))):
                value = kept[:, side].reshape((2,) * len(bits) + (share, cols // 2))
                left = bits[::-1]
                for b in order:
                    axis = left.index(b)
                    bit = bit_of(b)
                    send = lax.dynamic_index_in_dim(value, 1 - bit, axis, keepdims=False)
                    keep = lax.dynamic_index_in_dim(value, bit, axis, keepdims=False)
                    value = keep + flip("dp", dp_size, b)(send)
                    left = [x for x in left if x != b]
                sides.append(value)
            return jnp.concatenate(sides, axis=1)

        def slots_of(shares):
            return [
                jnp.concatenate(
                    [s[:, k * (s.shape[1] // mp_size) : (k + 1) * (s.shape[1] // mp_size)] for s in shares], axis=1
                )
                for k in range(mp_size)
            ]

        def gather_grads(total):
            return lax.all_gather(total, "dp", axis=0, tiled=True)

        bias_two = jnp.sum(e2.astype(f32), axis=0)
        do2 = low(nn(e2, w_o2))
        dq2, dk2, dv2 = attend_backward(source_info, q2, k2, v2, o2, do2, lse2, False)
        memory_part = low(nt(dk2, w_k2) + nt(dv2, w_v2))
        back, gain_two, shift_two = norm_backward(first, gains[1], nt(dq2, w_q2))
        grad_first = grad_second + back
        e1 = low(grad_first)

        pair_perm = [(i, (i // group) * group + (i % group - 1) % group) for i in range(mp_size)]

        def row_sum(piece_of):
            total = piece_of(lax.rem(part + 1, group))
            for k in range(group - 2, -1, -1):
                total = lax.ppermute(total, "mp", pair_perm).astype(f32)
                total = total + piece_of(lax.rem(part - k + group, group)).astype(f32)
                if k:
                    total = low(total)
            return total

        def memory_piece(p):
            return lax.dynamic_slice_in_dim(memory_part, p * (source // group), source // group, 0)

        memory_slots = gather_slots(low(row_sum(memory_piece)))
        cross_share = halving_sum([(h2, dq2), (mem_row, dk2), (mem_row, dv2), (e2, o2)])

        bias_one = jnp.sum(e1.astype(f32), axis=0)
        do1 = low(nn(e1, w_o1))
        output = place(causal_places, output_slots, bf16).reshape(tokens.shape)
        do1 = after(do1, output)
        dq1, dk1, dv1 = attend_backward(target_info, q1, k1, v1, o1, do1, lse1, True)
        kv_part = low(nt(dk1, w_k1) + nt(dv1, w_v1))

        def causal_piece(p):
            return jnp.concatenate(
                [
                    lax.dynamic_slice_in_dim(kv_part, s, block, 0)
                    for s in (p * block, (2 * group - 1 - p) * block)
                ]
            )

        ffn_total = reduce_slots(slots_of([down_share, up_share]))
        ffn_full = gather_grads(ffn_total)
        cross_total = reduce_slots(slots_of([cross_share[:, i * width : (i + 1) * width] for i in range(4)]))
        cross_full = gather_grads(cross_total)

        grad_h1 = nt(dq1, w_q1) + row_sum(causal_piece)
        back, gain_one, shift_one = norm_backward(resid, gains[0], grad_h1)
        tokens_own = low(grad_first + back)
        tokens_slots = gather_slots(tokens_own)

        self_share = halving_sum([(h1, dq1), (h1_row, dk1), (h1_row, dv1), (e1, o1)])
        self_total = reduce_slots(slots_of([self_share[:, i * width : (i + 1) * width] for i in range(4)]))
        self_full = gather_grads(self_total)

        memory_grad = place(memory_places, memory_slots, f32).reshape(memory.shape)
        tokens_grad = place(causal_places, tokens_slots, f32).reshape(tokens.shape)

        def by_slot(vector):
            return vector.reshape(mp_size, -1)

        def total_of(values):
            return jnp.sum(values.astype(f32), axis=0)

        slot_sums = jnp.concatenate(
            [
                by_slot(total_of(dq1)),
                by_slot(total_of(dv1)),
                by_slot(total_of(dq2)),
                by_slot(total_of(dv2)),
                by_slot(up_bias_grad),
            ],
            axis=1,
        )
        flipped = slot_sums[::-1]
        twice = jnp.concatenate([flipped, flipped])
        in_order = lax.dynamic_slice_in_dim(twice, mp_size - 1 - z, mp_size, 0)
        whole = jnp.stack(
            [gain_one, gain_two, gain_three, shift_one, shift_two, shift_three, bias_one, bias_two, bias_three]
        )
        small = jnp.concatenate([in_order.reshape(-1, PAIR), whole.reshape(-1, PAIR)])
        for b in range(dp_bits):
            small = small + flip("dp", dp_size, b)(small)
        for b in range(mp_size.bit_length() - 1):
            small = small + flip("mp", mp_size, b)(small)
        small = small.reshape(-1)
        slot_part = small[: in_order.size].reshape(in_order.shape)
        mine = lax.dynamic_index_in_dim(slot_part, z, 0, keepdims=False)
        whole = small[in_order.size :].reshape(9, width)

        def cut(full, i):
            return full[:, i * per : (i + 1) * per].astype(f32)

        return (
            output,
            tokens_grad,
            memory_grad,
            whole[0:3],
            whole[3:6],
            jnp.stack([cut(self_full, 0), cut(self_full, 1), cut(self_full, 2)]),
            jnp.stack([mine[:per], mine[per : 2 * per]]),
            cut(self_full, 3).T,
            cut(cross_full, 0),
            jnp.stack([cut(cross_full, 1), cut(cross_full, 2)]),
            jnp.stack([mine[2 * per : 3 * per], mine[3 * per : 4 * per]]),
            cut(cross_full, 3).T,
            whole[6:9],
            ffn_full[:, hid:].astype(f32),
            mine[4 * per :],
            ffn_full[:, :hid].astype(f32).T,
        )

    return shards


def solution(mesh):
    placed = (
        P("dp", None, None),
        P("dp", None, None),
        P("dp"),
        P("dp"),
        P("dp", None, None),
        P(),
        P(),
        P(None, None, "mp"),
        P(None, "mp"),
        P("mp", None),
        P(None, "mp"),
        P(None, None, "mp"),
        P(None, "mp"),
        P("mp", None),
        P(),
        P(None, "mp"),
        P("mp"),
        P("mp", None),
    )
    return jax.shard_map(
        build(mesh.shape["dp"], mesh.shape["mp"]),
        mesh=mesh,
        in_specs=placed,
        out_specs=(
            P("dp", None, None),
            P("dp", None, None),
            P("dp", None, None),
            P(),
            P(),
            P(None, None, "mp"),
            P(None, "mp"),
            P("mp", None),
            P(None, "mp"),
            P(None, None, "mp"),
            P(None, "mp"),
            P("mp", None),
            P(),
            P(None, "mp"),
            P("mp"),
            P("mp", None),
        ),
        check_vma=False,
    )
```

time: 2070 us -> 873 us (0.42)
  waiting for transfers between devices: 1480 us -> 360 us
  other arithmetic: 224 us -> 57.7 us
  matrix products: 300 us -> 162 us
  local copies, waits for them, and re-layouts: 11.4 us -> 116 us
  Pallas kernels: 0 us -> 104 us
  starting transfers between devices: 0.69 us -> 52.6 us
  blocking collectives: 24.4 us -> 0 us
    psum x7 -> x0, waiting for transfers between devices: 1480 us -> none  [the longest x3 861 us: branch_output(): return lax.psum(partial_value, 'mp') + shift.astype(jnp.float32)]
    ppermute x0 -> x44, waiting for transfers between devices: none -> 354 us  [the longest x18 193 us: gather_slots(): slots.append(lax.ppermute(slots[-1], 'mp', ring))]
    dot_general x42 -> x38, matrix products: 300 us -> 162 us  [the longest x10 58.4 us: nt(): lax.dot_general(left, right, (((1,), (1,)), ((), ())), preferred_element_...]
    reduce_sum x17 -> x12, other arithmetic: 126 us -> 12.9 us  [the longest x4 4.28 us: total_of(): return jnp.sum(values.astype(f32), axis=0)]
    pallas_call x0 -> x7, Pallas kernels: none -> 104 us  [the longest x2 48.3 us: attend_backward(): pl.pallas_call(functools.partial(backward_kernel, block=queries // 2, cau...]
    convert_element_type x18 -> x10, other arithmetic: 80.2 us -> 16.1 us  [the longest x7 12 us: low(): return value.astype(bf16)]
    ppermute x0 -> x44, starting transfers between devices: none -> 51.7 us  [the longest x9 31.7 us: reduce_slots(): total = lax.ppermute(total, 'mp', back_ring) + slots[k]]
    unnamed x181 -> x252, local copies, waits for them, and re-layouts: 11 us -> 53.2 us
  transfers between devices with their start and end apart: 7 -> 52, of which waited for: 7 -> 36; matrix products, arithmetic and copies ran while one was open for 6% -> 30% of each run, Pallas kernels for 0% -> 12%
where the time goes in v1:
time: 873 us; the launch traced here: 868 us
  waiting for transfers between devices  360 us (41%)
  matrix products  162 us (19%)
  local copies, waits for them, and re-layouts  116 us (13%)
  Pallas kernels  104 us (12%)
  other arithmetic  57.7 us (7%)
  starting transfers between devices  52.6 us (6%)
  between operations  16.5 us (2%)
    ppermute x18, waiting for transfers between devices, gather_slots(): slots.append(lax.ppermute(slots[-1], 'mp', ring))  193 us
    ppermute x15, waiting for transfers between devices, flip(): lax.ppermute(value, axis, [(i, i ^ 1 << bit) for i in range(size)])  86.8 us
    dot_general x10, matrix products, nt(): lax.dot_general(left, right, (((1,), (1,)), ((), ())), preferred_element_...  58.4 us
    dot_general x18, matrix products, tn(): lax.dot_general(left, right, (((0,), (0,)), ((), ())), preferred_element_...  53.2 us
    unnamed x252, local copies, waits for them, and re-layouts  53.2 us
    ppermute x9, waiting for transfers between devices, reduce_slots(): total = lax.ppermute(total, 'mp', back_ring) + slots[k]  52.8 us
    dot_general x10, matrix products, nn(): lax.dot_general(left, right, (((1,), (0,)), ((), ())), preferred_element_...  50.1 us
    pallas_call x2, Pallas kernels, attend_backward(): pl.pallas_call(functools.partial(backward_kernel, block=queries // 2, cau...  48.3 us
  transfers between devices with their start and end apart: 52, of which 36 were waited for; matrix products, arithmetic and copies ran while one was open for 30% of the time, Pallas kernels for 12%

profile of v1, /device:TPU:0, one launch (start us, length us, event | category | flops | bytes accessed | tf_op | source)
XLA Modules:
  0.0 868.0 jit_solution(5924358726870489023)
XLA Ops:
  50.6 9.1 %collective-permute-done.4 = bf16[144,1024]{1,0:T(8,128)(2,1)S(1)} collective-permute-done((bf16[144,1024]{1,0:T(8,128)(2,1)S(1)}, bf16[144,1024]{1,0:T(8,128)(2,1)S(1)}, u32[]{:S(2)}, u32[]{:S(2)}) %collective-permute-start.4) | collective-permute-done | bytes 294944 | tf_op jit(solution)/shard_map/ppermute | solution.py:265
  72.1 15.3 %collective-permute-done.6 = bf16[144,2304]{1,0:T(8,128)(2,1)S(1)} collective-permute-done((bf16[144,2304]{1,0:T(8,128)(2,1)S(1)}, bf16[144,2304]{1,0:T(8,128)(2,1)S(1)}, u32[]{:S(2)}, u32[]{:S(2)}) %collective-permute-start.6) | collective-permute-done | bytes 663584 | tf_op jit(solution)/shard_map/ppermute | solution.py:265
  87.5 16.4 %collective-permute-done.7 = bf16[144,2304]{1,0:T(8,128)(2,1)S(1)} collective-permute-done((bf16[144,2304]{1,0:T(8,128)(2,1)S(1)}, bf16[144,2304]{1,0:T(8,128)(2,1)S(1)}, u32[]{:S(2)}, u32[]{:S(2)}) %collective-permute-start.7) | collective-permute-done | bytes 663584 | tf_op jit(solution)/shard_map/ppermute | solution.py:265
  103.9 12.4 %collective-permute-done.8 = bf16[144,2304]{1,0:T(8,128)(2,1)S(1)} collective-permute-done((bf16[144,2304]{1,0:T(8,128)(2,1)S(1)}, bf16[144,2304]{1,0:T(8,128)(2,1)S(1)}, u32[]{:S(2)}, u32[]{:S(2)}) %collective-permute-start.8) | collective-permute-done | bytes 663584 | tf_op jit(solution)/shard_map/ppermute | solution.py:265
  168.9 15.6 %shard_map.297 = (bf16[512,1024]{1,0:T(8,128)(2,1)S(1)}, f32[8,8,512]{2,1,0:T(8,128)S(1)}) custom-call(s32[3]{0:T(128)S(1)} %add_add_fusion.3.info, bf16[512,1024]{1,0:T(8,128)(2,1)S(1)} %add_convert_fusion.12.q_ref, bf16[1024,1024]{1,0:T(8,128)(2,1)S(1)} %convolution_convert_fusion.2.k_ref, bf16[1024,1024]{1,0:T(8,128)(2,1)S(1)} %add_convert_fusion.4.v_ref), custom_call_target="tpu_custom_call" | custom-call | flops 6442450944 | bytes 6291456 | tf_op jit(solution)/shard_map/pallas_call | solution.py:171
  215.7 18.7 %shard_map.298 = (bf16[512,1024]{1,0:T(8,128)(2,1)S(1)}, f32[8,8,512]{2,1,0:T(8,128)S(1)}) custom-call(s32[3]{0:T(128)S(1)} %add_add_fusion.4.info, bf16[512,1024]{1,0:T(8,128)(2,1)S(1)} %add_convert_fusion.10.q_ref, bf16[1024,1024]{1,0:T(8,128)(2,1)S(1)} %fusion.21.k_ref, bf16[1024,1024]{1,0:T(8,128)(2,1)S(1)} %add_convert_fusion.3.v_ref), custom_call_target="tpu_custom_call" | custom-call | flops 6442450944 | bytes 6291456 | tf_op jit(solution)/shard_map/pallas_call | solution.py:171
  246.1 10.7 %fusion.15 = f32[512,4096]{1,0:T(8,128)} fusion(bf16[1024,9216]{1,0:T(8,128)(2,1)} %all-gather.11.cloned.1.call-done, f32[512,1024]{1,0:T(8,128)S(1)} %get-tuple-element.241, f32[1024]{0:T(1024)S(1)} %bitcast.271, f32[1024]{0:T(1024)S(1)} %bitcast.259, f32[512]{0:T(512)S(1)} %add_rsqrt_fusion.2, f32[512]{0:T(512)S(1)} %broadcast_multiply_fusion.8), kind=kOutput, calls=%fused_computation.23 | convolution fusion | flops 4297588736 | bytes 18886656 | tf_op jit(solution)/shard_map/dot_general | solution.py:25
  258.0 13.0 %convert_reduce_fusion = (f32[4096]{0:T(1024)}, bf16[512,4096]{1,0:T(8,128)(2,1)}) fusion(f32[512,4096]{1,0:T(8,128)} %fusion.15, f32[4096]{0:T(1024)S(1)} %bitcast.253, bf16[1024,9216]{1,0:T(8,128)(2,1)S(1)} %bitcast.281, bf16[256,1024]{1,0:T(8,128)(2,1)S(1)} %copy-done.58, bf16[256,1024]{1,0:T(8,128)(2,1)S(1)} %copy-done.55), kind=kOutput, calls=%fused_computation.13 | convolution fusion | flops 4345294848 | bytes 22052864 | tf_op jit(solution)/shard_map/dot_general | solution.py:25
  271.0 9.2 %convolution_convert_fusion = bf16[1024,4096]{1,0:T(8,128)(2,1)} fusion(bf16[512,4096]{1,0:T(8,128)(2,1)} %get-tuple-element.246, f32[512,1024]{1,0:T(8,128)S(1)} %get-tuple-element.241, f32[1024]{0:T(1024)S(1)} %bitcast.272, f32[1024]{0:T(1024)S(1)} %bitcast.260, f32[512]{0:T(512)S(1)} %add_rsqrt_fusion.2, f32[512]{0:T(512)S(1)} %broadcast_multiply_fusion.8), kind=kOutput, calls=%fused_computation.15 | convolution fusion | flops 4301783040 | bytes 14692352 | tf_op jit(solution)/shard_map/dot_general | solution.py:33
  280.5 12.9 %add_convert_fusion.8.refs_0_ = bf16[512,1024]{1,0:T(8,128)(2,1)} fusion(f32[512,1024]{1,0:T(8,128)S(1)} %get-tuple-element.241, bf16[1024,9216]{1,0:T(8,128)(2,1)} %all-gather.11.cloned.1.call-done, f32[1024]{0:T(1024)S(1)} %bitcast.273, f32[512,4096]{1,0:T(8,128)} %fusion.15, f32[4096]{0:T(1024)S(1)} %bitcast.254), kind=kOutput, calls=%fused_computation.62 | convolution fusion | flops 4317511680 | bytes 19943424 | tf_op jit(solution)/shard_map/dot_general | solution.py:29
  316.5 26.8 %shard_map.300 = (bf16[512,1024]{1,0:T(8,128)(2,1)S(1)}, bf16[1024,1024]{1,0:T(8,128)(2,1)S(1)}, bf16[1024,1024]{1,0:T(8,128)(2,1)S(1)}) custom-call(s32[3]{0:T(128)S(1)} %add_add_fusion.4.info, bf16[512,1024]{1,0:T(8,128)(2,1)S(1)} %copy-done.24, bf16[1024,1024]{1,0:T(8,128)(2,1)S(1)} %copy-done.22, bf16[1024,1024]{1,0:T(8,128)(2,1)S(1)} %copy-done.28, ...), custom_call_target="tpu_custom_call" | custom-call | flops 10737418240 | bytes 6291456 | tf_op jit(solution)/shard_map/pallas_call | solution.py:195
  412.2 13.4 %collective-permute-done.11.refs_3_ = bf16[512,1024]{1,0:T(8,128)(2,1)S(1)} collective-permute-done((bf16[512,1024]{1,0:T(8,128)(2,1)}, bf16[512,1024]{1,0:T(8,128)(2,1)S(1)}, u32[]{:S(2)}, u32[]{:S(2)}) %collective-permute-start.11) | collective-permute-done | bytes 1048608 | tf_op jit(solution)/shard_map/ppermute | solution.py:265
  435.4 21.4 %shard_map.301 = (bf16[512,1024]{1,0:T(8,128)(2,1)S(1)}, bf16[1024,1024]{1,0:T(8,128)(2,1)S(1)}, bf16[1024,1024]{1,0:T(8,128)(2,1)S(1)}) custom-call(s32[3]{0:T(128)S(1)} %add_add_fusion.3.info, bf16[512,1024]{1,0:T(8,128)(2,1)S(1)} %copy-done.18, bf16[1024,1024]{1,0:T(8,128)(2,1)S(1)} %copy-done.20, bf16[1024,1024]{1,0:T(8,128)(2,1)S(1)} %copy-done.26, ...), custom_call_target="tpu_custom_call" | custom-call | flops 10737418240 | bytes 6291456 | tf_op jit(solution)/shard_map/pallas_call | solution.py:195
  477.5 20.3 %collective-permute-done.36 = bf16[2,128,2048]{2,1,0:T(8,128)(2,1)S(1)} collective-permute-done((bf16[2,128,2048]{2,1,0:T(8,128)(2,1)S(1)}, bf16[2,128,2048]{2,1,0:T(8,128)(2,1)S(1)}, u32[]{:S(2)}, u32[]{:S(2)}) %collective-permute-start.36) | collective-permute-done | bytes 1048608 | tf_op jit(solution)/shard_map/ppermute | solution.py:260
  500.3 10.7 %collective-permute-done.37 = bf16[128,2048]{1,0:T(8,128)(2,1)S(1)} collective-permute-done((bf16[128,2048]{1,0:T(8,128)(2,1)S(1)}, bf16[128,2048]{1,0:T(8,128)(2,1)S(1)}, u32[]{:S(2)}, u32[]{:S(2)}) %collective-permute-start.37) | collective-permute-done | bytes 524320 | tf_op jit(solution)/shard_map/ppermute | solution.py:260
  537.4 13.8 %collective-permute-done.28 = bf16[2,128,2048]{2,1,0:T(8,128)(2,1)} collective-permute-done((bf16[2,128,2048]{2,1,0:T(8,128)(2,1)S(1)}, bf16[2,128,2048]{2,1,0:T(8,128)(2,1)}, u32[]{:S(2)}, u32[]{:S(2)}) %collective-permute-start.28) | collective-permute-done | bytes 1048608 | tf_op jit(solution)/shard_map/ppermute | solution.py:260
  553.0 10.6 %collective-permute-done.26 = bf16[2,128,2048]{2,1,0:T(8,128)(2,1)} collective-permute-done((bf16[2,128,2048]{2,1,0:T(8,128)(2,1)}, bf16[2,128,2048]{2,1,0:T(8,128)(2,1)}, u32[]{:S(2)}, u32[]{:S(2)}) %collective-permute-start.26) | collective-permute-done | bytes 1048608 | tf_op jit(solution)/shard_map/ppermute | solution.py:260
  649.5 13.7 %collective-permute-done.43 = bf16[128,2048]{1,0:T(8,128)(2,1)S(1)} collective-permute-done((bf16[128,2048]{1,0:T(8,128)(2,1)S(1)}, bf16[128,2048]{1,0:T(8,128)(2,1)S(1)}, u32[]{:S(2)}, u32[]{:S(2)}) %collective-permute-start.43) | collective-permute-done | bytes 524320 | tf_op jit(solution)/shard_map/ppermute | solution.py:271
  678.8 22.1 %collective-permute-done.12 = bf16[512,1024]{1,0:T(8,128)(2,1)} collective-permute-done((bf16[512,1024]{1,0:T(8,128)(2,1)}, bf16[512,1024]{1,0:T(8,128)(2,1)}, u32[]{:S(2)}, u32[]{:S(2)}) %collective-permute-start.12) | collective-permute-done | bytes 1048608 | tf_op jit(solution)/shard_map/ppermute | solution.py:485
  706.7 16.7 %collective-permute-done.17.refs_1_ = bf16[512,1024]{1,0:T(8,128)(2,1)} collective-permute-done((bf16[512,1024]{1,0:T(8,128)(2,1)S(1)}, bf16[512,1024]{1,0:T(8,128)(2,1)}, u32[]{:S(2)}, u32[]{:S(2)}) %collective-permute-start.17) | collective-permute-done | bytes 1048608 | tf_op jit(solution)/shard_map/ppermute | solution.py:265
  725.8 20.1 %collective-permute-done.13.refs_1_ = bf16[512,1024]{1,0:T(8,128)(2,1)} collective-permute-done((bf16[512,1024]{1,0:T(8,128)(2,1)}, bf16[512,1024]{1,0:T(8,128)(2,1)}, u32[]{:S(2)}, u32[]{:S(2)}) %collective-permute-start.13) | collective-permute-done | bytes 1048608 | tf_op jit(solution)/shard_map/ppermute | solution.py:265
  747.8 20.5 %collective-permute-done.18.refs_2_ = bf16[512,1024]{1,0:T(8,128)(2,1)} collective-permute-done((bf16[512,1024]{1,0:T(8,128)(2,1)}, bf16[512,1024]{1,0:T(8,128)(2,1)}, u32[]{:S(2)}, u32[]{:S(2)}) %collective-permute-start.18) | collective-permute-done | bytes 1048608 | tf_op jit(solution)/shard_map/ppermute | solution.py:265
  769.0 21.8 %collective-permute-done.14.refs_2_ = bf16[512,1024]{1,0:T(8,128)(2,1)} collective-permute-done((bf16[512,1024]{1,0:T(8,128)(2,1)}, bf16[512,1024]{1,0:T(8,128)(2,1)}, u32[]{:S(2)}, u32[]{:S(2)}) %collective-permute-start.14) | collective-permute-done | bytes 1048608 | tf_op jit(solution)/shard_map/ppermute | solution.py:265
  801.6 13.7 %collective-permute-done.23 = f32[136,128]{1,0:T(8,128)S(1)} collective-permute-done((f32[136,128]{1,0:T(8,128)S(1)}, f32[136,128]{1,0:T(8,128)S(1)}, u32[]{:S(2)}, u32[]{:S(2)}) %collective-permute-start.23) | collective-permute-done | bytes 69664 | tf_op jit(solution)/shard_map/ppermute | solution.py:260
  (554 shorter events, 472.4 us)
Async XLA Ops:
  7.2 152.7 %all-gather.7.cloned.1.call-start = ((), (), s32[]{:S(2)}) async-start(), calls=%async_computation.2 | async-start | bytes 7077888 | tf_op jit(solution)/shard_map/all_gather | solution.py:339
  40.0 145.9 %all-gather.9.cloned.1.call-start = ((), (), s32[]{:S(2)}) async-start(), calls=%async_computation.3 | async-start | bytes 9437184 | tf_op jit(solution)/shard_map/all_gather | solution.py:339
  70.6 171.1 %all-gather.11.cloned.1.call-start = ((), (), s32[]{:S(2)}) async-start(), calls=%async_computation.4 | async-start | bytes 21233664 | tf_op jit(solution)/shard_map/all_gather | solution.py:339
  120.4 480.9 %reduce-scatter.5.cloned.1.call-start = ((), (), s32[]{:S(2)}) async-start(), calls=%async_computation.8 | async-start | bytes 9437184 | tf_op jit(solution)/shard_map/reduce_scatter | solution.py:424
  280.2 323.1 %reduce-scatter.3.cloned.1.call-start = ((), (), s32[]{:S(2)}) async-start(), calls=%async_computation.7 | async-start | bytes 9437184 | tf_op jit(solution)/shard_map/reduce_scatter | solution.py:424
  293.4 78.6 %collective-permute-start.9 = (bf16[512,1024]{1,0:T(8,128)(2,1)}, bf16[512,1024]{1,0:T(8,128)(2,1)}, u32[]{:S(2)}, u32[]{:S(2)}) collective-permute-start(bf16[512,1024]{1,0:T(8,128)(2,1)} %add_convert_fusion.8.refs_0_), channel_id=1, source_target_pairs={{0,1},{1,2},{2,3},{3,0},{4,5},{5,6},{6,7},{7,4},{8,9},{9,10},{10,1... | collective-permute-start | bytes 3145736 | tf_op jit(solution)/shard_map/ppermute | solution.py:265
  372.0 27.2 %collective-permute-start.10 = (bf16[512,1024]{1,0:T(8,128)(2,1)}, bf16[512,1024]{1,0:T(8,128)(2,1)}, u32[]{:S(2)}, u32[]{:S(2)}) collective-permute-start(bf16[512,1024]{1,0:T(8,128)(2,1)} %collective-permute-done.9.refs_1_), channel_id=1, source_target_pairs={{0,1},{1,2},{2,3},{3,0},{4,5},{5,6},{6,7},{7,4},{8,9},{9,10},{10,1... | collective-permute-start | bytes 3145736 | tf_op jit(solution)/shard_map/ppermute | solution.py:265
  380.4 82.9 %collective-permute-start.33 = (bf16[512,4096]{1,0:T(8,128)(2,1)}, bf16[512,4096]{1,0:T(8,128)(2,1)}, u32[]{:S(2)}, u32[]{:S(2)}) collective-permute-start(bf16[512,4096]{1,0:T(8,128)(2,1)} %pad_maximum_fusion.1), channel_id=1, source_target_pairs={{0,4},{4,0},{8,12},{12,8},{16,20},{20,16},{24,28},{28,24},{1,5},{5... | collective-permute-start | bytes 12582920 | tf_op jit(solution)/shard_map/ppermute | solution.py:260
  399.2 26.3 %collective-permute-start.11 = (bf16[512,1024]{1,0:T(8,128)(2,1)}, bf16[512,1024]{1,0:T(8,128)(2,1)S(1)}, u32[]{:S(2)}, u32[]{:S(2)}) collective-permute-start(bf16[512,1024]{1,0:T(8,128)(2,1)} %collective-permute-done.10.refs_2_), channel_id=1, source_target_pairs={{0,1},{1,2},{2,3},{3,0},{4,5},{5,6},{6,7},{7,4},{8,9},{9,10},{10,1... | collective-permute-start | bytes 3145736 | tf_op jit(solution)/shard_map/ppermute | solution.py:265
  404.8 433.5 %all-gather.15.cloned.1.call-start = ((), (), s32[]{:S(2)}) async-start(), calls=%async_computation.6 | async-start | bytes 2359296 | tf_op jit(solution)/shard_map/all_gather | solution.py:470
  468.5 29.3 %collective-permute-start.36 = (bf16[2,128,2048]{2,1,0:T(8,128)(2,1)S(1)}, bf16[2,128,2048]{2,1,0:T(8,128)(2,1)S(1)}, u32[]{:S(2)}, u32[]{:S(2)}) collective-permute-start(bf16[2,128,2048]{2,1,0:T(8,128)(2,1)S(1)} %dynamic-slice_bitcast_fusion), channel_id=1, source_target_pairs={{0,16},{4,20},{8,24},{12,28},{16,0},{20,4},{24,8},{28,12},{1,17},{... | collective-permute-start | bytes 3145736 | tf_op jit(solution)/shard_map/ppermute | solution.py:260
  470.4 53.7 %collective-permute-start.25 = (bf16[512,4096]{1,0:T(8,128)(2,1)S(1)}, bf16[512,4096]{1,0:T(8,128)(2,1)}, u32[]{:S(2)}, u32[]{:S(2)}) collective-permute-start(bf16[512,4096]{1,0:T(8,128)(2,1)S(1)} %pad_maximum_fusion), channel_id=1, source_target_pairs={{0,4},{4,0},{8,12},{12,8},{16,20},{20,16},{24,28},{28,24},{1,5},{5... | collective-permute-start | bytes 12582920 | tf_op jit(solution)/shard_map/ppermute | solution.py:260
  473.2 26.3 %collective-permute-start.34 = (bf16[2,128,2048]{2,1,0:T(8,128)(2,1)S(1)}, bf16[2,128,2048]{2,1,0:T(8,128)(2,1)S(1)}, u32[]{:S(2)}, u32[]{:S(2)}) collective-permute-start(bf16[2,128,2048]{2,1,0:T(8,128)(2,1)S(1)} %dynamic-slice_bitcast_fusion.1), channel_id=1, source_target_pairs={{0,8},{4,12},{8,0},{12,4},{16,24},{20,28},{24,16},{28,20},{1,9},{5... | collective-permute-start | bytes 3145736 | tf_op jit(solution)/shard_map/ppermute | solution.py:260
  533.5 30.1 %collective-permute-start.26 = (bf16[2,128,2048]{2,1,0:T(8,128)(2,1)}, bf16[2,128,2048]{2,1,0:T(8,128)(2,1)}, u32[]{:S(2)}, u32[]{:S(2)}) collective-permute-start(bf16[2,128,2048]{2,1,0:T(8,128)(2,1)} %dynamic-slice_bitcast_fusion.3), channel_id=1, source_target_pairs={{0,8},{4,12},{8,0},{12,4},{16,24},{20,28},{24,16},{28,20},{1,9},{5... | collective-permute-start | bytes 3145736 | tf_op jit(solution)/shard_map/ppermute | solution.py:260
  537.1 306.7 %all-gather.13.cloned.1.call-start = ((), (), s32[]{:S(2)}) async-start(), calls=%async_computation.5 | async-start | bytes 2359296 | tf_op jit(solution)/shard_map/all_gather | solution.py:470
  601.3 247.5 %all-gather.17.cloned.1.call-start = ((), (), s32[]{:S(2)}) async-start(), calls=%async_computation.9 | async-start | bytes 4718592 | tf_op jit(solution)/shard_map/all_gather | solution.py:470
  632.0 43.0 %collective-permute-start.16 = (bf16[512,1024]{1,0:T(8,128)(2,1)}, bf16[512,1024]{1,0:T(8,128)(2,1)}, u32[]{:S(2)}, u32[]{:S(2)}) collective-permute-start(bf16[512,1024]{1,0:T(8,128)(2,1)} %constant_dynamic-slice_fusion.13), channel_id=1, source_target_pairs={{0,1},{1,0},{2,3},{3,2},{4,5},{5,4},{6,7},{7,6},{8,9},{9,8},{10,11... | collective-permute-start | bytes 3145736 | tf_op jit(solution)/shard_map/ppermute | solution.py:485
  672.3 28.7 %collective-permute-start.12 = (bf16[512,1024]{1,0:T(8,128)(2,1)}, bf16[512,1024]{1,0:T(8,128)(2,1)}, u32[]{:S(2)}, u32[]{:S(2)}) collective-permute-start(bf16[512,1024]{1,0:T(8,128)(2,1)} %pad_maximum_fusion.5), channel_id=1, source_target_pairs={{0,1},{1,0},{2,3},{3,2},{4,5},{5,4},{6,7},{7,6},{8,9},{9,8},{10,11... | collective-permute-start | bytes 3145736 | tf_op jit(solution)/shard_map/ppermute | solution.py:485
  677.0 46.4 %collective-permute-start.17 = (bf16[512,1024]{1,0:T(8,128)(2,1)S(1)}, bf16[512,1024]{1,0:T(8,128)(2,1)}, u32[]{:S(2)}, u32[]{:S(2)}) collective-permute-start(bf16[512,1024]{1,0:T(8,128)(2,1)S(1)} %add_convert_fusion.6.refs_0_), channel_id=1, source_target_pairs={{0,1},{1,2},{2,3},{3,0},{4,5},{5,6},{6,7},{7,4},{8,9},{9,10},{10,1... | collective-permute-start | bytes 3145736 | tf_op jit(solution)/shard_map/ppermute | solution.py:265
  706.7 39.2 %collective-permute-start.13 = (bf16[512,1024]{1,0:T(8,128)(2,1)}, bf16[512,1024]{1,0:T(8,128)(2,1)}, u32[]{:S(2)}, u32[]{:S(2)}) collective-permute-start(bf16[512,1024]{1,0:T(8,128)(2,1)} %add_convert_fusion.7.refs_0_), channel_id=1, source_target_pairs={{0,1},{1,2},{2,3},{3,0},{4,5},{5,6},{6,7},{7,4},{8,9},{9,10},{10,1... | collective-permute-start | bytes 3145736 | tf_op jit(solution)/shard_map/ppermute | solution.py:265
  723.4 44.9 %collective-permute-start.18 = (bf16[512,1024]{1,0:T(8,128)(2,1)}, bf16[512,1024]{1,0:T(8,128)(2,1)}, u32[]{:S(2)}, u32[]{:S(2)}) collective-permute-start(bf16[512,1024]{1,0:T(8,128)(2,1)} %collective-permute-done.17.refs_1_), channel_id=1, source_target_pairs={{0,1},{1,2},{2,3},{3,0},{4,5},{5,6},{6,7},{7,4},{8,9},{9,10},{10,1... | collective-permute-start | bytes 3145736 | tf_op jit(solution)/shard_map/ppermute | solution.py:265
  745.9 44.9 %collective-permute-start.14 = (bf16[512,1024]{1,0:T(8,128)(2,1)}, bf16[512,1024]{1,0:T(8,128)(2,1)}, u32[]{:S(2)}, u32[]{:S(2)}) collective-permute-start(bf16[512,1024]{1,0:T(8,128)(2,1)} %collective-permute-done.13.refs_1_), channel_id=1, source_target_pairs={{0,1},{1,2},{2,3},{3,0},{4,5},{5,6},{6,7},{7,4},{8,9},{9,10},{10,1... | collective-permute-start | bytes 3145736 | tf_op jit(solution)/shard_map/ppermute | solution.py:265
  768.3 49.7 %collective-permute-start.19 = (bf16[512,1024]{1,0:T(8,128)(2,1)}, bf16[512,1024]{1,0:T(8,128)(2,1)S(1)}, u32[]{:S(2)}, u32[]{:S(2)}) collective-permute-start(bf16[512,1024]{1,0:T(8,128)(2,1)} %collective-permute-done.18.refs_2_), channel_id=1, source_target_pairs={{0,1},{1,2},{2,3},{3,0},{4,5},{5,6},{6,7},{7,4},{8,9},{9,10},{10,1... | collective-permute-start | bytes 3145736 | tf_op jit(solution)/shard_map/ppermute | solution.py:265
  790.8 39.0 %collective-permute-start.15 = (bf16[512,1024]{1,0:T(8,128)(2,1)}, bf16[512,1024]{1,0:T(8,128)(2,1)}, u32[]{:S(2)}, u32[]{:S(2)}) collective-permute-start(bf16[512,1024]{1,0:T(8,128)(2,1)} %collective-permute-done.14.refs_2_), channel_id=1, source_target_pairs={{0,1},{1,2},{2,3},{3,0},{4,5},{5,6},{6,7},{7,4},{8,9},{9,10},{10,1... | collective-permute-start | bytes 3145736 | tf_op jit(solution)/shard_map/ppermute | solution.py:265
  (129 other events, 1067.4 us)
Sparse Core Ops, SparseCore 0:
  40.1 43.4 all-gather.6
  86.1 54.4 all-gather.8
  143.0 98.7 all-gather.10
  280.3 71.2 reduce-scatter.4
  404.9 77.2 reduce-scatter.2
  537.2 34.6 all-gather.14
  601.4 29.0 all-gather.12
  664.3 37.5 all-gather.16

commit v2 on v1

v2 whole, which is shorter than its diff:
```python
import functools

import jax
import jax.numpy as jnp
from jax import lax
from jax.experimental import pallas as pl
from jax.experimental.pallas import tpu as pltpu
from jax.sharding import PartitionSpec as P

neg_fill = -1000000000.0
open_cap = 3e38
eps_norm = 1e-05
PAIR = 128
HALF = 64
QUERY_SCALE = 0.125
ROOT = 0.7978845608028654
CUBE = 0.044715
f32 = jnp.float32
bf16 = jnp.bfloat16
ROW, FIRST, SECOND, TARGET, SOURCE, PLANE, CORE = range(7)


def low(value):
    return value.astype(bf16)


def nn(left, right):
    return lax.dot_general(left, right, (((1,), (0,)), ((), ())), preferred_element_type=f32)


def nt(left, right):
    return lax.dot_general(left, right, (((1,), (1,)), ((), ())), preferred_element_type=f32)


def tn(left, right):
    return lax.dot_general(left, right, (((0,), (0,)), ((), ())), preferred_element_type=f32)


def after(value, *others):
    return lax.optimization_barrier((value,) + others)[0]


def wall(*values):
    return lax.optimization_barrier(values)


def call(kernel, info, grid, ins, outs, scratch=(), micros=1.0):
    return pl.pallas_call(
        kernel,
        out_shape=tuple(jax.ShapeDtypeStruct(s, t) for s, t, _, _ in outs),
        grid_spec=pltpu.PrefetchScalarGridSpec(
            num_scalar_prefetch=1,
            grid=grid,
            in_specs=[pl.BlockSpec(b, m) for _, b, m in ins],
            out_specs=tuple(pl.BlockSpec(b, m) for _, _, b, m in outs),
            scratch_shapes=list(scratch),
        ),
        compiler_params=pltpu.CompilerParams(vmem_limit_bytes=52 << 20),
        cost_estimate=pl.CostEstimate(flops=int(micros * 1e7), bytes_accessed=1 << 10, transcendentals=0),
    )(info, *(a for a, _, _ in ins))


def rows_of_eight(values):
    return jnp.sum(values.reshape(values.shape[0] // 8, 8, values.shape[1]), axis=0)


def norm_stats(values):
    centre = jnp.mean(values, axis=-1, keepdims=True)
    offset = values - centre
    spread = jnp.mean(offset * offset, axis=-1, keepdims=True)
    scale = lax.rsqrt(spread + eps_norm)
    return offset * scale, scale


def norm_back(values, gain, grad):
    hat, scale = norm_stats(values)
    scaled = grad * gain
    mean_one = jnp.mean(scaled, axis=-1, keepdims=True)
    mean_two = jnp.mean(scaled * hat, axis=-1, keepdims=True)
    return scale * (scaled - mean_one - hat * mean_two), grad * hat


def head_halves(both):
    lane = lax.broadcasted_iota(jnp.int32, both.shape, 1)
    zero = jnp.zeros_like(both)
    return jnp.where(lane < HALF, both, zero), jnp.where(lane < HALF, zero, both)


def fill_caps(info, cap_ref, block, causal):
    length = cap_ref.shape[0]
    for t in range(2):
        keys = lax.broadcasted_iota(jnp.int32, (length, block), 0)
        allowed = keys < info[TARGET if causal else SOURCE]
        if causal:
            places = lax.broadcasted_iota(jnp.int32, (length, block), 1) + info[FIRST + t] * block
            allowed = allowed & (keys <= places)
        cap_ref[:, t * block : (t + 1) * block] = jnp.where(allowed, open_cap, neg_fill)


def forward_kernel(info, q_ref, k_ref, v_ref, o_ref, lse_ref, cap_ref, s_ref, *, block, causal, chunk):
    length = k_ref.shape[0]

    @pl.when(pl.program_id(0) == 0)
    def _():
        fill_caps(info, cap_ref, block, causal)

    for t in (1, 0):
        rows = slice(t * block, (t + 1) * block)
        span = length // 2 if (causal and t == 0) else length
        queries = jnp.concatenate(head_halves(q_ref[rows, :] * bf16(QUERY_SCALE)), axis=0)
        most = jnp.full((8, 2 * block), -open_cap, f32)
        for c in range(0, span, chunk):
            keys = slice(c, c + chunk)
            cap = cap_ref[keys, rows]
            scores = jnp.minimum(nt(k_ref[keys, :], queries), jnp.concatenate([cap, cap], axis=1))
            s_ref[t, keys, :] = scores
            most = jnp.maximum(most, jnp.max(scores.reshape(chunk // 8, 8, 2 * block), axis=0))
        most = jnp.max(most, axis=0, keepdims=True)
        total = jnp.zeros((8, 2 * block), f32)
        mixed = jnp.zeros((PAIR, 2 * block), f32)
        for c in range(0, span, chunk):
            keys = slice(c, c + chunk)
            weights = jnp.exp(s_ref[t, keys, :] - most)
            total = total + rows_of_eight(weights)
            mixed = mixed + tn(v_ref[keys, :], low(weights))
        total = jnp.sum(total, axis=0, keepdims=True)
        mixed = mixed / total
        sub = lax.broadcasted_iota(jnp.int32, (PAIR, block), 0)
        o_ref[rows, :] = low(jnp.where(sub < HALF, mixed[:, :block], mixed[:, block:]).T)
        lse = most + jnp.log(total)
        lse_ref[0, 0:1, rows] = lse[:, :block]
        lse_ref[0, 1:2, rows] = lse[:, block:]


def backward_kernel(
    info, q_ref, k_ref, v_ref, o_ref, g_ref, lse_ref, dq_ref, dk_ref, dv_ref, qs_ref, vs_ref, cap_ref, dk_acc, dv_acc,
    *, block, causal, chunk
):
    length = k_ref.shape[0]

    @pl.when(pl.program_id(0) == 0)
    def _():
        fill_caps(info, cap_ref, block, causal)

    q_sums = jnp.zeros((8, PAIR), f32)
    for t in (1, 0):
        rows = slice(t * block, (t + 1) * block)
        span = length // 2 if (causal and t == 0) else length
        grads = g_ref[rows, :]
        prod = (grads.astype(f32) * o_ref[rows, :].astype(f32)).T
        centre = jnp.concatenate(
            [jnp.sum(prod[:HALF], axis=0, keepdims=True), jnp.sum(prod[HALF:], axis=0, keepdims=True)], axis=1
        )
        lse = jnp.concatenate([lse_ref[0, 0:1, rows], lse_ref[0, 1:2, rows]], axis=1)
        queries = jnp.concatenate(head_halves(q_ref[rows, :] * bf16(QUERY_SCALE)), axis=0)
        grads = jnp.concatenate(head_halves(grads), axis=0)
        dq = jnp.zeros((PAIR, 2 * block), f32)
        for c in range(0, span, chunk):
            keys = slice(c, c + chunk)
            k, v = k_ref[keys, :], v_ref[keys, :]
            cap = cap_ref[keys, rows]
            scores = jnp.minimum(nt(k, queries), jnp.concatenate([cap, cap], axis=1))
            probs = jnp.exp(scores - lse)
            grad_scores = low(probs * (nt(v, grads) - centre))
            dv = nn(low(probs), grads)
            dk = nn(grad_scores, queries)
            dq = dq + tn(k, grad_scores)
            if t == 1:
                dk_acc[keys, :] = dk
                dv_acc[keys, :] = dv
            else:
                dk_acc[keys, :] += dk
                dv_acc[keys, :] += dv
        sub = lax.broadcasted_iota(jnp.int32, (PAIR, block), 0)
        dq = jnp.where(sub < HALF, dq[:, :block], dq[:, block:]) * QUERY_SCALE
        dq = low(dq.T)
        dq_ref[rows, :] = dq
        q_sums = q_sums + rows_of_eight(dq.astype(f32))
    dk_ref[...] = low(dk_acc[...])
    dv = low(dv_acc[...])
    dv_ref[...] = dv
    qs_ref[...] = q_sums
    vs_ref[...] = rows_of_eight(dv.astype(f32))


def attend_forward(info, query, keys, values, causal):
    queries, width = query.shape
    length = keys.shape[0]
    here = lambda i, _: (0, i)
    return call(
        functools.partial(forward_kernel, block=queries // 2, causal=causal, chunk=min(256, length // 2)),
        info,
        (width // PAIR,),
        [(query, (queries, PAIR), here), (keys, (length, PAIR), here), (values, (length, PAIR), here)],
        [
            ((queries, width), bf16, (queries, PAIR), here),
            ((width // PAIR, 8, queries), f32, (1, 8, queries), lambda i, _: (i, 0, 0)),
        ],
        [pltpu.VMEM((length, queries), f32), pltpu.VMEM((2, length, queries), f32)],
        micros=16,
    )


def attend_backward(info, query, keys, values, mixed, grad, lse_rows, causal):
    queries, width = query.shape
    length = keys.shape[0]
    here = lambda i, _: (0, i)
    one, key = (queries, PAIR), (length, PAIR)
    return call(
        functools.partial(backward_kernel, block=queries // 2, causal=causal, chunk=min(256, length // 2)),
        info,
        (width // PAIR,),
        [
            (query, one, here),
            (keys, key, here),
            (values, key, here),
            (mixed, one, here),
            (grad, one, here),
            (lse_rows, (1, 8, queries), lambda i, _: (i, 0, 0)),
        ],
        [
            ((queries, width), bf16, one, here),
            ((length, width), bf16, key, here),
            ((length, width), bf16, key, here),
            ((8, width), f32, (8, PAIR), here),
            ((8, width), f32, (8, PAIR), here),
        ],
        [pltpu.VMEM((length, queries), f32), pltpu.VMEM((length, PAIR), f32), pltpu.VMEM((length, PAIR), f32)],
        micros=24,
    )


def order_kernel(info, same_ref, other_ref, out_ref, *, part_of):
    mine = lax.rem(part_of(pl.program_id(0)), 2) == info[CORE]

    @pl.when(mine)
    def _():
        out_ref[...] = same_ref[...].astype(out_ref.dtype)

    @pl.when(jnp.logical_not(mine))
    def _():
        out_ref[...] = other_ref[...].astype(out_ref.dtype)


def order_rows(info, found, got, rows, group, pieces, kind):
    half, width = got.shape
    steps = group * pieces
    block = half // (rows * steps // 2)

    def part_of(i):
        b = lax.rem(i, steps)
        return jnp.where(b >= group, steps - 1 - b, b)

    def source(i):
        late = (lax.rem(i, steps) >= group).astype(jnp.int32)
        return (lax.div(i, steps) * (group // 2) + lax.div(part_of(i), 2)) * pieces + late

    return call(
        functools.partial(order_kernel, part_of=part_of),
        info,
        (rows * steps,),
        [
            (found, (block, width), lambda i, info: (source(i) + info[CORE] * (half // block), 0)),
            (got, (block, width), lambda i, _: (source(i), 0)),
        ],
        [((2 * half, width), kind, (block, width), lambda i, _: (i, 0))],
        micros=4,
    )[0]


def entry_kernel(info, x_ref, gain_ref, shift_ref, h_ref, *, which):
    hat, _ = norm_stats(x_ref[...].astype(f32))
    one = slice(which, which + 1)
    h_ref[...] = low(hat * gain_ref[one, :].astype(f32) + shift_ref[one, :].astype(f32))


def entry_norm(info, tokens, gains, shifts):
    _, length, width = tokens.shape
    tile = min(256, length)
    whole = lambda i, _: (0, 0)
    return call(
        functools.partial(entry_kernel, which=0),
        info,
        (length // tile,),
        [
            (tokens, (None, tile, width), lambda i, info: (info[ROW], i, 0)),
            (gains, gains.shape, whole),
            (shifts, shifts.shape, whole),
        ],
        [((length, width), bf16, (tile, width), lambda i, _: (i, 0))],
        micros=3,
    )[0]


def weight_ins(weight, slots):
    own, lead, rest, place = weight
    depth = rest.shape[0]
    wide = own.shape[1] * own.shape[2] // depth
    return [
        (own, (None,) + own.shape[1:], lambda *_: (lead, 0, 0)),
        (rest, (depth, (slots - 1) * wide), lambda *_: (0, place)),
    ]


def project_kernel(info, x_ref, own_ref, rest_ref, *others, flipped):
    x = x_ref[...]
    mine = nt(x, own_ref[...]) if flipped else nn(x, own_ref[...])
    wide = mine.shape[1]
    rest = nn(x, rest_ref[...])
    out_ref = others[-1]
    if len(others) > 1:
        mine = mine + others[0][:, :wide]
        rest = rest + others[0][:, wide:]
    out_ref[:, :wide] = low(mine)
    out_ref[:, wide:] = low(rest)


def project(info, x, place_of, tiles, weight, bias, slots, flipped=False):
    count, tile = tiles
    depth = x.shape[2]
    ins = [(x, (None, tile, depth), lambda i, info: place_of(i, info) + (0,))] + weight_ins(weight, slots)
    own = weight[0]
    width = slots * (own.shape[1] * own.shape[2] // depth)
    if bias is not None:
        ins.append((bias, bias.shape, lambda i, _: (0, 0)))
    return call(
        functools.partial(project_kernel, flipped=flipped),
        info,
        (count,),
        ins,
        [((count * tile, width), bf16, (tile, width), lambda i, _: (i, 0))],
        micros=2.5 * count * tile / 1024,
    )[0]


def mix_kernel(info, x_ref, own_ref, rest_ref, resid_ref, bias_ref, gain_ref, shift_ref, sum_ref, h_ref, *, which):
    wide = own_ref.shape[0]
    found = nn(x_ref[:, :wide], own_ref[...]) + nt(x_ref[:, wide:], rest_ref[...])
    found = resid_ref[...].astype(f32) + found + bias_ref[which : which + 1, :].astype(f32)
    sum_ref[...] = found
    hat, _ = norm_stats(found)
    one = slice(which + 1, which + 2)
    h_ref[...] = low(hat * gain_ref[one, :].astype(f32) + shift_ref[one, :].astype(f32))


def mix(info, x, weight, resid, resid_place, biases, gains, shifts, which, slots):
    rows, width = x.shape
    block = rows // 2
    whole = lambda i, _: (0, 0)
    here = lambda i, _: (i, 0)
    depth = resid.shape[2]
    return call(
        functools.partial(mix_kernel, which=which),
        info,
        (2,),
        [(x, (block, width), here)]
        + weight_ins(weight, slots)
        + [
            (resid, (None, block, depth), lambda i, info: resid_place(i, info) + (0,)),
            (biases, biases.shape, whole),
            (gains, gains.shape, whole),
            (shifts, shifts.shape, whole),
        ],
        [((rows, depth), f32, (block, depth), here), ((rows, depth), bf16, (block, depth), here)],
        micros=4,
    )


def back_dots(pairs):
    total = None
    for x_ref, own_ref, rest_ref in pairs:
        wide = own_ref.shape[1]
        found = nt(x_ref[:, :wide], own_ref[...]) + nt(x_ref[:, wide:], rest_ref[...])
        total = found if total is None else total + found
    return total


def back_kernel(info, *refs, count):
    pairs = [refs[3 * j : 3 * j + 3] for j in range(count)]
    refs[-1][...] = low(back_dots(pairs))


def back(info, terms, slots):
    rows, width = terms[0][0].shape
    depth = terms[0][1][2].shape[0]
    tile = min(256, rows)
    ins = []
    for x, weight in terms:
        ins += [(x, (tile, width), lambda i, _: (i, 0))] + weight_ins(weight, slots)
    return call(
        functools.partial(back_kernel, count=len(terms)),
        info,
        (rows // tile,),
        ins,
        [((rows, depth), bf16, (tile, depth), lambda i, _: (i, 0))],
        micros=5,
    )[0]


def back_norm_kernel(info, *refs, extras, which, keep):
    x_ref, own_ref, rest_ref = refs[:3]
    extra = refs[3 : 3 + extras]
    v_ref, add_ref, gain_ref = refs[3 + extras : 6 + extras]
    outs = refs[6 + extras :]
    grad = back_dots([(x_ref, own_ref, rest_ref)])
    for e in extra:
        grad = grad + e[...].astype(f32)
    found, to_gain = norm_back(v_ref[...].astype(f32), gain_ref[which : which + 1, :].astype(f32), grad)
    found = add_ref[...] + found
    low_found = low(found)
    if keep:
        outs[0][...] = found
    outs[-2][...] = low_found
    sums = jnp.concatenate([rows_of_eight(to_gain), rows_of_eight(grad), rows_of_eight(low_found.astype(f32))])

    @pl.when(pl.program_id(0) == 0)
    def _():
        outs[-1][...] = sums

    @pl.when(pl.program_id(0) > 0)
    def _():
        outs[-1][...] += sums


def back_norm(info, x, weight, extras, values, values_place, add, gains, which, slots, keep):
    rows, width = x.shape
    block = rows // 2
    depth = add.shape[1]
    here = lambda i, _: (i, 0)
    whole = lambda i, _: (0, 0)
    one = (block, depth)
    outs = [((rows, depth), bf16, one, here), ((24, depth), f32, (24, depth), whole)]
    if keep:
        outs = [((rows, depth), f32, one, here)] + outs
    return call(
        functools.partial(back_norm_kernel, extras=len(extras), which=which, keep=keep),
        info,
        (2,),
        [(x, (block, width), here)]
        + weight_ins(weight, slots)
        + [(e, one, here) for e in extras]
        + [
            (values, (None, block, depth), lambda i, info: values_place(i, info) + (0,)),
            (add, one, here),
            (gains, gains.shape, whole),
        ],
        outs,
        micros=4,
    )


def feed_kernel(
    info, h_ref, c0_ref, c1_ref, second_ref, upo_ref, downo_ref, upr_ref, downr_ref, ub_ref, bias_ref, gain_ref,
    a_ref, du_ref, us_ref, final_ref, g_ref, e_ref, sums_ref, out_acc, dh_acc, *, own_tiles
):
    i = pl.program_id(0)
    block = c0_ref.shape[0]
    cots = (c0_ref, c1_ref)
    which = 2

    def tile(own):
        sums = None
        for t in range(2):
            rows = slice(t * block, (t + 1) * block)
            up = upo_ref[...] if own else upr_ref[...]
            pre = nn(h_ref[rows, :], up) + ub_ref[...]
            square = pre * pre
            curve = jnp.tanh(ROOT * (pre + CUBE * square * pre))
            act = low(0.5 * pre * (1.0 + curve))
            slope = 0.5 * (1.0 + curve) + 0.5 * pre * (1.0 - curve * curve) * (ROOT * (1.0 + 3.0 * CUBE * square))
            a_ref[rows, :] = act
            if own:
                grad = nt(cots[t][...], downo_ref[...])
                out = nn(act, downo_ref[...])
            else:
                grad = nn(cots[t][...], downr_ref[...])
                out = nt(act, downr_ref[...])
            du = low(slope * grad)
            du_ref[rows, :] = du
            part = rows_of_eight(du.astype(f32))
            sums = part if sums is None else sums + part
            dh = nt(du, up)
            first = i == 0
            if own:

                @pl.when(first)
                def _():
                    out_acc[rows, :] = out
                    dh_acc[rows, :] = dh

                @pl.when(jnp.logical_not(first))
                def _():
                    out_acc[rows, :] += out
                    dh_acc[rows, :] += dh
            else:
                out_acc[rows, :] += out
                dh_acc[rows, :] += dh
        us_ref[...] = sums

    @pl.when(i < own_tiles)
    def _():
        tile(True)

    @pl.when(i >= own_tiles)
    def _():
        tile(False)

    @pl.when(i == pl.num_programs(0) - 1)
    def _():
        sums = None
        gain = gain_ref[which : which + 1, :].astype(f32)
        for t in range(2):
            rows = slice(t * block, (t + 1) * block)
            second = second_ref[rows, :]
            final_ref[rows, :] = low(second + out_acc[rows, :] + bias_ref[which : which + 1, :].astype(f32))
            cot = cots[t][...].astype(f32)
            grad = dh_acc[rows, :]
            found, to_gain = norm_back(second, gain, grad)
            found = cot + found
            g_ref[rows, :] = found
            rounded = low(found)
            e_ref[rows, :] = rounded
            part = jnp.concatenate(
                [
                    rows_of_eight(to_gain),
                    rows_of_eight(grad),
                    rows_of_eight(rounded.astype(f32)),
                    rows_of_eight(cot),
                ]
            )
            sums = part if sums is None else sums + part
        sums_ref[...] = sums


def feed_forward(info, h, cotangent, second, up, down, up_bias, biases, gains, slots):
    rows, depth = h.shape
    block = rows // 2
    up_own, _, up_rest, up_place = up
    down_own, _, down_rest, down_place = down
    hidden = up_own.shape[2]
    tile = min(512, hidden)
    own_tiles = hidden // tile
    total = slots * own_tiles
    rest_tiles = (slots - 1) * own_tiles
    own_at = lambda i: jnp.minimum(i, own_tiles - 1)
    rest_at = lambda i: jnp.maximum(i - own_tiles, 0)
    whole = lambda i, _: (0, 0)
    full = (rows, depth)
    return call(
        functools.partial(feed_kernel, own_tiles=own_tiles),
        info,
        (total,),
        [
            (h, full, whole),
            (cotangent, (None, block, depth), lambda i, _: (0, 0, 0)),
            (cotangent, (None, block, depth), lambda i, _: (0, 1, 0)),
            (second, full, whole),
            (up_own, (None, depth, tile), lambda i, _: (0, 0, own_at(i))),
            (down_own, (None, tile, depth), lambda i, _: (0, own_at(i), 0)),
            (up_rest, (depth, tile), lambda i, _: (0, up_place * rest_tiles + rest_at(i))),
            (down_rest, (depth, tile), lambda i, _: (0, down_place * rest_tiles + rest_at(i))),
            (up_bias, (1, tile), lambda i, _: (0, i)),
            (biases, biases.shape, whole),
            (gains, gains.shape, whole),
        ],
        [
            ((rows, total * tile), bf16, (rows, tile), lambda i, _: (0, i)),
            ((rows, total * tile), bf16, (rows, tile), lambda i, _: (0, i)),
            ((8, total * tile), f32, (8, tile), lambda i, _: (0, i)),
            (full, bf16, full, whole),
            (full, f32, full, whole),
            (full, bf16, full, whole),
            ((32, depth), f32, (32, depth), whole),
        ],
        [pltpu.VMEM(full, f32), pltpu.VMEM(full, f32)],
        micros=32,
    )


def grad_kernel(info, *refs, plan, share, plane, mine):
    acts = refs[: sum(len(pieces) for pieces, _ in plan)]
    refs = refs[len(acts) :]
    grads = refs[: len(plan)]
    refs = refs[len(plan) :]
    got_ref = None
    if mine:
        got_ref, refs = refs[0], refs[1:]
    outs, turned = refs[: plane if mine else 1], refs[-len(plan) :]
    core = info[CORE] if mine else 1 - info[CORE]

    @pl.when(pl.program_id(0) == 0)
    def _():
        at = 0
        for t, (pieces, _) in enumerate(plan):
            start = 0
            for length in pieces:
                for r in range(plane):
                    if share % PAIR == 0:
                        block = 2 * jnp.bitwise_xor(info[PLANE], r) + core
                        cols = acts[at][:, pl.ds(pl.multiple_of(block * share, share), share)]
                    else:
                        cols = acts[at][:, r * share : (r + 1) * share]
                    turned[t][r * share : (r + 1) * share, start : start + length] = cols.T
                start += length
                at += 1

    first = 0
    for t, (_, wide) in enumerate(plan):
        cols = slice(first, first + wide)
        found = nn(turned[t][...], grads[t][...])
        if mine:
            found = low(found + got_ref[:, cols].astype(f32))
            for r in range(plane):
                outs[r][:, cols] = found[r * share : (r + 1) * share, :]
        else:
            outs[0][:, cols] = low(found)
        first += wide


def weight_grads(info, tensors, d, dp_size, slots, got=None):
    depth = tensors[0][0][0][0].shape[2]
    share, plane = depth // dp_size, dp_size // 2
    core = lax.rem(d, 2) if got is not None else 1 - lax.rem(d, 2)
    plan = [(tuple(rows for _, rows, _ in pieces), grad.shape[1] // slots) for pieces, grad in tensors]
    ins = []
    for pieces, _ in tensors:
        for array, rows, place in pieces:
            if share % PAIR == 0:
                ins.append((array, (None, rows, depth), lambda i, info, place=place: place(info) + (0,)))
            else:
                wide = array.reshape(array.shape[:2] + (plane, 2, share))
                wide = lax.dynamic_index_in_dim(wide, core, 3, keepdims=False)
                order = [jnp.bitwise_xor(d // 2, r) for r in range(plane)]
                wide = jnp.concatenate([lax.dynamic_index_in_dim(wide, b, 2) for b in order], axis=2)
                wide = wide.reshape(array.shape[:2] + (depth // 2,))
                ins.append((wide, (None, rows, depth // 2), lambda i, info, place=place: place(info) + (0,)))
    for (_, grad), (_, wide) in zip(tensors, plan):
        ins.append((grad, (grad.shape[0], wide), lambda i, _: (0, i)))
    half = depth // 2
    tile = sum(wide for _, wide in plan)
    if got is not None:
        ins.append((got, (half, tile), lambda i, _: (0, i)))
        outs = [((share, slots * tile), bf16, (share, tile), lambda i, _: (0, i))] * plane
    else:
        outs = [((half, slots * tile), bf16, (half, tile), lambda i, _: (0, i))]
    return call(
        functools.partial(grad_kernel, plan=plan, share=share, plane=plane, mine=got is not None),
        info,
        (slots,),
        ins,
        outs,
        [pltpu.VMEM((half, g.shape[0]), bf16) for _, g in tensors],
        micros=8,
    )


def finish_kernel(info, in_ref, out_ref, *, turn):
    value = in_ref[...].astype(f32)
    out_ref[...] = value.T if turn else value


def finish(info, full, places, wide, turn=False):
    depth = full.shape[0]
    first = places[0]
    if turn:
        tile, cut = min(256, depth), min(512, wide)
        return call(
            functools.partial(finish_kernel, turn=True),
            info,
            (depth // tile, wide // cut),
            [(full, (tile, cut), lambda i, j, _: (i, first * (wide // cut) + j))],
            [((wide, depth), f32, (cut, tile), lambda i, j, _: (j, i))],
            micros=3,
        )[0]
    tile = min(512, depth)
    return call(
        functools.partial(finish_kernel, turn=False),
        info,
        (len(places), depth // tile),
        [(full, (tile, wide), lambda i, j, _: (j, first + i))],
        [((len(places), depth, wide), f32, (None, tile, wide), lambda i, j, _: (i, j, 0))],
        micros=3,
    )[0]


def finish_pair_kernel(info, in_ref, q_ref, kv_ref, o_ref, s_ref, so_ref):
    wide = q_ref.shape[1]

    def cols(t):
        return in_ref[:, t * wide : (t + 1) * wide].astype(f32)

    q_ref[...] = cols(0)
    for t in range(2):
        kv_ref[t] = cols(1 + t)
    o_ref[...] = cols(3).T
    for t in range(3):
        s_ref[t] = cols(4 + t)
    so_ref[...] = cols(7).T


def finish_pair(info, full):
    depth = full.shape[0]
    wide = full.shape[1] // 8
    tile = min(256, depth)
    return call(
        finish_pair_kernel,
        info,
        (depth // tile,),
        [(full, (tile, 8 * wide), lambda i, _: (i, 0))],
        [
            ((depth, wide), f32, (tile, wide), lambda i, _: (i, 0)),
            ((2, depth, wide), f32, (2, tile, wide), lambda i, _: (0, i, 0)),
            ((wide, depth), f32, (wide, tile), lambda i, _: (0, i)),
            ((3, depth, wide), f32, (3, tile, wide), lambda i, _: (0, i, 0)),
            ((wide, depth), f32, (wide, tile), lambda i, _: (0, i)),
        ],
        micros=4,
    )


def build(dp_size, mp_size):
    ring = [(i, (i + 1) % mp_size) for i in range(mp_size)]
    dp_bits = dp_size.bit_length() - 1
    plane = dp_size // 2

    def flip(axis, size, bits):
        return lambda value: lax.ppermute(value, axis, [(i, i ^ bits) for i in range(size)])

    def shards(
        tokens,
        memory,
        target_lengths,
        source_lengths,
        cotangent,
        norm_gain,
        norm_bias,
        self_in,
        self_in_bias,
        self_out,
        cross_query,
        cross_kv,
        cross_bias,
        cross_out,
        out_bias,
        ffn_up,
        ffn_up_bias,
        ffn_down,
    ):
        rows, length, width = tokens.shape
        source = memory.shape[1]
        d = lax.axis_index("dp")
        z = lax.axis_index("mp")
        group = mp_size // rows
        core = lax.rem(d, 2)
        chips = group // 2
        chip_row = z // chips
        part = (z % chips) * 2 + core
        held = chip_row // rows == core
        row = lax.rem(chip_row, rows)
        block = length // (2 * group)
        share = width // dp_size
        per = width // mp_size
        hid = ffn_up.shape[1]
        swap = flip("dp", dp_size, 1)

        def across(mine, theirs):
            return jnp.where(held, mine, swap(theirs))

        def take_row(values):
            return lax.dynamic_index_in_dim(values, row, 0, keepdims=False)

        def blocks_of(values, p):
            return jnp.concatenate(
                [
                    lax.dynamic_slice_in_dim(values, s * block, block, 0)
                    for s in (p, 2 * group - 1 - p)
                ]
            )

        own_place = lambda i, info: (info[ROW], info[FIRST + i])
        own_h_place = lambda i, info: (0, info[FIRST + i])
        flat_place = lambda i, info: (0, i)
        row_place = lambda i, info: (info[ROW], i)

        def rows_of(weight):
            return lax.dynamic_slice_in_dim(weight, d * share, share, 0)

        def cols_of(weight):
            return lax.dynamic_slice_in_dim(weight, d * share, share, 1).T

        def with_bias(piece, bias):
            extra = jnp.zeros((16, piece.shape[1]), bf16)
            if bias is not None:
                extra = lax.dynamic_update_slice(extra, bias[None], (0, 0))
            return jnp.concatenate([piece, extra])

        def side_by_side(pieces):
            return jnp.concatenate([with_bias(p, b) for p, b in pieces], axis=1)

        def pass_on(value):
            return lax.ppermute(value, "mp", ring)

        def gather_rest(found, wides, *held):
            starts = [0]
            for w in wides:
                starts.append(starts[-1] + w)
            both = jnp.concatenate([s[:, a:b] for a, b in zip(starts[:-1], starts[1:]) for s in found], axis=1)
            ours = both[:share]
            if held:
                ours = after(ours, *held)
            return lax.all_gather(ours, "dp", axis=0, tiled=True), both[share : share + 1].astype(f32)

        def bias_of(own, biases, t, wide):
            far = (mp_size - 1) * wide
            return jnp.concatenate([own.astype(f32)[None], biases[:, t * far : (t + 1) * far]], axis=1)

        found_a = [
            pass_on(
                side_by_side(
                    [
                        (rows_of(self_in[0]), self_in_bias[0]),
                        (rows_of(self_in[1]), None),
                        (rows_of(self_in[2]), self_in_bias[1]),
                    ]
                )
            )
        ]
        lengths = jnp.stack([target_lengths[row], source_lengths[row]])
        lengths = across(lengths, lengths)
        tokens_row = take_row(tokens)
        tokens_row = across(tokens_row, tokens_row)[None]
        info = jnp.stack(
            [0 * part, part, 2 * group - 1 - part, lengths[0], lengths[1], d // 2, core]
        ).astype(jnp.int32)
        found_a[0], tokens_row, info = wall(found_a[0], tokens_row, info)
        for _ in range(mp_size - 2):
            found_a.append(pass_on(found_a[-1]))
        h1_row = entry_norm(info, tokens_row, norm_gain, norm_bias)
        memory_row = take_row(memory)
        memory_row = across(memory_row, memory_row)[None]
        cot_row = take_row(cotangent)
        cot_own = across(blocks_of(cot_row, part), blocks_of(cot_row, jnp.bitwise_xor(part, 1)))[None]
        found_a[-1], h1_row, memory_row, cot_own = wall(found_a[-1], h1_row, memory_row, cot_own)
        found_b = [
            after(
                side_by_side(
                    [
                        (cols_of(self_out), None),
                        (rows_of(cross_query), cross_bias[0]),
                        (rows_of(cross_kv[0]), None),
                        (rows_of(cross_kv[1]), cross_bias[1]),
                    ]
                ),
                found_a[-1],
            )
        ]
        for _ in range(mp_size - 1):
            found_b.append(pass_on(found_b[-1]))
        found_b = found_b[1:]
        rest_a, bias_a = gather_rest(found_a, [per] * 3)
        rest_b, bias_b = gather_rest(found_b, [per] * 4)
        w_q1, w_k1, w_v1 = [(self_in, t, rest_a, t) for t in range(3)]
        w_o1 = (self_out[None], 0, rest_b, 0)
        w_q2 = (cross_query[None], 0, rest_b, 1)
        w_k2, w_v2 = (cross_kv, 0, rest_b, 2), (cross_kv, 1, rest_b, 3)

        last_share = after(
            side_by_side(
                [(rows_of(ffn_up), ffn_up_bias), (cols_of(ffn_down), None), (cols_of(cross_out), None)]
            ),
            found_b[-1],
        )
        found_c = [pass_on(last_share)]
        far = min(256, length)
        h1_flat = h1_row[None]
        k1 = project(info, h1_flat, flat_place, (length // far, far), w_k1, None, mp_size)
        v1 = project(
            info, h1_flat, flat_place, (length // far, far), w_v1, bias_of(self_in_bias[1], bias_a, 2, per), mp_size
        )
        found_c[0], k1, v1 = wall(found_c[0], k1, v1)
        for _ in range(mp_size - 3):
            found_c.append(pass_on(found_c[-1]))
        q1 = project(info, h1_flat, own_h_place, (2, block), w_q1, bias_of(self_in_bias[0], bias_a, 0, per), mp_size)
        found_c[-1], q1 = wall(found_c[-1], q1)
        found_c.append(pass_on(found_c[-1]))
        rest_c, bias_c = gather_rest(found_c, [hid, hid, per])
        w_up, w_down = (ffn_up[None], 0, rest_c, 0), (ffn_down[None], 0, rest_c, 1)
        w_o2 = (cross_out[None], 0, rest_c, 2 * hid // per)
        o1, lse1 = attend_forward(info, q1, k1, v1, True)
        first, h2 = mix(info, o1, w_o1, tokens_row, own_place, out_bias, norm_gain, norm_bias, 0, mp_size)
        q2 = project(info, h2[None], flat_place, (2, block), w_q2, bias_of(cross_bias[0], bias_b, 1, per), mp_size)
        k2 = project(info, memory_row, row_place, (source // far, far), w_k2, None, mp_size)
        v2 = project(
            info, memory_row, row_place, (source // far, far), w_v2, bias_of(cross_bias[1], bias_b, 3, per), mp_size
        )
        o2, lse2 = attend_forward(info, q2, k2, v2, False)
        second, h3 = mix(info, o2, w_o2, first[None], flat_place, out_bias, norm_gain, norm_bias, 1, mp_size)
        hidden, grad_pre, up_sums, final, g2, e2, sums_three = feed_forward(
            info, h3, cot_own, second, w_up, w_down, bias_of(ffn_up_bias, bias_c, 0, hid), out_bias, norm_gain, mp_size
        )

        def to_plane(piece, r):
            return flip("dp", dp_size, 2 * r)(piece)

        def slots_of(total):
            wide = total[0].shape[1] // mp_size
            slots = []
            for k in range(mp_size):
                cols = slice(k * wide, (k + 1) * wide)
                slots.append(low(sum(t[:, cols].astype(f32) for t in total)))
            return slots

        def to_owners(slots):
            return [
                lax.ppermute(slots[k], "mp", [(i, (i - k) % mp_size) for i in range(mp_size)])
                for k in range(1, mp_size)
            ]

        def add_up(values):
            return low(sum(v.astype(f32) for v in values))

        def gather_grads(total):
            return lax.all_gather(total, "dp", axis=0, tiled=True)

        def gather_rows(mine):
            return lax.all_gather(mine, "mp", axis=0, tiled=True)

        def for_other(found):
            half = found.shape[0] // 2
            return swap(lax.dynamic_slice_in_dim(found, (1 - core) * half, half, 0))

        def own_blocks(array, lead):
            return [
                (array, block, lambda info, t=t: ((info[ROW] if lead else 0), info[FIRST + t])) for t in range(2)
            ]

        def all_rows(array, lead=False):
            return [(array, array.shape[1], lambda info: ((info[ROW] if lead else 0), 0))]

        def core_send(tensors):
            return weight_grads(info, tensors, d, dp_size, mp_size)[0]

        def to_core(sent):
            return flip("dp", dp_size, 1)(sent)

        def core_keep(tensors, got):
            return weight_grads(info, tensors, d, dp_size, mp_size, got)

        row_perm = [(i, (i // chips) * chips + (i % chips - 1) % chips) for i in range(mp_size)]

        def row_sum(piece_of):
            got = [swap(piece_of(2 * c + 1 - core)) for c in range(chips)]
            if chips == 1:
                return got[0], piece_of(part)
            pieces = jnp.stack([add_up([got[c], piece_of(2 * c + core)]) for c in range(chips)])
            place = z % chips
            total = lax.dynamic_index_in_dim(pieces, lax.rem(place + 1, chips), 0, keepdims=False)
            for k in range(chips - 2, -1, -1):
                total = lax.ppermute(total, "mp", row_perm)
                here = lax.dynamic_index_in_dim(pieces, lax.rem(place - k + chips, chips), 0, keepdims=False)
                if k:
                    total = add_up([total, here])
            return total, here

        def all_planes(kept):
            return [kept[0]] + [to_plane(kept[r], r) for r in range(1, plane)]

        output_found = gather_rows(final)
        ffn_tensors = [(all_rows(h3[None]), grad_pre), (all_rows(cot_own), hidden)]
        ffn_sent = core_send(ffn_tensors)
        e2, ffn_sent = wall(e2, ffn_sent)

        ffn_got = to_core(ffn_sent)
        do2 = project(info, e2[None], flat_place, (2, block), w_o2, None, mp_size, flipped=True)
        dq2, dk2, dv2, sum_q2, sum_v2 = attend_backward(info, q2, k2, v2, o2, do2, lse2, False)
        memory_part = back(info, [(dk2, w_k2), (dv2, w_v2)], mp_size)

        def memory_piece(p):
            return lax.dynamic_slice_in_dim(memory_part, p * (source // group), source // group, 0)

        ffn_got, memory_part, dq2 = wall(ffn_got, memory_part, dq2)
        memory_got, memory_here = row_sum(memory_piece)
        ffn_kept = core_keep(ffn_tensors, ffn_got)
        memory_got, dq2, *ffn_kept = wall(memory_got, dq2, *ffn_kept)
        memory_own = add_up([memory_got, memory_here])
        memory_found = gather_rows(memory_own)
        memory_own, dq2 = wall(memory_own, dq2)

        late = plane - 1
        ffn_total = [ffn_kept[0]] + [to_plane(ffn_kept[r], r) for r in range(1, late)]
        g1, e1, sums_two = back_norm(
            info, dq2, w_q2, [], first[None], flat_place, g2, norm_gain, 1, mp_size, True
        )
        do1 = project(info, e1[None], flat_place, (2, block), w_o1, None, mp_size, flipped=True)
        dq1, dk1, dv1, sum_q1, sum_v1 = attend_backward(info, q1, k1, v1, o1, do1, lse1, True)
        kv_part = back(info, [(dk1, w_k1), (dv1, w_v1)], mp_size)
        cross_tensors = [
            (all_rows(h2[None]), dq2),
            (all_rows(memory_row), dk2),
            (all_rows(memory_row), dv2),
            (all_rows(e2[None]), o2),
        ]
        cross_sent = core_send(cross_tensors)
        kv_part, cross_sent, last_kept, *ffn_total = wall(kv_part, cross_sent, ffn_kept[late], *ffn_total)

        def causal_piece(p):
            return blocks_of(kv_part, p)

        ffn_total = ffn_total + [to_plane(last_kept, late)]
        got, here = row_sum(causal_piece)
        cross_got = to_core(cross_sent)
        self_tensors = [
            (own_blocks(h1_flat, False), dq1),
            (all_rows(h1_flat), dk1),
            (all_rows(h1_flat), dv1),
            (all_rows(e1[None]), o1),
        ]
        self_sent = core_send(self_tensors)
        output_got = for_other(output_found)
        got, cross_got, self_sent, output_got = wall(got, cross_got, self_sent, output_got)
        tokens_own, sums_one = back_norm(
            info, dq1, w_q1, [got, here], tokens_row, own_place, g1, norm_gain, 0, mp_size, False
        )
        tokens_found = gather_rows(tokens_own)
        tokens_own, self_sent, cross_got = wall(tokens_own, self_sent, cross_got)
        self_got = to_core(self_sent)
        cross_kept = core_keep(cross_tensors, cross_got)
        output = order_rows(info, output_found, output_got, rows, group, 2, bf16).reshape(tokens.shape)
        self_got, output, *kept = wall(self_got, output, *cross_kept)
        cross_total = all_planes(kept)
        self_kept = core_keep(self_tensors, self_got)
        *self_kept, ffn_total[0], ffn_total[late] = wall(*self_kept, ffn_total[0], ffn_total[late])
        ffn_slots = slots_of(ffn_total)
        self_kept[0], *ffn_slots = wall(self_kept[0], *ffn_slots)
        self_total = all_planes(self_kept)
        ffn_total = [ffn_slots[0]] + to_owners(ffn_slots)
        memory_got = for_other(memory_found)
        memory_got, *cross_total = wall(memory_got, *cross_total)
        cross_slots = slots_of(cross_total)
        cross_total = [cross_slots[0]] + to_owners(cross_slots)
        memory_grad = order_rows(info, memory_found, memory_got, rows, group, 1, f32).reshape(memory.shape)
        memory_grad, *kept = wall(memory_grad, *self_total, *ffn_total)
        self_slots = slots_of(kept[:plane])
        self_total = [self_slots[0]] + to_owners(self_slots)
        ffn_full = gather_grads(add_up(kept[plane:]))
        up_grad, down_grad = finish(info, ffn_full, [0], hid)[0], finish(info, ffn_full, [1], hid, True)
        tokens_got = for_other(tokens_found)
        tokens_grad = order_rows(info, tokens_found, tokens_got, rows, group, 2, f32).reshape(tokens.shape)
        tokens_grad, up_grad, down_grad, *kept = wall(tokens_grad, up_grad, down_grad, *cross_total, *self_total)
        joint = jnp.concatenate([add_up(kept[:mp_size]), add_up(kept[mp_size:])], axis=1)
        joint_full = gather_grads(joint)

        def by_slot(sums):
            return jnp.sum(sums, axis=0).reshape(mp_size, -1)

        slot_sums = jnp.concatenate([by_slot(s) for s in (sum_q1, sum_v1, sum_q2, sum_v2, up_sums)], axis=1)
        flipped = slot_sums[::-1]
        twice = jnp.concatenate([flipped, flipped])
        in_order = lax.dynamic_slice_in_dim(twice, mp_size - 1 - z, mp_size, 0)
        whole = [
            jnp.sum(sums.reshape(-1, 8, width), axis=1) for sums in (sums_one, sums_two, sums_three)
        ]
        whole = jnp.concatenate(
            [w[0:1] for w in whole] + [w[1:2] for w in whole] + [whole[1][2:3], whole[2][2:3], whole[2][3:4]]
        )
        small = jnp.concatenate([in_order.reshape(-1, PAIR), whole.reshape(-1, PAIR)])
        for b in range(dp_bits):
            small = small + flip("dp", dp_size, 1 << b)(small)
        for b in range(mp_size.bit_length() - 1):
            small = small + flip("mp", mp_size, 1 << b)(small)
        small = small.reshape(-1)
        slot_part = small[: in_order.size].reshape(in_order.shape)
        mine = lax.dynamic_index_in_dim(slot_part, z, 0, keepdims=False)
        whole = small[in_order.size :].reshape(9, width)
        cross_q, cross_both, cross_o, self_three, self_o = finish_pair(info, joint_full)
        return (
            output,
            tokens_grad,
            memory_grad,
            whole[0:3],
            whole[3:6],
            self_three,
            jnp.stack([mine[:per], mine[per : 2 * per]]),
            self_o,
            cross_q,
            cross_both,
            jnp.stack([mine[2 * per : 3 * per], mine[3 * per : 4 * per]]),
            cross_o,
            whole[6:9],
            up_grad,
            mine[4 * per :],
            down_grad,
        )

    return shards


def solution(mesh):
    placed = (
        P("dp", None, None),
        P("dp", None, None),
        P("dp"),
        P("dp"),
        P("dp", None, None),
        P(),
        P(),
        P(None, None, "mp"),
        P(None, "mp"),
        P("mp", None),
        P(None, "mp"),
        P(None, None, "mp"),
        P(None, "mp"),
        P("mp", None),
        P(),
        P(None, "mp"),
        P("mp"),
        P("mp", None),
    )
    return jax.shard_map(
        build(mesh.shape["dp"], mesh.shape["mp"]),
        mesh=mesh,
        in_specs=placed,
        out_specs=(
            P("dp", None, None),
            P("dp", None, None),
            P("dp", None, None),
            P(),
            P(),
            P(None, None, "mp"),
            P(None, "mp"),
            P("mp", None),
            P(None, "mp"),
            P(None, None, "mp"),
            P(None, "mp"),
            P("mp", None),
            P(),
            P(None, "mp"),
            P("mp"),
            P("mp", None),
        ),
        check_vma=False,
    )
```

time: 873 us -> 677 us (0.78)
  Pallas kernels: 104 us -> 311 us
  matrix products: 162 us -> 0 us
  waiting for transfers between devices: 360 us -> 233 us
  local copies, waits for them, and re-layouts: 116 us -> 47.2 us
  other arithmetic: 57.7 us -> 32.2 us
  starting transfers between devices: 52.6 us -> 30.5 us
    pallas_call x7 -> x32, Pallas kernels: 104 us -> 311 us  [call(): pl.pallas_call(kernel, out_shape=tuple((jax.ShapeDtypeStruct(s, t) for s,...]
    ppermute x44, waiting for transfers between devices: 354 us -> 176 us  [the longest x9 74.1 us: to_owners(): lax.ppermute(slots[k], 'mp', [(i, (i - k) % mp_size) for i in range(mp_si...]
    dot_general x38 -> x0, matrix products: 162 us -> none  [the longest x10 58.4 us: nt(): lax.dot_general(left, right, (((1,), (1,)), ((), ())), preferred_element_...]
    unnamed x252 -> x144, local copies, waits for them, and re-layouts: 53.2 us -> 18.7 us
    all_gather x3 -> x6, waiting for transfers between devices: 5.08 us -> 39.4 us  [the longest x3 21.7 us: gather_rows(): return lax.all_gather(mine, 'mp', axis=0, tiled=True)]
    dynamic_slice x15 -> x7, local copies, waits for them, and re-layouts: 32.9 us -> 10.2 us  [the longest x3 6.77 us: for_other(): return swap(lax.dynamic_slice_in_dim(found, (1 - core) * half, half, 0))]
    ppermute x44, starting transfers between devices: 51.7 us -> 29.9 us  [the longest x26 16.5 us: flip(): lax.ppermute(value, axis, [(i, i ^ bits) for i in range(size)])]
    all_gather x3 -> x2, waiting for transfers between devices: 0.01 us -> 16.9 us  [gather_grads(): return lax.all_gather(total, 'dp', axis=0, tiled=True)]
  transfers between devices with their start and end apart: 52 -> 52, of which waited for: 36 -> 24; matrix products, arithmetic and copies ran while one was open for 30% -> 9% of each run, Pallas kernels for 12% -> 38%
where the time goes in v2:
time: 677 us; the launch traced here: 670 us
  Pallas kernels  311 us (46%)
  waiting for transfers between devices  233 us (34%)
  local copies, waits for them, and re-layouts  47.2 us (7%)
  other arithmetic  32.2 us (5%)
  starting transfers between devices  30.5 us (5%)
  between operations  15.7 us (2%)
    pallas_call x32, Pallas kernels, call(): pl.pallas_call(kernel, out_shape=tuple((jax.ShapeDtypeStruct(s, t) for s,...  311 us
    ppermute x9, waiting for transfers between devices, to_owners(): lax.ppermute(slots[k], 'mp', [(i, (i - k) % mp_size) for i in range(mp_si...  74.1 us
    ppermute x9, waiting for transfers between devices, pass_on(): return lax.ppermute(value, 'mp', ring)  70.1 us
    ppermute x26, waiting for transfers between devices, flip(): lax.ppermute(value, axis, [(i, i ^ bits) for i in range(size)])  32.2 us
    all_gather x3, waiting for transfers between devices, gather_rows(): return lax.all_gather(mine, 'mp', axis=0, tiled=True)  21.7 us
    unnamed x144, local copies, waits for them, and re-layouts  18.7 us
    all_gather x3, waiting for transfers between devices, gather_rest(): lax.all_gather(ours, 'dp', axis=0, tiled=True)  17.7 us
    all_gather x2, waiting for transfers between devices, gather_grads(): return lax.all_gather(total, 'dp', axis=0, tiled=True)  16.9 us
  transfers between devices with their start and end apart: 52, of which 24 were waited for; matrix products, arithmetic and copies ran while one was open for 9% of the time, Pallas kernels for 38%

profile of v2, /device:TPU:0, one launch (start us, length us, event | category | flops | bytes accessed | tf_op | source)
XLA Modules:
  0.0 669.6 jit_solution(1622949317927185191)
XLA Ops:
  40.6 9.0 %collective-permute-done.4 = bf16[144,768]{1,0:T(8,128)(2,1)S(1)} collective-permute-done((bf16[144,768]{1,0:T(8,128)(2,1)S(1)}, bf16[144,768]{1,0:T(8,128)(2,1)S(1)}, u32[]{:S(2)}, u32[]{:S(2)}) %collective-permute-start.4) | collective-permute-done | bytes 221216 | tf_op jit(solution)/shard_map/ppermute | solution.py:801
  53.5 10.3 %collective-permute-done.7 = bf16[144,1024]{1,0:T(8,128)(2,1)S(1)} collective-permute-done((bf16[144,1024]{1,0:T(8,128)(2,1)S(1)}, bf16[144,1024]{1,0:T(8,128)(2,1)S(1)}, u32[]{:S(2)}, u32[]{:S(2)}) %collective-permute-start.7) | collective-permute-done | bytes 294944 | tf_op jit(solution)/shard_map/ppermute | solution.py:801
  63.9 9.5 %collective-permute-done.8 = bf16[144,1024]{1,0:T(8,128)(2,1)S(1)} collective-permute-done((bf16[144,1024]{1,0:T(8,128)(2,1)S(1)}, bf16[144,1024]{1,0:T(8,128)(2,1)S(1)}, u32[]{:S(2)}, u32[]{:S(2)}) %collective-permute-start.8) | collective-permute-done | bytes 294944 | tf_op jit(solution)/shard_map/ppermute | solution.py:801
  108.2 12.5 %collective-permute-done.11 = bf16[144,2304]{1,0:T(8,128)(2,1)S(1)} collective-permute-done((bf16[144,2304]{1,0:T(8,128)(2,1)}, bf16[144,2304]{1,0:T(8,128)(2,1)S(1)}, u32[]{:S(2)}, u32[]{:S(2)}) %collective-permute-start.11) | collective-permute-done | bytes 663584 | tf_op jit(solution)/shard_map/ppermute | solution.py:801
  121.7 14.1 %collective-permute-done.12 = bf16[144,2304]{1,0:T(8,128)(2,1)S(1)} collective-permute-done((bf16[144,2304]{1,0:T(8,128)(2,1)S(1)}, bf16[144,2304]{1,0:T(8,128)(2,1)S(1)}, u32[]{:S(2)}, u32[]{:S(2)}) %collective-permute-start.12) | collective-permute-done | bytes 663584 | tf_op jit(solution)/shard_map/ppermute | solution.py:801
  140.3 15.1 %shard_map.301 = (bf16[512,1024]{1,0:T(8,128)(2,1)S(1)}, f32[8,8,512]{2,1,0:T(8,128)S(1)}) custom-call(s32[7]{0:T(128)S(1)} %stack.31.info, bf16[512,1024]{1,0:T(8,128)(2,1)} %copy-done.11, bf16[1024,1024]{1,0:T(8,128)(2,1)} %shard_map.298.k_ref, bf16[1024,1024]{1,0:T(8,128)(2,1)} %shard_map.299.v_ref), custom_call_target="tpu_custom_call" | custom-call | flops 160000000 | bytes 1024 | tf_op jit(solution)/shard_map/pallas_call | solution.py:48
  181.4 17.9 %shard_map.306 = (bf16[512,1024]{1,0:T(8,128)(2,1)S(1)}, f32[8,8,512]{2,1,0:T(8,128)S(1)}) custom-call(s32[7]{0:T(128)S(1)} %stack.31.info, bf16[512,1024]{1,0:T(8,128)(2,1)} %copy-done.12, bf16[1024,1024]{1,0:T(8,128)(2,1)} %shard_map.304.k_ref, bf16[1024,1024]{1,0:T(8,128)(2,1)} %shard_map.305.v_ref), custom_call_target="tpu_custom_call" | custom-call | flops 160000000 | bytes 1024 | tf_op jit(solution)/shard_map/pallas_call | solution.py:48
  200.3 17.7 %all-gather.13.cloned.1.call-done.rest_ref.upr_ref.downr_ref = bf16[1024,6912]{1,0:T(8,128)(2,1)} async-done(((bf16[128,6912]{1,0:T(8,128)(2,1)}), bf16[1024,6912]{1,0:T(8,128)(2,1)}) %all-gather.13.cloned.1.call-update) | async-done | bytes 14155792 | tf_op jit(solution)/shard_map/all_gather | solution.py:811
  224.4 32.6 %shard_map.308 = (bf16[512,4096]{1,0:T(8,128)(2,1)}, bf16[512,4096]{1,0:T(8,128)(2,1)}, f32[8,4096]{1,0:T(8,128)S(1)}, bf16[512,1024]{1,0:T(8,128)(2,1)S(1)}, f3...) custom-call(s32[7]{0:T(128)S(1)} %stack.31.info, bf16[512,1024]{1,0:T(8,128)(2,1)} %copy-done.13, ...), custom_call_target="tpu_custom_call" | custom-call | flops 320000000 | bytes 1024 | tf_op jit(solution)/shard_map/pallas_call | solution.py:48
  258.0 10.8 %shard_map.309 = bf16[512,8192]{1,0:T(8,128)(2,1)} custom-call(s32[7]{0:T(128)S(1)} %stack.31.info, bf16[1,512,1024]{2,1,0:T(8,128)(2,1)S(1)} %bitcast.66, bf16[1,512,1024]{2,1,0:T(8,128)(2,1)} %fusion.6.c0_ref.c1_ref.refs_1_, bf16[512,4096]{1,0:T(8,128)(2,1)} %get-tuple-element.164.refs_2_, bf16[512,4096]{1,0:T(8,128)(2,1)} %get-tuple-element.165.refs_3_), custom_call_target="tpu_custom_call" | custom-call | flops 80000000 | bytes 1024 | tf_op jit(solution)/shard_map/pallas_call | solution.py:48
  273.8 25.7 %shard_map.311 = (bf16[512,1024]{1,0:T(8,128)(2,1)S(1)}, bf16[1024,1024]{1,0:T(8,128)(2,1)}, bf16[1024,1024]{1,0:T(8,128)(2,1)}, f32[8,1024]{1,0:T(8,128)S(1)}, f32[8,1024]{1,0:T(8,128)S(1)}) custom-call(s32[7]{0:T(128)S(1)} %stack.31.info, bf16[512,1024]{1,0:T(8,128)(2,1)} %copy-done.12, bf16[1024,1024]{1,0:T(8,128)(2,1)} %shard_map.304.k_ref, ...), custom_call_target="tpu_custom_call" | custom-call | flops 240000000 | bytes 1024 | tf_op jit(solution)/shard_map/pallas_call | solution.py:48
  299.6 8.9 %shard_map.312 = bf16[1024,1024]{1,0:T(8,128)(2,1)} custom-call(s32[7]{0:T(128)S(1)} %stack.31.info, bf16[1024,1024]{1,0:T(8,128)(2,1)} %get-tuple-element.169.refs_0_.refs_5_, bf16[2,1024,256]{2,1,0:T(8,128)(2,1)S(1)} %copy-done.2, bf16[1024,3072]{1,0:T(8,128)(2,1)} %all-gather.11.cloned.1.call-done.rest_ref.refs_2_.refs_5_, ...), custom_call_target="tpu_custom_call" | custom-call | flops 50000000 | bytes 1024 | tf_op jit(solution)/shard_map/pallas_call | solution.py:48
  310.1 12.6 %shard_map.313 = (bf16[128,8192]{1,0:T(8,128)(2,1)}, bf16[128,8192]{1,0:T(8,128)(2,1)}, bf16[128,8192]{1,0:T(8,128)(2,1)}, bf16[128,8192]{1,0:T(8,128)(2,1)}) custom-call(s32[7]{0:T(128)S(1)} %stack.31.info, bf16[1,512,1024]{2,1,0:T(8,128)(2,1)S(1)} %bitcast.67, bf16[1,512,1024]{2,1,0:T(8,128)(2,1)} %fusion.6.c0_ref.c1_ref.refs_1_, ...), custom_call_target="tpu_custom_call" | custom-call | flops 80000000 | bytes 1024 | tf_op jit(solution)/shard_map/pallas_call | solution.py:48
  341.1 20.6 %shard_map.316 = (bf16[512,1024]{1,0:T(8,128)(2,1)S(1)}, bf16[1024,1024]{1,0:T(8,128)(2,1)}, bf16[1024,1024]{1,0:T(8,128)(2,1)}, f32[8,1024]{1,0:T(8,128)S(1)}, f32[8,1024]{1,0:T(8,128)S(1)}) custom-call(s32[7]{0:T(128)S(1)} %stack.31.info, bf16[512,1024]{1,0:T(8,128)(2,1)} %copy-done.11, bf16[1024,1024]{1,0:T(8,128)(2,1)} %shard_map.298.k_ref, ...), custom_call_target="tpu_custom_call" | custom-call | flops 240000000 | bytes 1024 | tf_op jit(solution)/shard_map/pallas_call | solution.py:48
  362.7 8.9 %shard_map.317 = bf16[1024,1024]{1,0:T(8,128)(2,1)} custom-call(s32[7]{0:T(128)S(1)} %stack.31.info, bf16[1024,1024]{1,0:T(8,128)(2,1)} %get-tuple-element.186.refs_0_.refs_6_, bf16[3,1024,256]{2,1,0:T(8,128)(2,1)S(1)} %copy-done.1, bf16[1024,2304]{1,0:T(8,128)(2,1)} %all-gather.9.cloned.1.call-done.rest_ref.refs_2_.refs_5_, ...), custom_call_target="tpu_custom_call" | custom-call | flops 50000000 | bytes 1024 | tf_op jit(solution)/shard_map/pallas_call | solution.py:48
  371.6 10.6 %shard_map.318 = bf16[512,4096]{1,0:T(8,128)(2,1)} custom-call(s32[7]{0:T(128)S(1)} %stack.31.info, bf16[1,512,1024]{2,1,0:T(8,128)(2,1)S(1)} %bitcast.65, bf16[1,1024,1024]{2,1,0:T(8,128)(2,1)} %select_bitcast_fusion.x_ref.refs_1_.refs_2_, bf16[1,1024,1024]{2,1,0:T(8,128)(2,1)} %select_bitcast_fusion.x_ref.refs_1_.refs_2_, bf16[1,512,1024]{2,1,0:T(8,128)(2,1)} %bitcast.86, ...), custom_call_target="tpu_custom_call" | custom-call | flops 80000000 | bytes 1024 | tf_op jit(solution)/shard_map/pallas_call | solution.py:48
  387.4 10.7 %shard_map.319 = bf16[512,4096]{1,0:T(8,128)(2,1)} custom-call(s32[7]{0:T(128)S(1)} %stack.31.info, bf16[1,1024,1024]{2,1,0:T(8,128)(2,1)} %bitcast.77, bf16[1,1024,1024]{2,1,0:T(8,128)(2,1)} %bitcast.78, bf16[1,1024,1024]{2,1,0:T(8,128)(2,1)} %bitcast.79, bf16[1,1024,1024]{2,1,0:T(8,128)(2,1)} %bitcast.80, bf16[1,512,1024]{2,1,0:T(8,128)(2,1)S(1)} %bitcast.62, ...), custom_call_target="tpu_custom_call" | custom-call | flops 80000000 | bytes 1024 | tf_op jit(solution)/shard_map/pallas_call | solution.py:48
  409.0 21.7 %all-gather.19.cloned.1.call-done.same_ref = bf16[2048,1024]{1,0:T(8,128)(2,1)} async-done(((bf16[512,1024]{1,0:T(8,128)(2,1)}), bf16[2048,1024]{1,0:T(8,128)(2,1)}) %all-gather.19.cloned.1.call-update) | async-done | bytes 4194320 | tf_op jit(solution)/shard_map/all_gather | solution.py:926
  440.6 11.8 %shard_map.322 = (bf16[128,4096]{1,0:T(8,128)(2,1)S(1)}, bf16[128,4096]{1,0:T(8,128)(2,1)}, bf16[128,4096]{1,0:T(8,128)(2,1)}, bf16[128,4096]{1,0:T(8,128)(2,1)}) custom-call(s32[7]{0:T(128)S(1)} %stack.31.info, bf16[1,512,1024]{2,1,0:T(8,128)(2,1)} %bitcast.64, bf16[1,1024,1024]{2,1,0:T(8,128)(2,1)} %select_bitcast_fusion.x_ref.refs_1_.refs_2_, ...), custom_call_target="tpu_custom_call" | custom-call | flops 80000000 | bytes 1024 | tf_op jit(solution)/shard_map/pallas_call | solution.py:48
  452.5 11.9 %shard_map.325 = (bf16[128,4096]{1,0:T(8,128)(2,1)S(1)}, bf16[128,4096]{1,0:T(8,128)(2,1)}, bf16[128,4096]{1,0:T(8,128)(2,1)}, bf16[128,4096]{1,0:T(8,128)(2,1)}) custom-call(s32[7]{0:T(128)S(1)} %stack.31.info, bf16[1,1024,1024]{2,1,0:T(8,128)(2,1)} %bitcast.81, bf16[1,1024,1024]{2,1,0:T(8,128)(2,1)} %bitcast.82, bf16[1,1024,1024]{2,1,0:T(8,128)(2,1)} %bitcast.83, ...), custom_call_target="tpu_custom_call" | custom-call | flops 80000000 | bytes 1024 | tf_op jit(solution)/shard_map/pallas_call | solution.py:48
  476.3 36.1 %collective-permute-done.30 = bf16[128,2048]{1,0:T(8,128)(2,1)S(1)} collective-permute-done((bf16[128,2048]{1,0:T(8,128)(2,1)S(1)}, bf16[128,2048]{1,0:T(8,128)(2,1)S(1)}, u32[]{:S(2)}, u32[]{:S(2)}) %collective-permute-start.30) | collective-permute-done | bytes 524320 | tf_op jit(solution)/shard_map/ppermute | solution.py:915
  529.3 27.1 %collective-permute-done.31 = bf16[128,2048]{1,0:T(8,128)(2,1)S(1)} collective-permute-done((bf16[128,2048]{1,0:T(8,128)(2,1)}, bf16[128,2048]{1,0:T(8,128)(2,1)S(1)}, u32[]{:S(2)}, u32[]{:S(2)}) %collective-permute-start.31) | collective-permute-done | bytes 524320 | tf_op jit(solution)/shard_map/ppermute | solution.py:915
  583.7 9.3 %shard_map.323 = f32[2048,1024]{1,0:T(8,128)} custom-call(s32[7]{0:T(128)S(1)} %stack.31.info, bf16[2048,1024]{1,0:T(8,128)(2,1)} %all-gather.17.cloned.1.call-done.same_ref, bf16[1024,1024]{1,0:T(8,128)(2,1)} %copy-done.38), custom_call_target="tpu_custom_call" | custom-call | flops 40000000 | bytes 1024 | tf_op jit(solution)/shard_map/pallas_call | solution.py:48
  646.4 9.5 %all-gather.23.cloned.1.call-done.in_ref = bf16[1024,2048]{1,0:T(8,128)(2,1)} async-done(((bf16[128,2048]{1,0:T(8,128)(2,1)}), bf16[1024,2048]{1,0:T(8,128)(2,1)}) %all-gather.23.cloned.1.call-update) | async-done | bytes 4194320 | tf_op jit(solution)/shard_map/all_gather | solution.py:923
  (363 shorter events, 279.2 us)
Async XLA Ops:
  7.2 82.4 %all-gather.9.cloned.1.call-start = ((), (), s32[]{:S(2)}) async-start(), calls=%async_computation | async-start | bytes 5308416 | tf_op jit(solution)/shard_map/all_gather | solution.py:811
  51.4 105.6 %all-gather.11.cloned.1.call-start = ((), (), s32[]{:S(2)}) async-start(), calls=%async_computation.1 | async-start | bytes 7077888 | tf_op jit(solution)/shard_map/all_gather | solution.py:811
  83.9 134.1 %all-gather.13.cloned.1.call-start = ((), (), s32[]{:S(2)}) async-start(), calls=%async_computation.2 | async-start | bytes 15925248 | tf_op jit(solution)/shard_map/all_gather | solution.py:811
  139.1 243.2 %all-gather.15.cloned.1.call-start = ((), (), s32[]{:S(2)}) async-start(), calls=%async_computation.3 | async-start | bytes 5242880 | tf_op jit(solution)/shard_map/all_gather | solution.py:926
  268.7 39.7 %collective-permute-start.13 = (bf16[512,8192]{1,0:T(8,128)(2,1)}, bf16[512,8192]{1,0:T(8,128)(2,1)}, u32[]{:S(2)}, u32[]{:S(2)}) collective-permute-start(bf16[512,8192]{1,0:T(8,128)(2,1)} %shard_map.309), channel_id=1, source_target_pairs={{0,4},{4,0},{8,12},{12,8},{16,20},{20,16},{24,28},{28,24},{1,5},{5... | collective-permute-start | bytes 25165832 | tf_op jit(solution)/shard_map/ppermute | solution.py:727
  269.0 161.7 %all-gather.19.cloned.1.call-start = ((), (), s32[]{:S(2)}) async-start(), calls=%async_computation.5 | async-start | bytes 5242880 | tf_op jit(solution)/shard_map/all_gather | solution.py:926
  323.7 58.5 %collective-permute-start.15 = (bf16[128,8192]{1,0:T(8,128)(2,1)}, bf16[128,8192]{1,0:T(8,128)(2,1)}, u32[]{:S(2)}, u32[]{:S(2)}) collective-permute-start(bf16[128,8192]{1,0:T(8,128)(2,1)} %get-tuple-element.190), channel_id=1, source_target_pairs={{0,8},{4,12},{8,0},{12,4},{16,24},{20,28},{24,16},{28,20},{1,9},{5... | collective-permute-start | bytes 6291464 | tf_op jit(solution)/shard_map/ppermute | solution.py:727
  325.1 57.1 %collective-permute-start.16 = (bf16[128,8192]{1,0:T(8,128)(2,1)}, bf16[128,8192]{1,0:T(8,128)(2,1)}, u32[]{:S(2)}, u32[]{:S(2)}) collective-permute-start(bf16[128,8192]{1,0:T(8,128)(2,1)} %get-tuple-element.191), channel_id=1, source_target_pairs={{0,16},{4,20},{8,24},{12,28},{16,0},{20,4},{24,8},{28,12},{1,17},{... | collective-permute-start | bytes 6291464 | tf_op jit(solution)/shard_map/ppermute | solution.py:727
  328.7 237.2 %all-gather.17.cloned.1.call-start = ((), (), s32[]{:S(2)}) async-start(), calls=%async_computation.4 | async-start | bytes 5242880 | tf_op jit(solution)/shard_map/all_gather | solution.py:926
  407.2 45.2 %collective-permute-start.20 = (bf16[512,4096]{1,0:T(8,128)(2,1)}, bf16[512,4096]{1,0:T(8,128)(2,1)}, u32[]{:S(2)}, u32[]{:S(2)}) collective-permute-start(bf16[512,4096]{1,0:T(8,128)(2,1)} %shard_map.319), channel_id=1, source_target_pairs={{0,4},{4,0},{8,12},{12,8},{16,20},{20,16},{24,28},{28,24},{1,5},{5... | collective-permute-start | bytes 12582920 | tf_op jit(solution)/shard_map/ppermute | solution.py:727
  407.3 193.1 %all-gather.21.cloned.1.call-start = ((), (), s32[]{:S(2)}) async-start(), calls=%async_computation.6 | async-start | bytes 4718592 | tf_op jit(solution)/shard_map/all_gather | solution.py:923
  407.4 57.0 %collective-permute-start.26 = (bf16[128,8192]{1,0:T(8,128)(2,1)}, bf16[128,8192]{1,0:T(8,128)(2,1)}, u32[]{:S(2)}, u32[]{:S(2)}) collective-permute-start(bf16[128,8192]{1,0:T(8,128)(2,1)} %get-tuple-element.219), channel_id=1, source_target_pairs={{0,24},{4,28},{8,16},{12,20},{16,8},{20,12},{24,0},{28,4},{1,25},{... | collective-permute-start | bytes 6291464 | tf_op jit(solution)/shard_map/ppermute | solution.py:727
  432.5 42.3 %collective-permute-start.22 = (bf16[1024,1024]{1,0:T(8,128)(2,1)S(1)}, bf16[1024,1024]{1,0:T(8,128)(2,1)S(1)}, u32[]{:S(2)}, u32[]{:S(2)}) collective-permute-start(bf16[1024,1024]{1,0:T(8,128)(2,1)S(1)} %constant_dynamic-slice_fusion.1), channel_id=1, source_target_pairs={{0,4},{4,0},{8,12},{12,8},{16,20},{20,16},{24,28},{28,24},{1,5},{5... | collective-permute-start | bytes 6291464 | tf_op jit(solution)/shard_map/ppermute | solution.py:727
  464.4 48.0 %collective-permute-start.23 = (bf16[128,4096]{1,0:T(8,128)(2,1)}, bf16[128,4096]{1,0:T(8,128)(2,1)S(1)}, u32[]{:S(2)}, u32[]{:S(2)}) collective-permute-start(bf16[128,4096]{1,0:T(8,128)(2,1)} %get-tuple-element.209), channel_id=1, source_target_pairs={{0,8},{4,12},{8,0},{12,4},{16,24},{20,28},{24,16},{28,20},{1,9},{5... | collective-permute-start | bytes 3145736 | tf_op jit(solution)/shard_map/ppermute | solution.py:727
  471.6 48.4 %collective-permute-start.24 = (bf16[128,4096]{1,0:T(8,128)(2,1)S(1)}, bf16[128,4096]{1,0:T(8,128)(2,1)S(1)}, u32[]{:S(2)}, u32[]{:S(2)}) collective-permute-start(bf16[128,4096]{1,0:T(8,128)(2,1)S(1)} %copy-done.53), channel_id=1, source_target_pairs={{0,16},{4,20},{8,24},{12,28},{16,0},{20,4},{24,8},{28,12},{1,17},{... | collective-permute-start | bytes 3145736 | tf_op jit(solution)/shard_map/ppermute | solution.py:727
  473.0 39.3 %collective-permute-start.30 = (bf16[128,2048]{1,0:T(8,128)(2,1)S(1)}, bf16[128,2048]{1,0:T(8,128)(2,1)S(1)}, u32[]{:S(2)}, u32[]{:S(2)}) collective-permute-start(bf16[128,2048]{1,0:T(8,128)(2,1)S(1)} %get-tuple-element.230), channel_id=1, source_target_pairs={{0,3},{1,0},{2,1},{3,2},{4,7},{5,4},{6,5},{7,6},{8,11},{9,8},{10,9... | collective-permute-start | bytes 1572872 | tf_op jit(solution)/shard_map/ppermute | solution.py:915
  474.3 46.7 %collective-permute-start.25 = (bf16[128,4096]{1,0:T(8,128)(2,1)S(1)}, bf16[128,4096]{1,0:T(8,128)(2,1)S(1)}, u32[]{:S(2)}, u32[]{:S(2)}) collective-permute-start(bf16[128,4096]{1,0:T(8,128)(2,1)S(1)} %copy-done.52), channel_id=1, source_target_pairs={{0,24},{4,28},{8,16},{12,20},{16,8},{20,12},{24,0},{28,4},{1,25},{... | collective-permute-start | bytes 3145736 | tf_op jit(solution)/shard_map/ppermute | solution.py:727
  474.7 81.7 %collective-permute-start.27 = (bf16[128,4096]{1,0:T(8,128)(2,1)}, bf16[128,4096]{1,0:T(8,128)(2,1)}, u32[]{:S(2)}, u32[]{:S(2)}) collective-permute-start(bf16[128,4096]{1,0:T(8,128)(2,1)} %get-tuple-element.226), channel_id=1, source_target_pairs={{0,8},{4,12},{8,0},{12,4},{16,24},{20,28},{24,16},{28,20},{1,9},{5... | collective-permute-start | bytes 3145736 | tf_op jit(solution)/shard_map/ppermute | solution.py:727
  512.3 52.3 %collective-permute-start.28 = (bf16[128,4096]{1,0:T(8,128)(2,1)}, bf16[128,4096]{1,0:T(8,128)(2,1)}, u32[]{:S(2)}, u32[]{:S(2)}) collective-permute-start(bf16[128,4096]{1,0:T(8,128)(2,1)} %get-tuple-element.227), channel_id=1, source_target_pairs={{0,16},{4,20},{8,24},{12,28},{16,0},{20,4},{24,8},{28,12},{1,17},{... | collective-permute-start | bytes 3145736 | tf_op jit(solution)/shard_map/ppermute | solution.py:727
  512.4 52.3 %collective-permute-start.29 = (bf16[128,4096]{1,0:T(8,128)(2,1)}, bf16[128,4096]{1,0:T(8,128)(2,1)}, u32[]{:S(2)}, u32[]{:S(2)}) collective-permute-start(bf16[128,4096]{1,0:T(8,128)(2,1)} %get-tuple-element.228), channel_id=1, source_target_pairs={{0,24},{4,28},{8,16},{12,20},{16,8},{20,12},{24,0},{28,4},{1,25},{... | collective-permute-start | bytes 3145736 | tf_op jit(solution)/shard_map/ppermute | solution.py:727
  565.8 90.1 %all-gather.23.cloned.1.call-start = ((), (), s32[]{:S(2)}) async-start(), calls=%async_computation.7 | async-start | bytes 4718592 | tf_op jit(solution)/shard_map/all_gather | solution.py:923
  572.0 39.2 %collective-permute-start.37 = (bf16[128,1024]{1,0:T(8,128)(2,1)}, bf16[128,1024]{1,0:T(8,128)(2,1)S(1)}, u32[]{:S(2)}, u32[]{:S(2)}) collective-permute-start(bf16[128,1024]{1,0:T(8,128)(2,1)} %get-tuple-element.275), channel_id=1, source_target_pairs={{0,2},{1,3},{2,0},{3,1},{4,6},{5,7},{6,4},{7,5},{8,10},{9,11},{10,... | collective-permute-start | bytes 786440 | tf_op jit(solution)/shard_map/ppermute | solution.py:915
  572.0 39.2 %collective-permute-start.38 = (bf16[128,1024]{1,0:T(8,128)(2,1)}, bf16[128,1024]{1,0:T(8,128)(2,1)S(1)}, u32[]{:S(2)}, u32[]{:S(2)}) collective-permute-start(bf16[128,1024]{1,0:T(8,128)(2,1)} %get-tuple-element.274), channel_id=1, source_target_pairs={{0,1},{1,2},{2,3},{3,0},{4,5},{5,6},{6,7},{7,4},{8,9},{9,10},{10,1... | collective-permute-start | bytes 786440 | tf_op jit(solution)/shard_map/ppermute | solution.py:915
  581.5 36.7 %collective-permute-start.34 = (bf16[128,1024]{1,0:T(8,128)(2,1)}, bf16[128,1024]{1,0:T(8,128)(2,1)S(1)}, u32[]{:S(2)}, u32[]{:S(2)}) collective-permute-start(bf16[128,1024]{1,0:T(8,128)(2,1)} %get-tuple-element.279), channel_id=1, source_target_pairs={{0,2},{1,3},{2,0},{3,1},{4,6},{5,7},{6,4},{7,5},{8,10},{9,11},{10,... | collective-permute-start | bytes 786440 | tf_op jit(solution)/shard_map/ppermute | solution.py:915
  (84 other events, 804.5 us)
Sparse Core Ops, SparseCore 0:
  51.5 37.1 all-gather.8
  91.1 45.5 all-gather.10
  139.2 78.7 all-gather.12
  269.1 80.7 all-gather.14
  351.4 79.2 all-gather.18
  432.7 91.4 all-gather.16
  565.9 34.4 all-gather.20
  619.5 36.2 all-gather.22

commit v3 on v2

--- a/solution.py
+++ b/solution.py
@@ -720,6 +720,7 @@
 
 def build(dp_size, mp_size):
     ring = [(i, (i + 1) % mp_size) for i in range(mp_size)]
+    back_ring = [(i, (i - 1) % mp_size) for i in range(mp_size)]
     dp_bits = dp_size.bit_length() - 1
     plane = dp_size // 2
 
@@ -763,9 +764,6 @@
         hid = ffn_up.shape[1]
         swap = flip("dp", dp_size, 1)
 
-        def across(mine, theirs):
-            return jnp.where(held, mine, swap(theirs))
-
         def take_row(values):
             return lax.dynamic_index_in_dim(values, row, 0, keepdims=False)
 
@@ -814,6 +812,15 @@
             far = (mp_size - 1) * wide
             return jnp.concatenate([own.astype(f32)[None], biases[:, t * far : (t + 1) * far]], axis=1)
 
+        def row_of(mine, theirs, cut=lambda values: values):
+            return jnp.where(held, cut(take_row(mine)), cut(take_row(theirs)))[None]
+
+        lengths = jnp.stack([target_lengths, source_lengths])
+        lengths = jnp.where(held, lengths, swap(lengths))
+        lengths = lax.dynamic_index_in_dim(lengths, row, 1, keepdims=False)
+        info = jnp.stack(
+            [0 * part, part, 2 * group - 1 - part, lengths[0], lengths[1], d // 2, core]
+        ).astype(jnp.int32)
         found_a = [
             pass_on(
                 side_by_side(
@@ -825,38 +832,32 @@
                 )
             )
         ]
-        lengths = jnp.stack([target_lengths[row], source_lengths[row]])
-        lengths = across(lengths, lengths)
-        tokens_row = take_row(tokens)
-        tokens_row = across(tokens_row, tokens_row)[None]
-        info = jnp.stack(
-            [0 * part, part, 2 * group - 1 - part, lengths[0], lengths[1], d // 2, core]
-        ).astype(jnp.int32)
-        found_a[0], tokens_row, info = wall(found_a[0], tokens_row, info)
-        for _ in range(mp_size - 2):
+        for _ in range(mp_size - 3):
             found_a.append(pass_on(found_a[-1]))
+        found_a[-1], tokens_got, info = wall(found_a[-1], swap(tokens), info)
+        found_a.append(pass_on(found_a[-1]))
+        tokens_row = row_of(tokens, tokens_got)
+        share_b = side_by_side(
+            [
+                (cols_of(self_out), None),
+                (rows_of(cross_query), cross_bias[0]),
+                (rows_of(cross_kv[0]), None),
+                (rows_of(cross_kv[1]), cross_bias[1]),
+            ]
+        )
+        share_c = side_by_side(
+            [(rows_of(ffn_up), ffn_up_bias), (cols_of(ffn_down), None), (cols_of(cross_out), None)]
+        )
+        found_a[-1], tokens_row, share_b, share_c = wall(found_a[-1], tokens_row, share_b, share_c)
+        found_b = [pass_on(share_b)]
         h1_row = entry_norm(info, tokens_row, norm_gain, norm_bias)
-        memory_row = take_row(memory)
-        memory_row = across(memory_row, memory_row)[None]
-        cot_row = take_row(cotangent)
-        cot_own = across(blocks_of(cot_row, part), blocks_of(cot_row, jnp.bitwise_xor(part, 1)))[None]
-        found_a[-1], h1_row, memory_row, cot_own = wall(found_a[-1], h1_row, memory_row, cot_own)
-        found_b = [
-            after(
-                side_by_side(
-                    [
-                        (cols_of(self_out), None),
-                        (rows_of(cross_query), cross_bias[0]),
-                        (rows_of(cross_kv[0]), None),
-                        (rows_of(cross_kv[1]), cross_bias[1]),
-                    ]
-                ),
-                found_a[-1],
-            )
-        ]
-        for _ in range(mp_size - 1):
+        found_b[0], h1_row = wall(found_b[0], h1_row)
+        for _ in range(mp_size - 3):
             found_b.append(pass_on(found_b[-1]))
-        found_b = found_b[1:]
+        found_b[-1], memory_got = wall(found_b[-1], swap(memory))
+        found_b.append(pass_on(found_b[-1]))
+        memory_row = row_of(memory, memory_got)
+        found_b[-1], memory_row = wall(found_b[-1], memory_row)
         rest_a, bias_a = gather_rest(found_a, [per] * 3)
         rest_b, bias_b = gather_rest(found_b, [per] * 4)
         w_q1, w_k1, w_v1 = [(self_in, t, rest_a, t) for t in range(3)]
@@ -864,25 +865,20 @@
         w_q2 = (cross_query[None], 0, rest_b, 1)
         w_k2, w_v2 = (cross_kv, 0, rest_b, 2), (cross_kv, 1, rest_b, 3)
 
-        last_share = after(
-            side_by_side(
-                [(rows_of(ffn_up), ffn_up_bias), (cols_of(ffn_down), None), (cols_of(cross_out), None)]
-            ),
-            found_b[-1],
-        )
-        found_c = [pass_on(last_share)]
+        found_c = [pass_on(after(share_c, found_b[-1]))]
+        for _ in range(mp_size - 3):
+            found_c.append(pass_on(found_c[-1]))
         far = min(256, length)
         h1_flat = h1_row[None]
         k1 = project(info, h1_flat, flat_place, (length // far, far), w_k1, None, mp_size)
+        found_c[-1], k1, h1_flat = wall(found_c[-1], k1, h1_flat)
+        found_c.append(pass_on(found_c[-1]))
         v1 = project(
             info, h1_flat, flat_place, (length // far, far), w_v1, bias_of(self_in_bias[1], bias_a, 2, per), mp_size
         )
-        found_c[0], k1, v1 = wall(found_c[0], k1, v1)
-        for _ in range(mp_size - 3):
-            found_c.append(pass_on(found_c[-1]))
         q1 = project(info, h1_flat, own_h_place, (2, block), w_q1, bias_of(self_in_bias[0], bias_a, 0, per), mp_size)
-        found_c[-1], q1 = wall(found_c[-1], q1)
-        found_c.append(pass_on(found_c[-1]))
+        cot_own = row_of(cotangent, swap(cotangent), lambda values: blocks_of(values, part))
+        found_c[-1], v1, q1 = wall(found_c[-1], v1, q1)
         rest_c, bias_c = gather_rest(found_c, [hid, hid, per])
         w_up, w_down = (ffn_up[None], 0, rest_c, 0), (ffn_down[None], 0, rest_c, 1)
         w_o2 = (cross_out[None], 0, rest_c, 2 * hid // per)
@@ -902,10 +898,10 @@
         def to_plane(piece, r):
             return flip("dp", dp_size, 2 * r)(piece)
 
-        def slots_of(total):
-            wide = total[0].shape[1] // mp_size
+        def slots_of(total, count=mp_size):
+            wide = total[0].shape[1] // count
             slots = []
-            for k in range(mp_size):
+            for k in range(count):
                 cols = slice(k * wide, (k + 1) * wide)
                 slots.append(low(sum(t[:, cols].astype(f32) for t in total)))
             return slots
@@ -991,9 +987,6 @@
         g1, e1, sums_two = back_norm(
             info, dq2, w_q2, [], first[None], flat_place, g2, norm_gain, 1, mp_size, True
         )
-        do1 = project(info, e1[None], flat_place, (2, block), w_o1, None, mp_size, flipped=True)
-        dq1, dk1, dv1, sum_q1, sum_v1 = attend_backward(info, q1, k1, v1, o1, do1, lse1, True)
-        kv_part = back(info, [(dk1, w_k1), (dv1, w_v1)], mp_size)
         cross_tensors = [
             (all_rows(h2[None]), dq2),
             (all_rows(memory_row), dk2),
@@ -1001,14 +994,21 @@
             (all_rows(e2[None]), o2),
         ]
         cross_sent = core_send(cross_tensors)
-        kv_part, cross_sent, last_kept, *ffn_total = wall(kv_part, cross_sent, ffn_kept[late], *ffn_total)
+        cross_got = to_core(cross_sent)
+        e1 = after(e1, cross_sent)
+        do1 = project(info, e1[None], flat_place, (2, block), w_o1, None, mp_size, flipped=True)
+        dq1, dk1, dv1, sum_q1, sum_v1 = attend_backward(info, q1, k1, v1, o1, do1, lse1, True)
+        kv_part = back(info, [(dk1, w_k1), (dv1, w_v1)], mp_size)
+        wide = ffn_kept[late].shape[1] // 2
+        last_one, last_two = ffn_kept[late][:, :wide], ffn_kept[late][:, wide:]
+        kv_part, cross_got, last_one, last_two, *ffn_total = wall(kv_part, cross_got, last_one, last_two, *ffn_total)
 
         def causal_piece(p):
             return blocks_of(kv_part, p)
 
-        ffn_total = ffn_total + [to_plane(last_kept, late)]
+        last_two = to_plane(last_two, late)
         got, here = row_sum(causal_piece)
-        cross_got = to_core(cross_sent)
+        cross_kept = core_keep(cross_tensors, cross_got)
         self_tensors = [
             (own_blocks(h1_flat, False), dq1),
             (all_rows(h1_flat), dk1),
@@ -1017,38 +1017,16 @@
         ]
         self_sent = core_send(self_tensors)
         output_got = for_other(output_found)
-        got, cross_got, self_sent, output_got = wall(got, cross_got, self_sent, output_got)
+        got, self_sent, output_got, last_one, last_two, *cross_kept = wall(
+            got, self_sent, output_got, last_one, last_two, *cross_kept
+        )
+        last_one = to_plane(last_one, late)
+        cross_total = all_planes(cross_kept)
+        self_got = to_core(self_sent)
         tokens_own, sums_one = back_norm(
             info, dq1, w_q1, [got, here], tokens_row, own_place, g1, norm_gain, 0, mp_size, False
         )
         tokens_found = gather_rows(tokens_own)
-        tokens_own, self_sent, cross_got = wall(tokens_own, self_sent, cross_got)
-        self_got = to_core(self_sent)
-        cross_kept = core_keep(cross_tensors, cross_got)
-        output = order_rows(info, output_found, output_got, rows, group, 2, bf16).reshape(tokens.shape)
-        self_got, output, *kept = wall(self_got, output, *cross_kept)
-        cross_total = all_planes(kept)
-        self_kept = core_keep(self_tensors, self_got)
-        *self_kept, ffn_total[0], ffn_total[late] = wall(*self_kept, ffn_total[0], ffn_total[late])
-        ffn_slots = slots_of(ffn_total)
-        self_kept[0], *ffn_slots = wall(self_kept[0], *ffn_slots)
-        self_total = all_planes(self_kept)
-        ffn_total = [ffn_slots[0]] + to_owners(ffn_slots)
-        memory_got = for_other(memory_found)
-        memory_got, *cross_total = wall(memory_got, *cross_total)
-        cross_slots = slots_of(cross_total)
-        cross_total = [cross_slots[0]] + to_owners(cross_slots)
-        memory_grad = order_rows(info, memory_found, memory_got, rows, group, 1, f32).reshape(memory.shape)
-        memory_grad, *kept = wall(memory_grad, *self_total, *ffn_total)
-        self_slots = slots_of(kept[:plane])
-        self_total = [self_slots[0]] + to_owners(self_slots)
-        ffn_full = gather_grads(add_up(kept[plane:]))
-        up_grad, down_grad = finish(info, ffn_full, [0], hid)[0], finish(info, ffn_full, [1], hid, True)
-        tokens_got = for_other(tokens_found)
-        tokens_grad = order_rows(info, tokens_found, tokens_got, rows, group, 2, f32).reshape(tokens.shape)
-        tokens_grad, up_grad, down_grad, *kept = wall(tokens_grad, up_grad, down_grad, *cross_total, *self_total)
-        joint = jnp.concatenate([add_up(kept[:mp_size]), add_up(kept[mp_size:])], axis=1)
-        joint_full = gather_grads(joint)
 
         def by_slot(sums):
             return jnp.sum(sums, axis=0).reshape(mp_size, -1)
@@ -1064,15 +1042,54 @@
             [w[0:1] for w in whole] + [w[1:2] for w in whole] + [whole[1][2:3], whole[2][2:3], whole[2][3:4]]
         )
         small = jnp.concatenate([in_order.reshape(-1, PAIR), whole.reshape(-1, PAIR)])
-        for b in range(dp_bits):
-            small = small + flip("dp", dp_size, 1 << b)(small)
-        for b in range(mp_size.bit_length() - 1):
-            small = small + flip("mp", mp_size, 1 << b)(small)
+        small_steps = [("dp", dp_size, 1 << b) for b in range(dp_bits)]
+        small_steps += [("mp", mp_size, 1 << b) for b in range(mp_size.bit_length() - 1)]
+
+        self_got, tokens_own = wall(self_got, tokens_own)
+        self_kept = core_keep(self_tensors, self_got)
+        last_one, *self_kept = wall(last_one, *self_kept)
+        self_total = all_planes(self_kept)
+        ffn_slots = slots_of([t[:, :wide] for t in ffn_total] + [last_one], mp_size // 2)
+        ffn_slots += slots_of([t[:, wide:] for t in ffn_total] + [last_two], mp_size // 2)
+        output = order_rows(info, output_found, output_got, rows, group, 2, bf16).reshape(tokens.shape)
+        output, small, *ffn_slots = wall(output, small, *ffn_slots)
+
+        def ring_start(slots):
+            return lax.ppermute(slots[mp_size - 1], "mp", back_ring)
+
+        def ring_next(slots, k, state):
+            return lax.ppermute(add_up([slots[k], state]), "mp", back_ring)
+
+        ffn_state = ring_start(ffn_slots)
+        memory_got = for_other(memory_found)
+        memory_got, small, ffn_state, *cross_total = wall(memory_got, small, ffn_state, *cross_total)
+        for k in range(mp_size - 2, 1, -1):
+            ffn_state = ring_next(ffn_slots, k, ffn_state)
+        cross_slots = slots_of(cross_total)
+        cross_state = ring_start(cross_slots)
+        memory_grad = order_rows(info, memory_found, memory_got, rows, group, 1, f32).reshape(memory.shape)
+        memory_grad, small, ffn_state, cross_state = wall(memory_grad, small, ffn_state, cross_state)
+        ffn_state = ring_next(ffn_slots, 1, ffn_state)
+        for k in range(mp_size - 2, 1, -1):
+            cross_state = ring_next(cross_slots, k, cross_state)
+        ffn_state, small, cross_state, *self_total = wall(ffn_state, small, cross_state, *self_total)
+        ffn_full = gather_grads(add_up([ffn_slots[0], ffn_state]))
+        cross_state = ring_next(cross_slots, 1, cross_state)
+        self_slots = slots_of(self_total)
+        self_total = [self_slots[0]] + to_owners(self_slots)
+        tokens_got = for_other(tokens_found)
+        tokens_grad = order_rows(info, tokens_found, tokens_got, rows, group, 2, f32).reshape(tokens.shape)
+        tokens_grad, small, cross_state, *self_total = wall(tokens_grad, small, cross_state, *self_total)
+        for step in small_steps:
+            small = small + flip(*step)(small)
+        joint = jnp.concatenate([add_up([cross_slots[0], cross_state]), add_up(self_total)], axis=1)
+        joint_full = gather_grads(joint)
+        up_grad, down_grad = finish(info, ffn_full, [0], hid)[0], finish(info, ffn_full, [1], hid, True)
         small = small.reshape(-1)
         slot_part = small[: in_order.size].reshape(in_order.shape)
         mine = lax.dynamic_index_in_dim(slot_part, z, 0, keepdims=False)
         whole = small[in_order.size :].reshape(9, width)
-        cross_q, cross_both, cross_o, self_three, self_o = finish_pair(info, joint_full)
+        cross_q, cross_both, cross_o, self_three, self_o = finish_pair(after(info, up_grad, down_grad), joint_full)
         return (
             output,
             tokens_grad,

time: 677 us -> 648 us (0.957)
  waiting for transfers between devices: 233 us -> 189 us
  starting transfers between devices: 30.5 us -> 49.3 us
    ppermute x9 -> x3, waiting for transfers between devices: 74.1 us -> 9.23 us  [to_owners(): lax.ppermute(slots[k], 'mp', [(i, (i - k) % mp_size) for i in range(mp_si...]
    ppermute x26 -> x27, waiting for transfers between devices: 32.2 us -> 69.4 us  [flip(): lax.ppermute(value, axis, [(i, i ^ bits) for i in range(size)])]
    ppermute x0 -> x6, waiting for transfers between devices: none -> 22 us  [the longest x2 19.3 us: ring_start(): return lax.ppermute(slots[mp_size - 1], 'mp', back_ring)]
    ppermute x26 -> x27, starting transfers between devices: 16.5 us -> 29.1 us  [flip(): lax.ppermute(value, axis, [(i, i ^ bits) for i in range(size)])]
    all_gather x2, waiting for transfers between devices: 16.9 us -> 4.4 us  [gather_grads(): return lax.all_gather(total, 'dp', axis=0, tiled=True)]
    all_gather x3, waiting for transfers between devices: 21.7 us -> 10.3 us  [gather_rows(): return lax.all_gather(mine, 'mp', axis=0, tiled=True)]
    ppermute x0 -> x6, starting transfers between devices: none -> 11.4 us  [the longest x4 8.45 us: ring_next(): return lax.ppermute(add_up([slots[k], state]), 'mp', back_ring)]
    all_gather x3, waiting for transfers between devices: 17.7 us -> 7.67 us  [gather_rest(): lax.all_gather(ours, 'dp', axis=0, tiled=True)]
  transfers between devices with their start and end apart: 52 -> 53, of which waited for: 24 -> 26; matrix products, arithmetic and copies ran while one was open for 9% -> 9% of each run, Pallas kernels for 38% -> 40%
where the time goes in v3:
time: 648 us; the launch traced here: 640 us
  Pallas kernels  312 us (48%)
  waiting for transfers between devices  189 us (29%)
  starting transfers between devices  49.3 us (8%)
  local copies, waits for them, and re-layouts  48.6 us (8%)
  other arithmetic  25.7 us (4%)
  between operations  15.7 us (2%)
    pallas_call x32, Pallas kernels, call(): pl.pallas_call(kernel, out_shape=tuple((jax.ShapeDtypeStruct(s, t) for s,...  312 us
    ppermute x27, waiting for transfers between devices, flip(): lax.ppermute(value, axis, [(i, i ^ bits) for i in range(size)])  69.4 us
    ppermute x9, waiting for transfers between devices, pass_on(): return lax.ppermute(value, 'mp', ring)  66.1 us
    ppermute x27, starting transfers between devices, flip(): lax.ppermute(value, axis, [(i, i ^ bits) for i in range(size)])  29.1 us
    ppermute x2, waiting for transfers between devices, ring_start(): return lax.ppermute(slots[mp_size - 1], 'mp', back_ring)  19.3 us
    unnamed x155, local copies, waits for them, and re-layouts  16.4 us
  transfers between devices with their start and end apart: 53, of which 26 were waited for; matrix products, arithmetic and copies ran while one was open for 9% of the time, Pallas kernels for 40%

profile of v3, /device:TPU:0, one launch (start us, length us, event | category | flops | bytes accessed | tf_op | source)
XLA Modules:
  0.0 640.3 jit_solution(15570835122594955170)
XLA Ops:
  53.5 10.3 %collective-permute-done.6 = bf16[144,1024]{1,0:T(8,128)(2,1)S(1)} collective-permute-done((bf16[144,1024]{1,0:T(8,128)(2,1)S(1)}, bf16[144,1024]{1,0:T(8,128)(2,1)S(1)}, u32[]{:S(2)}, u32[]{:S(2)}) %collective-permute-start.6) | collective-permute-done | bytes 294944 | tf_op jit(solution)/shard_map/ppermute | solution.py:799
  65.4 7.9 %collective-permute-done.8 = bf16[144,1024]{1,0:T(8,128)(2,1)S(1)} collective-permute-done((bf16[144,1024]{1,0:T(8,128)(2,1)S(1)}, bf16[144,1024]{1,0:T(8,128)(2,1)S(1)}, u32[]{:S(2)}, u32[]{:S(2)}) %collective-permute-start.8) | collective-permute-done | bytes 294944 | tf_op jit(solution)/shard_map/ppermute | solution.py:799
  75.5 16.8 %collective-permute-done.9 = bf16[144,2304]{1,0:T(8,128)(2,1)} collective-permute-done((bf16[144,2304]{1,0:T(8,128)(2,1)}, bf16[144,2304]{1,0:T(8,128)(2,1)}, u32[]{:S(2)}, u32[]{:S(2)}) %collective-permute-start.9) | collective-permute-done | bytes 663584 | tf_op jit(solution)/shard_map/ppermute | solution.py:799
  99.4 8.7 %collective-permute-done.10 = bf16[144,2304]{1,0:T(8,128)(2,1)} collective-permute-done((bf16[144,2304]{1,0:T(8,128)(2,1)}, bf16[144,2304]{1,0:T(8,128)(2,1)}, u32[]{:S(2)}, u32[]{:S(2)}) %collective-permute-start.10) | collective-permute-done | bytes 663584 | tf_op jit(solution)/shard_map/ppermute | solution.py:799
  140.8 15.1 %shard_map.301 = (bf16[512,1024]{1,0:T(8,128)(2,1)S(1)}, f32[8,8,512]{2,1,0:T(8,128)S(1)}) custom-call(s32[7]{0:T(128)S(1)} %stack.38.info, bf16[512,1024]{1,0:T(8,128)(2,1)} %copy-done.11, bf16[1024,1024]{1,0:T(8,128)(2,1)} %shard_map.298.k_ref, bf16[1024,1024]{1,0:T(8,128)(2,1)} %shard_map.299.v_ref), custom_call_target="tpu_custom_call" | custom-call | flops 160000000 | bytes 1024 | tf_op jit(solution)/shard_map/pallas_call | solution.py:48
  181.9 18.0 %shard_map.306 = (bf16[512,1024]{1,0:T(8,128)(2,1)S(1)}, f32[8,8,512]{2,1,0:T(8,128)S(1)}) custom-call(s32[7]{0:T(128)S(1)} %stack.38.info, bf16[512,1024]{1,0:T(8,128)(2,1)} %copy-done.12, bf16[1024,1024]{1,0:T(8,128)(2,1)} %shard_map.304.k_ref, bf16[1024,1024]{1,0:T(8,128)(2,1)} %shard_map.305.v_ref), custom_call_target="tpu_custom_call" | custom-call | flops 160000000 | bytes 1024 | tf_op jit(solution)/shard_map/pallas_call | solution.py:48
  214.9 32.6 %shard_map.308 = (bf16[512,4096]{1,0:T(8,128)(2,1)}, bf16[512,4096]{1,0:T(8,128)(2,1)}, f32[8,4096]{1,0:T(8,128)S(1)}, bf16[512,1024]{1,0:T(8,128)(2,1)S(1)}, f3...) custom-call(s32[7]{0:T(128)S(1)} %stack.38.info, bf16[512,1024]{1,0:T(8,128)(2,1)} %copy-done.13, ...), custom_call_target="tpu_custom_call" | custom-call | flops 320000000 | bytes 1024 | tf_op jit(solution)/shard_map/pallas_call | solution.py:48
  248.5 10.8 %shard_map.309 = bf16[512,8192]{1,0:T(8,128)(2,1)} custom-call(s32[7]{0:T(128)S(1)} %stack.38.info, bf16[1,512,1024]{2,1,0:T(8,128)(2,1)S(1)} %bitcast.48, bf16[1,512,1024]{2,1,0:T(8,128)(2,1)} %maximum_select_fusion.c0_ref.c1_ref.refs_1_, bf16[512,4096]{1,0:T(8,128)(2,1)} %get-tuple-element.178.refs_2_, bf16[512,4096]{1,0:T(8,128)(2,1)} %get-tuple-element.179.refs_3_), custom_call_target="tpu_custom_call" | custom-call | flops 80000000 | bytes 1024 | tf_op jit(solution)/shard_map/pallas_call | solution.py:48
  264.4 25.7 %shard_map.311 = (bf16[512,1024]{1,0:T(8,128)(2,1)S(1)}, bf16[1024,1024]{1,0:T(8,128)(2,1)}, bf16[1024,1024]{1,0:T(8,128)(2,1)}, f32[8,1024]{1,0:T(8,128)S(1)}, f32[8,1024]{1,0:T(8,128)S(1)}) custom-call(s32[7]{0:T(128)S(1)} %stack.38.info, bf16[512,1024]{1,0:T(8,128)(2,1)} %copy-done.12, bf16[1024,1024]{1,0:T(8,128)(2,1)} %shard_map.304.k_ref, ...), custom_call_target="tpu_custom_call" | custom-call | flops 240000000 | bytes 1024 | tf_op jit(solution)/shard_map/pallas_call | solution.py:48
  290.1 8.9 %shard_map.312 = bf16[1024,1024]{1,0:T(8,128)(2,1)} custom-call(s32[7]{0:T(128)S(1)} %stack.38.info, bf16[1024,1024]{1,0:T(8,128)(2,1)} %get-tuple-element.183.refs_0_.refs_5_, bf16[2,1024,256]{2,1,0:T(8,128)(2,1)S(1)} %copy-done.2, bf16[1024,3072]{1,0:T(8,128)(2,1)} %all-gather.11.cloned.1.call-done.rest_ref.refs_2_.refs_5_, ...), custom_call_target="tpu_custom_call" | custom-call | flops 50000000 | bytes 1024 | tf_op jit(solution)/shard_map/pallas_call | solution.py:48
  301.6 12.7 %shard_map.313 = (bf16[128,8192]{1,0:T(8,128)(2,1)}, bf16[128,8192]{1,0:T(8,128)(2,1)}, bf16[128,8192]{1,0:T(8,128)(2,1)}, bf16[128,8192]{1,0:T(8,128)(2,1)}) custom-call(s32[7]{0:T(128)S(1)} %stack.38.info, bf16[1,512,1024]{2,1,0:T(8,128)(2,1)S(1)} %bitcast.49, bf16[1,512,1024]{2,1,0:T(8,128)(2,1)} %maximum_select_fusion.c0_ref.c1_ref.refs_1_, ...), custom_call_target="tpu_custom_call" | custom-call | flops 80000000 | bytes 1024 | tf_op jit(solution)/shard_map/pallas_call | solution.py:48
  317.1 10.7 %shard_map.315 = bf16[512,4096]{1,0:T(8,128)(2,1)} custom-call(s32[7]{0:T(128)S(1)} %stack.38.info, bf16[1,512,1024]{2,1,0:T(8,128)(2,1)S(1)} %bitcast.47, bf16[1,1024,1024]{2,1,0:T(8,128)(2,1)} %dynamic-slice_select_fusion.x_ref.refs_1_.refs_2_, bf16[1,1024,1024]{2,1,0:T(8,128)(2,1)} %dynamic-slice_select_fusion.x_ref.refs_1_.refs_2_, ...), custom_call_target="tpu_custom_call" | custom-call | flops 80000000 | bytes 1024 | tf_op jit(solution)/shard_map/pallas_call | solution.py:48
  330.2 10.3 %all-gather.15.cloned.1.call-done.same_ref = bf16[2048,1024]{1,0:T(8,128)(2,1)} async-done(((bf16[512,1024]{1,0:T(8,128)(2,1)}), bf16[2048,1024]{1,0:T(8,128)(2,1)}) %all-gather.15.cloned.1.call-update) | async-done | bytes 4194320 | tf_op jit(solution)/shard_map/all_gather | solution.py:922
  354.7 20.6 %shard_map.317 = (bf16[512,1024]{1,0:T(8,128)(2,1)S(1)}, bf16[1024,1024]{1,0:T(8,128)(2,1)}, bf16[1024,1024]{1,0:T(8,128)(2,1)}, f32[8,1024]{1,0:T(8,128)S(1)}, f32[8,1024]{1,0:T(8,128)S(1)}) custom-call(s32[7]{0:T(128)S(1)} %stack.38.info, bf16[512,1024]{1,0:T(8,128)(2,1)} %copy-done.11, bf16[1024,1024]{1,0:T(8,128)(2,1)} %shard_map.298.k_ref, ...), custom_call_target="tpu_custom_call" | custom-call | flops 240000000 | bytes 1024 | tf_op jit(solution)/shard_map/pallas_call | solution.py:48
  375.3 9.3 %shard_map.318 = bf16[1024,1024]{1,0:T(8,128)(2,1)} custom-call(s32[7]{0:T(128)S(1)} %stack.38.info, bf16[1024,1024]{1,0:T(8,128)(2,1)} %get-tuple-element.200.refs_0_.refs_6_, bf16[3,1024,256]{2,1,0:T(8,128)(2,1)S(1)} %copy-done.1, bf16[1024,2304]{1,0:T(8,128)(2,1)} %all-gather.9.cloned.1.call-done.rest_ref.refs_2_.refs_5_, ...), custom_call_target="tpu_custom_call" | custom-call | flops 50000000 | bytes 1024 | tf_op jit(solution)/shard_map/pallas_call | solution.py:48
  390.2 10.6 %shard_map.319 = bf16[512,4096]{1,0:T(8,128)(2,1)} custom-call(s32[7]{0:T(128)S(1)} %stack.38.info, bf16[1,1024,1024]{2,1,0:T(8,128)(2,1)} %bitcast.59, bf16[1,1024,1024]{2,1,0:T(8,128)(2,1)} %bitcast.60, bf16[1,1024,1024]{2,1,0:T(8,128)(2,1)} %bitcast.61, bf16[1,1024,1024]{2,1,0:T(8,128)(2,1)} %bitcast.62, bf16[1,512,1024]{2,1,0:T(8,128)(2,1)S(1)} %bitcast.44, ...), custom_call_target="tpu_custom_call" | custom-call | flops 80000000 | bytes 1024 | tf_op jit(solution)/shard_map/pallas_call | solution.py:48
  400.8 11.9 %shard_map.320 = (bf16[128,4096]{1,0:T(8,128)(2,1)S(1)}, bf16[128,4096]{1,0:T(8,128)(2,1)}, bf16[128,4096]{1,0:T(8,128)(2,1)}, bf16[128,4096]{1,0:T(8,128)(2,1)}) custom-call(s32[7]{0:T(128)S(1)} %stack.38.info, bf16[1,512,1024]{2,1,0:T(8,128)(2,1)} %bitcast.46, bf16[1,1024,1024]{2,1,0:T(8,128)(2,1)} %dynamic-slice_select_fusion.x_ref.refs_1_.refs_2_, ...), custom_call_target="tpu_custom_call" | custom-call | flops 80000000 | bytes 1024 | tf_op jit(solution)/shard_map/pallas_call | solution.py:48
  440.9 12.0 %shard_map.323 = (bf16[128,4096]{1,0:T(8,128)(2,1)S(1)}, bf16[128,4096]{1,0:T(8,128)(2,1)}, bf16[128,4096]{1,0:T(8,128)(2,1)}, bf16[128,4096]{1,0:T(8,128)(2,1)}) custom-call(s32[7]{0:T(128)S(1)} %stack.38.info, bf16[1,1024,1024]{2,1,0:T(8,128)(2,1)} %bitcast.63, bf16[1,1024,1024]{2,1,0:T(8,128)(2,1)} %bitcast.64, bf16[1,1024,1024]{2,1,0:T(8,128)(2,1)} %bitcast.65, ...), custom_call_target="tpu_custom_call" | custom-call | flops 80000000 | bytes 1024 | tf_op jit(solution)/shard_map/pallas_call | solution.py:48
  458.1 15.0 %collective-permute-done.26 = bf16[128,4096]{1,0:T(8,128)(2,1)S(1)} collective-permute-done((bf16[128,4096]{1,0:T(8,128)(2,1)}, bf16[128,4096]{1,0:T(8,128)(2,1)S(1)}, u32[]{:S(2)}, u32[]{:S(2)}) %collective-permute-start.26) | collective-permute-done | bytes 1048608 | tf_op jit(solution)/shard_map/ppermute | solution.py:728
  473.0 22.0 %collective-permute-done.28 = bf16[128,4096]{1,0:T(8,128)(2,1)S(1)} collective-permute-done((bf16[128,4096]{1,0:T(8,128)(2,1)}, bf16[128,4096]{1,0:T(8,128)(2,1)S(1)}, u32[]{:S(2)}, u32[]{:S(2)}) %collective-permute-start.28) | collective-permute-done | bytes 1048608 | tf_op jit(solution)/shard_map/ppermute | solution.py:728
  509.0 19.3 %collective-permute-done.30 = bf16[128,1024]{1,0:T(8,128)(2,1)S(1)} collective-permute-done((bf16[128,1024]{1,0:T(8,128)(2,1)S(1)}, bf16[128,1024]{1,0:T(8,128)(2,1)S(1)}, u32[]{:S(2)}, u32[]{:S(2)}) %collective-permute-start.30) | collective-permute-done | bytes 262176 | tf_op jit(solution)/shard_map/ppermute | solution.py:1058
  533.0 11.9 %collective-permute-done.34 = bf16[128,4096]{1,0:T(8,128)(2,1)} collective-permute-done((bf16[128,4096]{1,0:T(8,128)(2,1)S(1)}, bf16[128,4096]{1,0:T(8,128)(2,1)}, u32[]{:S(2)}, u32[]{:S(2)}) %collective-permute-start.34) | collective-permute-done | bytes 1048608 | tf_op jit(solution)/shard_map/ppermute | solution.py:728
  562.8 9.3 %shard_map.324 = f32[2048,1024]{1,0:T(8,128)} custom-call(s32[7]{0:T(128)S(1)} %stack.38.info, bf16[2048,1024]{1,0:T(8,128)(2,1)} %all-gather.17.cloned.1.call-done.same_ref, bf16[1024,1024]{1,0:T(8,128)(2,1)} %copy-done.39), custom_call_target="tpu_custom_call" | custom-call | flops 40000000 | bytes 1024 | tf_op jit(solution)/shard_map/pallas_call | solution.py:48
  572.1 9.2 %collective-permute-done.38 = bf16[128,1024]{1,0:T(8,128)(2,1)S(1)} collective-permute-done((bf16[128,1024]{1,0:T(8,128)(2,1)S(1)}, bf16[128,1024]{1,0:T(8,128)(2,1)S(1)}, u32[]{:S(2)}, u32[]{:S(2)}) %collective-permute-start.38) | collective-permute-done | bytes 262176 | tf_op jit(solution)/shard_map/ppermute | solution.py:911
  (380 shorter events, 285.3 us)
Async XLA Ops:
  7.2 85.8 %all-gather.9.cloned.1.call-start = ((), (), s32[]{:S(2)}) async-start(), calls=%async_computation | async-start | bytes 5308416 | tf_op jit(solution)/shard_map/all_gather | solution.py:809
  42.1 115.4 %all-gather.11.cloned.1.call-start = ((), (), s32[]{:S(2)}) async-start(), calls=%async_computation.1 | async-start | bytes 7077888 | tf_op jit(solution)/shard_map/all_gather | solution.py:809
  75.4 133.2 %all-gather.13.cloned.1.call-start = ((), (), s32[]{:S(2)}) async-start(), calls=%async_computation.2 | async-start | bytes 15925248 | tf_op jit(solution)/shard_map/all_gather | solution.py:809
  128.8 211.6 %all-gather.15.cloned.1.call-start = ((), (), s32[]{:S(2)}) async-start(), calls=%async_computation.3 | async-start | bytes 5242880 | tf_op jit(solution)/shard_map/all_gather | solution.py:922
  259.3 39.8 %collective-permute-start.13 = (bf16[512,8192]{1,0:T(8,128)(2,1)}, bf16[512,8192]{1,0:T(8,128)(2,1)}, u32[]{:S(2)}, u32[]{:S(2)}) collective-permute-start(bf16[512,8192]{1,0:T(8,128)(2,1)} %shard_map.309), channel_id=1, source_target_pairs={{0,4},{4,0},{8,12},{12,8},{16,20},{20,16},{24,28},{28,24},{1,5},{5... | collective-permute-start | bytes 25165832 | tf_op jit(solution)/shard_map/ppermute | solution.py:728
  259.6 166.3 %all-gather.19.cloned.1.call-start = ((), (), s32[]{:S(2)}) async-start(), calls=%async_computation.5 | async-start | bytes 5242880 | tf_op jit(solution)/shard_map/all_gather | solution.py:922
  327.8 58.3 %collective-permute-start.15 = (bf16[512,4096]{1,0:T(8,128)(2,1)}, bf16[512,4096]{1,0:T(8,128)(2,1)}, u32[]{:S(2)}, u32[]{:S(2)}) collective-permute-start(bf16[512,4096]{1,0:T(8,128)(2,1)} %shard_map.315), channel_id=1, source_target_pairs={{0,4},{4,0},{8,12},{12,8},{16,20},{20,16},{24,28},{28,24},{1,5},{5... | collective-permute-start | bytes 12582920 | tf_op jit(solution)/shard_map/ppermute | solution.py:728
  328.1 221.6 %all-gather.17.cloned.1.call-start = ((), (), s32[]{:S(2)}) async-start(), calls=%async_computation.4 | async-start | bytes 5242880 | tf_op jit(solution)/shard_map/all_gather | solution.py:922
  328.1 58.0 %collective-permute-start.16 = (bf16[128,8192]{1,0:T(8,128)(2,1)}, bf16[128,8192]{1,0:T(8,128)(2,1)}, u32[]{:S(2)}, u32[]{:S(2)}) collective-permute-start(bf16[128,8192]{1,0:T(8,128)(2,1)} %get-tuple-element.204), channel_id=1, source_target_pairs={{0,8},{4,12},{8,0},{12,4},{16,24},{20,28},{24,16},{28,20},{1,9},{5... | collective-permute-start | bytes 6291464 | tf_op jit(solution)/shard_map/ppermute | solution.py:728
  329.6 56.5 %collective-permute-start.17 = (bf16[128,8192]{1,0:T(8,128)(2,1)}, bf16[128,8192]{1,0:T(8,128)(2,1)}, u32[]{:S(2)}, u32[]{:S(2)}) collective-permute-start(bf16[128,8192]{1,0:T(8,128)(2,1)} %get-tuple-element.205), channel_id=1, source_target_pairs={{0,16},{4,20},{8,24},{12,28},{16,0},{20,4},{24,8},{28,12},{1,17},{... | collective-permute-start | bytes 6291464 | tf_op jit(solution)/shard_map/ppermute | solution.py:728
  342.2 70.5 %collective-permute-start.19 = (bf16[1024,1024]{1,0:T(8,128)(2,1)S(1)}, bf16[1024,1024]{1,0:T(8,128)(2,1)}, u32[]{:S(2)}, u32[]{:S(2)}) collective-permute-start(bf16[1024,1024]{1,0:T(8,128)(2,1)S(1)} %constant_dynamic-slice_fusion.5), channel_id=1, source_target_pairs={{0,4},{4,0},{8,12},{12,8},{16,20},{20,16},{24,28},{28,24},{1,5},{5... | collective-permute-start | bytes 6291464 | tf_op jit(solution)/shard_map/ppermute | solution.py:728
  422.3 189.2 %all-gather.21.cloned.1.call-start = ((), (), s32[]{:S(2)}) async-start(), calls=%async_computation.6 | async-start | bytes 4718592 | tf_op jit(solution)/shard_map/all_gather | solution.py:919
  423.3 29.5 %collective-permute-start.21 = (bf16[128,4096]{1,0:T(8,128)(2,1)}, bf16[128,4096]{1,0:T(8,128)(2,1)S(1)}, u32[]{:S(2)}, u32[]{:S(2)}) collective-permute-start(bf16[128,4096]{1,0:T(8,128)(2,1)} %get-tuple-element.229), channel_id=1, source_target_pairs={{0,24},{4,28},{8,16},{12,20},{16,8},{20,12},{24,0},{28,4},{1,25},{... | collective-permute-start | bytes 3145736 | tf_op jit(solution)/shard_map/ppermute | solution.py:728
  428.9 66.1 %collective-permute-start.24 = (bf16[1024,1024]{1,0:T(8,128)(2,1)}, bf16[1024,1024]{1,0:T(8,128)(2,1)}, u32[]{:S(2)}, u32[]{:S(2)}) collective-permute-start(bf16[1024,1024]{1,0:T(8,128)(2,1)} %constant_dynamic-slice_fusion.1), channel_id=1, source_target_pairs={{0,4},{4,0},{8,12},{12,8},{16,20},{20,16},{24,28},{28,24},{1,5},{5... | collective-permute-start | bytes 6291464 | tf_op jit(solution)/shard_map/ppermute | solution.py:728
  429.5 43.6 %collective-permute-start.26 = (bf16[128,4096]{1,0:T(8,128)(2,1)}, bf16[128,4096]{1,0:T(8,128)(2,1)S(1)}, u32[]{:S(2)}, u32[]{:S(2)}) collective-permute-start(bf16[128,4096]{1,0:T(8,128)(2,1)} %get-tuple-element.244), channel_id=1, source_target_pairs={{0,8},{4,12},{8,0},{12,4},{16,24},{20,28},{24,16},{28,20},{1,9},{5... | collective-permute-start | bytes 3145736 | tf_op jit(solution)/shard_map/ppermute | solution.py:728
  430.1 43.0 %collective-permute-start.27 = (bf16[128,4096]{1,0:T(8,128)(2,1)}, bf16[128,4096]{1,0:T(8,128)(2,1)S(1)}, u32[]{:S(2)}, u32[]{:S(2)}) collective-permute-start(bf16[128,4096]{1,0:T(8,128)(2,1)} %get-tuple-element.245), channel_id=1, source_target_pairs={{0,16},{4,20},{8,24},{12,28},{16,0},{20,4},{24,8},{28,12},{1,17},{... | collective-permute-start | bytes 3145736 | tf_op jit(solution)/shard_map/ppermute | solution.py:728
  438.4 56.6 %collective-permute-start.28 = (bf16[128,4096]{1,0:T(8,128)(2,1)}, bf16[128,4096]{1,0:T(8,128)(2,1)S(1)}, u32[]{:S(2)}, u32[]{:S(2)}) collective-permute-start(bf16[128,4096]{1,0:T(8,128)(2,1)} %get-tuple-element.246), channel_id=1, source_target_pairs={{0,24},{4,28},{8,16},{12,20},{16,8},{20,12},{24,0},{28,4},{1,25},{... | collective-permute-start | bytes 3145736 | tf_op jit(solution)/shard_map/ppermute | solution.py:728
  457.0 38.0 %collective-permute-start.25 = (bf16[128,2048]{1,0:T(8,128)(2,1)S(1)}, bf16[128,2048]{1,0:T(8,128)(2,1)S(1)}, u32[]{:S(2)}, u32[]{:S(2)}) collective-permute-start(bf16[128,2048]{1,0:T(8,128)(2,1)S(1)} %get-tuple-element.242), channel_id=1, source_target_pairs={{0,3},{1,0},{2,1},{3,2},{4,7},{5,4},{6,5},{7,6},{8,11},{9,8},{10,9... | collective-permute-start | bytes 1572872 | tf_op jit(solution)/shard_map/ppermute | solution.py:1058
  495.2 33.1 %collective-permute-start.29 = (bf16[128,2048]{1,0:T(8,128)(2,1)S(1)}, bf16[128,2048]{1,0:T(8,128)(2,1)S(1)}, u32[]{:S(2)}, u32[]{:S(2)}) collective-permute-start(bf16[128,2048]{1,0:T(8,128)(2,1)S(1)} %add_convert_fusion.3), channel_id=1, source_target_pairs={{0,3},{1,0},{2,1},{3,2},{4,7},{5,4},{6,5},{7,6},{8,11},{9,8},{10,9... | collective-permute-start | bytes 1572872 | tf_op jit(solution)/shard_map/ppermute | solution.py:1061
  496.2 32.1 %collective-permute-start.30 = (bf16[128,1024]{1,0:T(8,128)(2,1)S(1)}, bf16[128,1024]{1,0:T(8,128)(2,1)S(1)}, u32[]{:S(2)}, u32[]{:S(2)}) collective-permute-start(bf16[128,1024]{1,0:T(8,128)(2,1)S(1)} %add_convert_fusion.19), channel_id=1, source_target_pairs={{0,3},{1,0},{2,1},{3,2},{4,7},{5,4},{6,5},{7,6},{8,11},{9,8},{10,9... | collective-permute-start | bytes 786440 | tf_op jit(solution)/shard_map/ppermute | solution.py:1058
  498.0 34.9 %collective-permute-start.33 = (bf16[128,4096]{1,0:T(8,128)(2,1)}, bf16[128,4096]{1,0:T(8,128)(2,1)S(1)}, u32[]{:S(2)}, u32[]{:S(2)}) collective-permute-start(bf16[128,4096]{1,0:T(8,128)(2,1)} %get-tuple-element.259), channel_id=1, source_target_pairs={{0,8},{4,12},{8,0},{12,4},{16,24},{20,28},{24,16},{28,20},{1,9},{5... | collective-permute-start | bytes 3145736 | tf_op jit(solution)/shard_map/ppermute | solution.py:728
  499.5 45.4 %collective-permute-start.34 = (bf16[128,4096]{1,0:T(8,128)(2,1)S(1)}, bf16[128,4096]{1,0:T(8,128)(2,1)}, u32[]{:S(2)}, u32[]{:S(2)}) collective-permute-start(bf16[128,4096]{1,0:T(8,128)(2,1)S(1)} %copy-done.61), channel_id=1, source_target_pairs={{0,16},{4,20},{8,24},{12,28},{16,0},{20,4},{24,8},{28,12},{1,17},{... | collective-permute-start | bytes 3145736 | tf_op jit(solution)/shard_map/ppermute | solution.py:728
  501.0 44.9 %collective-permute-start.35 = (bf16[128,4096]{1,0:T(8,128)(2,1)S(1)}, bf16[128,4096]{1,0:T(8,128)(2,1)}, u32[]{:S(2)}, u32[]{:S(2)}) collective-permute-start(bf16[128,4096]{1,0:T(8,128)(2,1)S(1)} %copy-done.60), channel_id=1, source_target_pairs={{0,24},{4,28},{8,16},{12,20},{16,8},{20,12},{24,0},{28,4},{1,25},{... | collective-permute-start | bytes 3145736 | tf_op jit(solution)/shard_map/ppermute | solution.py:728
  549.6 77.1 %all-gather.23.cloned.1.call-start = ((), (), s32[]{:S(2)}) async-start(), calls=%async_computation.7 | async-start | bytes 4718592 | tf_op jit(solution)/shard_map/all_gather | solution.py:919
  (91 other events, 1078.7 us)
Sparse Core Ops, SparseCore 0:
  42.2 36.9 all-gather.8
  81.7 45.5 all-gather.10
  129.7 78.7 all-gather.12
  259.7 80.7 all-gather.14
  341.9 79.2 all-gather.18
  423.2 99.7 all-gather.16
  549.7 37.7 all-gather.20
  590.0 36.7 all-gather.22

commit v4 on v3

--- a/solution.py
+++ b/solution.py
@@ -836,20 +836,21 @@
             found_a.append(pass_on(found_a[-1]))
         found_a[-1], tokens_got, info = wall(found_a[-1], swap(tokens), info)
         found_a.append(pass_on(found_a[-1]))
-        tokens_row = row_of(tokens, tokens_got)
         share_b = side_by_side(
             [
                 (cols_of(self_out), None),
                 (rows_of(cross_query), cross_bias[0]),
                 (rows_of(cross_kv[0]), None),
                 (rows_of(cross_kv[1]), cross_bias[1]),
+                (cols_of(cross_out), None),
             ]
         )
         share_c = side_by_side(
-            [(rows_of(ffn_up), ffn_up_bias), (cols_of(ffn_down), None), (cols_of(cross_out), None)]
+            [(rows_of(ffn_up), ffn_up_bias), (cols_of(ffn_down), None)]
         )
-        found_a[-1], tokens_row, share_b, share_c = wall(found_a[-1], tokens_row, share_b, share_c)
+        found_a[-1], tokens_got, share_b, share_c = wall(found_a[-1], tokens_got, share_b, share_c)
         found_b = [pass_on(share_b)]
+        tokens_row = row_of(tokens, tokens_got)
         h1_row = entry_norm(info, tokens_row, norm_gain, norm_bias)
         found_b[0], h1_row = wall(found_b[0], h1_row)
         for _ in range(mp_size - 3):
@@ -859,11 +860,12 @@
         memory_row = row_of(memory, memory_got)
         found_b[-1], memory_row = wall(found_b[-1], memory_row)
         rest_a, bias_a = gather_rest(found_a, [per] * 3)
-        rest_b, bias_b = gather_rest(found_b, [per] * 4)
+        rest_b, bias_b = gather_rest(found_b, [per] * 5)
         w_q1, w_k1, w_v1 = [(self_in, t, rest_a, t) for t in range(3)]
         w_o1 = (self_out[None], 0, rest_b, 0)
         w_q2 = (cross_query[None], 0, rest_b, 1)
         w_k2, w_v2 = (cross_kv, 0, rest_b, 2), (cross_kv, 1, rest_b, 3)
+        w_o2 = (cross_out[None], 0, rest_b, 4)
 
         found_c = [pass_on(after(share_c, found_b[-1]))]
         for _ in range(mp_size - 3):
@@ -879,9 +881,8 @@
         q1 = project(info, h1_flat, own_h_place, (2, block), w_q1, bias_of(self_in_bias[0], bias_a, 0, per), mp_size)
         cot_own = row_of(cotangent, swap(cotangent), lambda values: blocks_of(values, part))
         found_c[-1], v1, q1 = wall(found_c[-1], v1, q1)
-        rest_c, bias_c = gather_rest(found_c, [hid, hid, per])
+        rest_c, bias_c = gather_rest(found_c, [hid, hid])
         w_up, w_down = (ffn_up[None], 0, rest_c, 0), (ffn_down[None], 0, rest_c, 1)
-        w_o2 = (cross_out[None], 0, rest_c, 2 * hid // per)
         o1, lse1 = attend_forward(info, q1, k1, v1, True)
         first, h2 = mix(info, o1, w_o1, tokens_row, own_place, out_bias, norm_gain, norm_bias, 0, mp_size)
         q2 = project(info, h2[None], flat_place, (2, block), w_q2, bias_of(cross_bias[0], bias_b, 1, per), mp_size)

time: 648 us -> 643 us (level)
    unnamed x155 -> x159, local copies, waits for them, and re-layouts: 16.4 us -> 17.9 us
  transfers between devices with their start and end apart: 53 -> 53, of which waited for: 26 -> 26; matrix products, arithmetic and copies ran while one was open for 9% -> 9% of each run, Pallas kernels for 40% -> 41%
where the time goes in v4:
time: 643 us; the launch traced here: 636 us
  Pallas kernels  312 us (49%)
  waiting for transfers between devices  184 us (29%)
  local copies, waits for them, and re-layouts  49.9 us (8%)
  starting transfers between devices  47.9 us (7%)
  other arithmetic  26.3 us (4%)
  between operations  15.7 us (2%)
    pallas_call x32, Pallas kernels, call(): pl.pallas_call(kernel, out_shape=tuple((jax.ShapeDtypeStruct(s, t) for s,...  312 us
    ppermute x27, waiting for transfers between devices, flip(): lax.ppermute(value, axis, [(i, i ^ bits) for i in range(size)])  69.1 us
    ppermute x9, waiting for transfers between devices, pass_on(): return lax.ppermute(value, 'mp', ring)  62.6 us
    ppermute x27, starting transfers between devices, flip(): lax.ppermute(value, axis, [(i, i ^ bits) for i in range(size)])  29.1 us
    ppermute x2, waiting for transfers between devices, ring_start(): return lax.ppermute(slots[mp_size - 1], 'mp', back_ring)  20.6 us
    unnamed x159, local copies, waits for them, and re-layouts  17.9 us
  transfers between devices with their start and end apart: 53, of which 26 were waited for; matrix products, arithmetic and copies ran while one was open for 9% of the time, Pallas kernels for 41%

profile of v4, /device:TPU:0, one launch (start us, length us, event | category | flops | bytes accessed | tf_op | source)
XLA Modules:
  0.0 635.8 jit_solution(8566373738023550696)
XLA Ops:
  52.1 11.9 %collective-permute-done.6 = bf16[144,1280]{1,0:T(8,128)(2,1)S(1)} collective-permute-done((bf16[144,1280]{1,0:T(8,128)(2,1)S(1)}, bf16[144,1280]{1,0:T(8,128)(2,1)S(1)}, u32[]{:S(2)}, u32[]{:S(2)}) %collective-permute-start.6) | collective-permute-done | bytes 368672 | tf_op jit(solution)/shard_map/ppermute | solution.py:799
  65.5 9.5 %collective-permute-done.8 = bf16[144,1280]{1,0:T(8,128)(2,1)S(1)} collective-permute-done((bf16[144,1280]{1,0:T(8,128)(2,1)S(1)}, bf16[144,1280]{1,0:T(8,128)(2,1)S(1)}, u32[]{:S(2)}, u32[]{:S(2)}) %collective-permute-start.8) | collective-permute-done | bytes 368672 | tf_op jit(solution)/shard_map/ppermute | solution.py:799
  77.4 15.2 %collective-permute-done.9 = bf16[144,2048]{1,0:T(8,128)(2,1)} collective-permute-done((bf16[144,2048]{1,0:T(8,128)(2,1)}, bf16[144,2048]{1,0:T(8,128)(2,1)}, u32[]{:S(2)}, u32[]{:S(2)}) %collective-permute-start.9) | collective-permute-done | bytes 589856 | tf_op jit(solution)/shard_map/ppermute | solution.py:799
  136.2 15.1 %shard_map.301 = (bf16[512,1024]{1,0:T(8,128)(2,1)S(1)}, f32[8,8,512]{2,1,0:T(8,128)S(1)}) custom-call(s32[7]{0:T(128)S(1)} %stack.38.info, bf16[512,1024]{1,0:T(8,128)(2,1)} %copy-done.11, bf16[1024,1024]{1,0:T(8,128)(2,1)} %shard_map.298.k_ref, bf16[1024,1024]{1,0:T(8,128)(2,1)} %shard_map.299.v_ref), custom_call_target="tpu_custom_call" | custom-call | flops 160000000 | bytes 1024 | tf_op jit(solution)/shard_map/pallas_call | solution.py:48
  177.4 17.9 %shard_map.306 = (bf16[512,1024]{1,0:T(8,128)(2,1)S(1)}, f32[8,8,512]{2,1,0:T(8,128)S(1)}) custom-call(s32[7]{0:T(128)S(1)} %stack.38.info, bf16[512,1024]{1,0:T(8,128)(2,1)} %copy-done.12, bf16[1024,1024]{1,0:T(8,128)(2,1)} %shard_map.304.k_ref, bf16[1024,1024]{1,0:T(8,128)(2,1)} %shard_map.305.v_ref), custom_call_target="tpu_custom_call" | custom-call | flops 160000000 | bytes 1024 | tf_op jit(solution)/shard_map/pallas_call | solution.py:48
  210.1 32.8 %shard_map.308 = (bf16[512,4096]{1,0:T(8,128)(2,1)}, bf16[512,4096]{1,0:T(8,128)(2,1)}, f32[8,4096]{1,0:T(8,128)S(1)}, bf16[512,1024]{1,0:T(8,128)(2,1)S(1)}, f3...) custom-call(s32[7]{0:T(128)S(1)} %stack.38.info, bf16[512,1024]{1,0:T(8,128)(2,1)} %copy-done.13, ...), custom_call_target="tpu_custom_call" | custom-call | flops 320000000 | bytes 1024 | tf_op jit(solution)/shard_map/pallas_call | solution.py:48
  243.9 10.8 %shard_map.309 = bf16[512,8192]{1,0:T(8,128)(2,1)} custom-call(s32[7]{0:T(128)S(1)} %stack.38.info, bf16[1,512,1024]{2,1,0:T(8,128)(2,1)S(1)} %bitcast.48, bf16[1,512,1024]{2,1,0:T(8,128)(2,1)} %maximum_select_fusion.c0_ref.c1_ref.refs_1_, bf16[512,4096]{1,0:T(8,128)(2,1)} %get-tuple-element.178.refs_2_, bf16[512,4096]{1,0:T(8,128)(2,1)} %get-tuple-element.179.refs_3_), custom_call_target="tpu_custom_call" | custom-call | flops 80000000 | bytes 1024 | tf_op jit(solution)/shard_map/pallas_call | solution.py:48
  260.8 25.8 %shard_map.311 = (bf16[512,1024]{1,0:T(8,128)(2,1)S(1)}, bf16[1024,1024]{1,0:T(8,128)(2,1)}, bf16[1024,1024]{1,0:T(8,128)(2,1)}, f32[8,1024]{1,0:T(8,128)S(1)}, f32[8,1024]{1,0:T(8,128)S(1)}) custom-call(s32[7]{0:T(128)S(1)} %stack.38.info, bf16[512,1024]{1,0:T(8,128)(2,1)} %copy-done.12, bf16[1024,1024]{1,0:T(8,128)(2,1)} %shard_map.304.k_ref, ...), custom_call_target="tpu_custom_call" | custom-call | flops 240000000 | bytes 1024 | tf_op jit(solution)/shard_map/pallas_call | solution.py:48
  286.7 8.9 %shard_map.312 = bf16[1024,1024]{1,0:T(8,128)(2,1)} custom-call(s32[7]{0:T(128)S(1)} %stack.38.info, bf16[1024,1024]{1,0:T(8,128)(2,1)} %get-tuple-element.183.refs_0_.refs_5_, bf16[2,1024,256]{2,1,0:T(8,128)(2,1)S(1)} %copy-done.2, bf16[1024,3840]{1,0:T(8,128)(2,1)} %all-gather.11.cloned.1.call-done.rest_ref.refs_2_.refs_5_, ...), custom_call_target="tpu_custom_call" | custom-call | flops 50000000 | bytes 1024 | tf_op jit(solution)/shard_map/pallas_call | solution.py:48
  298.2 12.7 %shard_map.313 = (bf16[128,8192]{1,0:T(8,128)(2,1)}, bf16[128,8192]{1,0:T(8,128)(2,1)}, bf16[128,8192]{1,0:T(8,128)(2,1)}, bf16[128,8192]{1,0:T(8,128)(2,1)}) custom-call(s32[7]{0:T(128)S(1)} %stack.38.info, bf16[1,512,1024]{2,1,0:T(8,128)(2,1)S(1)} %bitcast.49, bf16[1,512,1024]{2,1,0:T(8,128)(2,1)} %maximum_select_fusion.c0_ref.c1_ref.refs_1_, ...), custom_call_target="tpu_custom_call" | custom-call | flops 80000000 | bytes 1024 | tf_op jit(solution)/shard_map/pallas_call | solution.py:48
  313.7 10.7 %shard_map.315 = bf16[512,4096]{1,0:T(8,128)(2,1)} custom-call(s32[7]{0:T(128)S(1)} %stack.38.info, bf16[1,512,1024]{2,1,0:T(8,128)(2,1)S(1)} %bitcast.44, bf16[1,1024,1024]{2,1,0:T(8,128)(2,1)} %dynamic-slice_select_fusion.x_ref.refs_1_.refs_2_, bf16[1,1024,1024]{2,1,0:T(8,128)(2,1)} %dynamic-slice_select_fusion.x_ref.refs_1_.refs_2_, ...), custom_call_target="tpu_custom_call" | custom-call | flops 80000000 | bytes 1024 | tf_op jit(solution)/shard_map/pallas_call | solution.py:48
  326.7 9.3 %all-gather.15.cloned.1.call-done.same_ref = bf16[2048,1024]{1,0:T(8,128)(2,1)} async-done(((bf16[512,1024]{1,0:T(8,128)(2,1)}), bf16[2048,1024]{1,0:T(8,128)(2,1)}) %all-gather.15.cloned.1.call-update) | async-done | bytes 4194320 | tf_op jit(solution)/shard_map/all_gather | solution.py:923
  350.3 20.6 %shard_map.317 = (bf16[512,1024]{1,0:T(8,128)(2,1)S(1)}, bf16[1024,1024]{1,0:T(8,128)(2,1)}, bf16[1024,1024]{1,0:T(8,128)(2,1)}, f32[8,1024]{1,0:T(8,128)S(1)}, f32[8,1024]{1,0:T(8,128)S(1)}) custom-call(s32[7]{0:T(128)S(1)} %stack.38.info, bf16[512,1024]{1,0:T(8,128)(2,1)} %copy-done.11, bf16[1024,1024]{1,0:T(8,128)(2,1)} %shard_map.298.k_ref, ...), custom_call_target="tpu_custom_call" | custom-call | flops 240000000 | bytes 1024 | tf_op jit(solution)/shard_map/pallas_call | solution.py:48
  370.9 9.3 %shard_map.318 = bf16[1024,1024]{1,0:T(8,128)(2,1)} custom-call(s32[7]{0:T(128)S(1)} %stack.38.info, bf16[1024,1024]{1,0:T(8,128)(2,1)} %get-tuple-element.200.refs_0_.refs_6_, bf16[3,1024,256]{2,1,0:T(8,128)(2,1)S(1)} %copy-done.1, bf16[1024,2304]{1,0:T(8,128)(2,1)} %all-gather.9.cloned.1.call-done.rest_ref.refs_2_.refs_5_, ...), custom_call_target="tpu_custom_call" | custom-call | flops 50000000 | bytes 1024 | tf_op jit(solution)/shard_map/pallas_call | solution.py:48
  385.8 10.7 %shard_map.319 = bf16[512,4096]{1,0:T(8,128)(2,1)} custom-call(s32[7]{0:T(128)S(1)} %stack.38.info, bf16[1,1024,1024]{2,1,0:T(8,128)(2,1)} %bitcast.59, bf16[1,1024,1024]{2,1,0:T(8,128)(2,1)} %bitcast.60, bf16[1,1024,1024]{2,1,0:T(8,128)(2,1)} %bitcast.61, bf16[1,1024,1024]{2,1,0:T(8,128)(2,1)} %bitcast.62, bf16[1,512,1024]{2,1,0:T(8,128)(2,1)S(1)} %bitcast.47, ...), custom_call_target="tpu_custom_call" | custom-call | flops 80000000 | bytes 1024 | tf_op jit(solution)/shard_map/pallas_call | solution.py:48
  396.5 12.0 %shard_map.320 = (bf16[128,4096]{1,0:T(8,128)(2,1)S(1)}, bf16[128,4096]{1,0:T(8,128)(2,1)}, bf16[128,4096]{1,0:T(8,128)(2,1)}, bf16[128,4096]{1,0:T(8,128)(2,1)}) custom-call(s32[7]{0:T(128)S(1)} %stack.38.info, bf16[1,512,1024]{2,1,0:T(8,128)(2,1)} %bitcast.43, bf16[1,1024,1024]{2,1,0:T(8,128)(2,1)} %dynamic-slice_select_fusion.x_ref.refs_1_.refs_2_, ...), custom_call_target="tpu_custom_call" | custom-call | flops 80000000 | bytes 1024 | tf_op jit(solution)/shard_map/pallas_call | solution.py:48
  426.2 7.7 %shard_map.321 = bf16[2048,1024]{1,0:T(8,128)(2,1)} custom-call(s32[7]{0:T(128)S(1)} %stack.38.info, bf16[2048,1024]{1,0:T(8,128)(2,1)} %all-gather.15.cloned.1.call-done.same_ref, bf16[1024,1024]{1,0:T(8,128)(2,1)} %collective-permute-done.19.other_ref), custom_call_target="tpu_custom_call" | custom-call | flops 40000000 | bytes 1024 | tf_op jit(solution)/shard_map/pallas_call | solution.py:48
  436.5 11.9 %shard_map.323 = (bf16[128,4096]{1,0:T(8,128)(2,1)S(1)}, bf16[128,4096]{1,0:T(8,128)(2,1)}, bf16[128,4096]{1,0:T(8,128)(2,1)}, bf16[128,4096]{1,0:T(8,128)(2,1)}) custom-call(s32[7]{0:T(128)S(1)} %stack.38.info, bf16[1,1024,1024]{2,1,0:T(8,128)(2,1)} %bitcast.63, bf16[1,1024,1024]{2,1,0:T(8,128)(2,1)} %bitcast.64, bf16[1,1024,1024]{2,1,0:T(8,128)(2,1)} %bitcast.65, ...), custom_call_target="tpu_custom_call" | custom-call | flops 80000000 | bytes 1024 | tf_op jit(solution)/shard_map/pallas_call | solution.py:48
  454.0 14.7 %collective-permute-done.26 = bf16[128,4096]{1,0:T(8,128)(2,1)S(1)} collective-permute-done((bf16[128,4096]{1,0:T(8,128)(2,1)}, bf16[128,4096]{1,0:T(8,128)(2,1)S(1)}, u32[]{:S(2)}, u32[]{:S(2)}) %collective-permute-start.26) | collective-permute-done | bytes 1048608 | tf_op jit(solution)/shard_map/ppermute | solution.py:728
  468.7 21.9 %collective-permute-done.28 = bf16[128,4096]{1,0:T(8,128)(2,1)S(1)} collective-permute-done((bf16[128,4096]{1,0:T(8,128)(2,1)S(1)}, bf16[128,4096]{1,0:T(8,128)(2,1)S(1)}, u32[]{:S(2)}, u32[]{:S(2)}) %collective-permute-start.28) | collective-permute-done | bytes 1048608 | tf_op jit(solution)/shard_map/ppermute | solution.py:728
  504.6 19.1 %collective-permute-done.30 = bf16[128,1024]{1,0:T(8,128)(2,1)S(1)} collective-permute-done((bf16[128,1024]{1,0:T(8,128)(2,1)S(1)}, bf16[128,1024]{1,0:T(8,128)(2,1)S(1)}, u32[]{:S(2)}, u32[]{:S(2)}) %collective-permute-start.30) | collective-permute-done | bytes 262176 | tf_op jit(solution)/shard_map/ppermute | solution.py:1059
  528.5 12.0 %collective-permute-done.34 = bf16[128,4096]{1,0:T(8,128)(2,1)} collective-permute-done((bf16[128,4096]{1,0:T(8,128)(2,1)S(1)}, bf16[128,4096]{1,0:T(8,128)(2,1)}, u32[]{:S(2)}, u32[]{:S(2)}) %collective-permute-start.34) | collective-permute-done | bytes 1048608 | tf_op jit(solution)/shard_map/ppermute | solution.py:728
  558.7 9.3 %shard_map.324 = f32[2048,1024]{1,0:T(8,128)} custom-call(s32[7]{0:T(128)S(1)} %stack.38.info, bf16[2048,1024]{1,0:T(8,128)(2,1)} %all-gather.17.cloned.1.call-done.same_ref, bf16[1024,1024]{1,0:T(8,128)(2,1)} %copy-done.39), custom_call_target="tpu_custom_call" | custom-call | flops 40000000 | bytes 1024 | tf_op jit(solution)/shard_map/pallas_call | solution.py:48
  568.0 9.2 %collective-permute-done.38 = bf16[128,1024]{1,0:T(8,128)(2,1)S(1)} collective-permute-done((bf16[128,1024]{1,0:T(8,128)(2,1)S(1)}, bf16[128,1024]{1,0:T(8,128)(2,1)S(1)}, u32[]{:S(2)}, u32[]{:S(2)}) %collective-permute-start.38) | collective-permute-done | bytes 262176 | tf_op jit(solution)/shard_map/ppermute | solution.py:912
  (386 shorter events, 281.1 us)
Async XLA Ops:
  7.2 86.2 %all-gather.9.cloned.1.call-start = ((), (), s32[]{:S(2)}) async-start(), calls=%async_computation | async-start | bytes 5308416 | tf_op jit(solution)/shard_map/all_gather | solution.py:809
  39.2 113.8 %all-gather.11.cloned.1.call-start = ((), (), s32[]{:S(2)}) async-start(), calls=%async_computation.1 | async-start | bytes 8847360 | tf_op jit(solution)/shard_map/all_gather | solution.py:809
  77.3 131.4 %all-gather.13.cloned.1.call-start = ((), (), s32[]{:S(2)}) async-start(), calls=%async_computation.2 | async-start | bytes 14155776 | tf_op jit(solution)/shard_map/all_gather | solution.py:809
  124.5 211.5 %all-gather.15.cloned.1.call-start = ((), (), s32[]{:S(2)}) async-start(), calls=%async_computation.3 | async-start | bytes 5242880 | tf_op jit(solution)/shard_map/all_gather | solution.py:923
  254.7 40.9 %collective-permute-start.13 = (bf16[512,8192]{1,0:T(8,128)(2,1)}, bf16[512,8192]{1,0:T(8,128)(2,1)}, u32[]{:S(2)}, u32[]{:S(2)}) collective-permute-start(bf16[512,8192]{1,0:T(8,128)(2,1)} %shard_map.309), channel_id=1, source_target_pairs={{0,4},{4,0},{8,12},{12,8},{16,20},{20,16},{24,28},{28,24},{1,5},{5... | collective-permute-start | bytes 25165832 | tf_op jit(solution)/shard_map/ppermute | solution.py:728
  255.0 166.5 %all-gather.19.cloned.1.call-start = ((), (), s32[]{:S(2)}) async-start(), calls=%async_computation.5 | async-start | bytes 5242880 | tf_op jit(solution)/shard_map/all_gather | solution.py:923
  324.4 57.4 %collective-permute-start.15 = (bf16[512,4096]{1,0:T(8,128)(2,1)}, bf16[512,4096]{1,0:T(8,128)(2,1)}, u32[]{:S(2)}, u32[]{:S(2)}) collective-permute-start(bf16[512,4096]{1,0:T(8,128)(2,1)} %shard_map.315), channel_id=1, source_target_pairs={{0,4},{4,0},{8,12},{12,8},{16,20},{20,16},{24,28},{28,24},{1,5},{5... | collective-permute-start | bytes 12582920 | tf_op jit(solution)/shard_map/ppermute | solution.py:728
  324.6 220.6 %all-gather.17.cloned.1.call-start = ((), (), s32[]{:S(2)}) async-start(), calls=%async_computation.4 | async-start | bytes 5242880 | tf_op jit(solution)/shard_map/all_gather | solution.py:923
  324.7 57.1 %collective-permute-start.16 = (bf16[128,8192]{1,0:T(8,128)(2,1)}, bf16[128,8192]{1,0:T(8,128)(2,1)}, u32[]{:S(2)}, u32[]{:S(2)}) collective-permute-start(bf16[128,8192]{1,0:T(8,128)(2,1)} %get-tuple-element.204), channel_id=1, source_target_pairs={{0,8},{4,12},{8,0},{12,4},{16,24},{20,28},{24,16},{28,20},{1,9},{5... | collective-permute-start | bytes 6291464 | tf_op jit(solution)/shard_map/ppermute | solution.py:728
  326.2 55.6 %collective-permute-start.17 = (bf16[128,8192]{1,0:T(8,128)(2,1)}, bf16[128,8192]{1,0:T(8,128)(2,1)}, u32[]{:S(2)}, u32[]{:S(2)}) collective-permute-start(bf16[128,8192]{1,0:T(8,128)(2,1)} %get-tuple-element.205), channel_id=1, source_target_pairs={{0,16},{4,20},{8,24},{12,28},{16,0},{20,4},{24,8},{28,12},{1,17},{... | collective-permute-start | bytes 6291464 | tf_op jit(solution)/shard_map/ppermute | solution.py:728
  337.7 70.7 %collective-permute-start.19 = (bf16[1024,1024]{1,0:T(8,128)(2,1)S(1)}, bf16[1024,1024]{1,0:T(8,128)(2,1)}, u32[]{:S(2)}, u32[]{:S(2)}) collective-permute-start(bf16[1024,1024]{1,0:T(8,128)(2,1)S(1)} %constant_dynamic-slice_fusion.5), channel_id=1, source_target_pairs={{0,4},{4,0},{8,12},{12,8},{16,20},{20,16},{24,28},{28,24},{1,5},{5... | collective-permute-start | bytes 6291464 | tf_op jit(solution)/shard_map/ppermute | solution.py:728
  417.9 189.3 %all-gather.21.cloned.1.call-start = ((), (), s32[]{:S(2)}) async-start(), calls=%async_computation.6 | async-start | bytes 4718592 | tf_op jit(solution)/shard_map/all_gather | solution.py:920
  419.0 29.4 %collective-permute-start.21 = (bf16[128,4096]{1,0:T(8,128)(2,1)}, bf16[128,4096]{1,0:T(8,128)(2,1)}, u32[]{:S(2)}, u32[]{:S(2)}) collective-permute-start(bf16[128,4096]{1,0:T(8,128)(2,1)} %get-tuple-element.229), channel_id=1, source_target_pairs={{0,24},{4,28},{8,16},{12,20},{16,8},{20,12},{24,0},{28,4},{1,25},{... | collective-permute-start | bytes 3145736 | tf_op jit(solution)/shard_map/ppermute | solution.py:728
  424.6 66.1 %collective-permute-start.24 = (bf16[1024,1024]{1,0:T(8,128)(2,1)}, bf16[1024,1024]{1,0:T(8,128)(2,1)}, u32[]{:S(2)}, u32[]{:S(2)}) collective-permute-start(bf16[1024,1024]{1,0:T(8,128)(2,1)} %constant_dynamic-slice_fusion.1), channel_id=1, source_target_pairs={{0,4},{4,0},{8,12},{12,8},{16,20},{20,16},{24,28},{28,24},{1,5},{5... | collective-permute-start | bytes 6291464 | tf_op jit(solution)/shard_map/ppermute | solution.py:728
  425.1 43.6 %collective-permute-start.26 = (bf16[128,4096]{1,0:T(8,128)(2,1)}, bf16[128,4096]{1,0:T(8,128)(2,1)S(1)}, u32[]{:S(2)}, u32[]{:S(2)}) collective-permute-start(bf16[128,4096]{1,0:T(8,128)(2,1)} %get-tuple-element.244), channel_id=1, source_target_pairs={{0,8},{4,12},{8,0},{12,4},{16,24},{20,28},{24,16},{28,20},{1,9},{5... | collective-permute-start | bytes 3145736 | tf_op jit(solution)/shard_map/ppermute | solution.py:728
  425.7 43.0 %collective-permute-start.27 = (bf16[128,4096]{1,0:T(8,128)(2,1)}, bf16[128,4096]{1,0:T(8,128)(2,1)S(1)}, u32[]{:S(2)}, u32[]{:S(2)}) collective-permute-start(bf16[128,4096]{1,0:T(8,128)(2,1)} %get-tuple-element.245), channel_id=1, source_target_pairs={{0,16},{4,20},{8,24},{12,28},{16,0},{20,4},{24,8},{28,12},{1,17},{... | collective-permute-start | bytes 3145736 | tf_op jit(solution)/shard_map/ppermute | solution.py:728
  434.0 56.6 %collective-permute-start.28 = (bf16[128,4096]{1,0:T(8,128)(2,1)S(1)}, bf16[128,4096]{1,0:T(8,128)(2,1)S(1)}, u32[]{:S(2)}, u32[]{:S(2)}) collective-permute-start(bf16[128,4096]{1,0:T(8,128)(2,1)S(1)} %copy-done.60), channel_id=1, source_target_pairs={{0,24},{4,28},{8,16},{12,20},{16,8},{20,12},{24,0},{28,4},{1,25},{... | collective-permute-start | bytes 3145736 | tf_op jit(solution)/shard_map/ppermute | solution.py:728
  453.0 39.2 %collective-permute-start.25 = (bf16[128,2048]{1,0:T(8,128)(2,1)S(1)}, bf16[128,2048]{1,0:T(8,128)(2,1)S(1)}, u32[]{:S(2)}, u32[]{:S(2)}) collective-permute-start(bf16[128,2048]{1,0:T(8,128)(2,1)S(1)} %get-tuple-element.242), channel_id=1, source_target_pairs={{0,3},{1,0},{2,1},{3,2},{4,7},{5,4},{6,5},{7,6},{8,11},{9,8},{10,9... | collective-permute-start | bytes 1572872 | tf_op jit(solution)/shard_map/ppermute | solution.py:1059
  492.3 31.5 %collective-permute-start.29 = (bf16[128,2048]{1,0:T(8,128)(2,1)S(1)}, bf16[128,2048]{1,0:T(8,128)(2,1)S(1)}, u32[]{:S(2)}, u32[]{:S(2)}) collective-permute-start(bf16[128,2048]{1,0:T(8,128)(2,1)S(1)} %add_convert_fusion.3), channel_id=1, source_target_pairs={{0,3},{1,0},{2,1},{3,2},{4,7},{5,4},{6,5},{7,6},{8,11},{9,8},{10,9... | collective-permute-start | bytes 1572872 | tf_op jit(solution)/shard_map/ppermute | solution.py:1062
  492.5 31.2 %collective-permute-start.30 = (bf16[128,1024]{1,0:T(8,128)(2,1)S(1)}, bf16[128,1024]{1,0:T(8,128)(2,1)S(1)}, u32[]{:S(2)}, u32[]{:S(2)}) collective-permute-start(bf16[128,1024]{1,0:T(8,128)(2,1)S(1)} %add_convert_fusion.19), channel_id=1, source_target_pairs={{0,3},{1,0},{2,1},{3,2},{4,7},{5,4},{6,5},{7,6},{8,11},{9,8},{10,9... | collective-permute-start | bytes 786440 | tf_op jit(solution)/shard_map/ppermute | solution.py:1059
  493.7 34.8 %collective-permute-start.33 = (bf16[128,4096]{1,0:T(8,128)(2,1)}, bf16[128,4096]{1,0:T(8,128)(2,1)}, u32[]{:S(2)}, u32[]{:S(2)}) collective-permute-start(bf16[128,4096]{1,0:T(8,128)(2,1)} %get-tuple-element.259), channel_id=1, source_target_pairs={{0,8},{4,12},{8,0},{12,4},{16,24},{20,28},{24,16},{28,20},{1,9},{5... | collective-permute-start | bytes 3145736 | tf_op jit(solution)/shard_map/ppermute | solution.py:728
  495.1 45.3 %collective-permute-start.34 = (bf16[128,4096]{1,0:T(8,128)(2,1)S(1)}, bf16[128,4096]{1,0:T(8,128)(2,1)}, u32[]{:S(2)}, u32[]{:S(2)}) collective-permute-start(bf16[128,4096]{1,0:T(8,128)(2,1)S(1)} %copy-done.62), channel_id=1, source_target_pairs={{0,16},{4,20},{8,24},{12,28},{16,0},{20,4},{24,8},{28,12},{1,17},{... | collective-permute-start | bytes 3145736 | tf_op jit(solution)/shard_map/ppermute | solution.py:728
  496.6 45.0 %collective-permute-start.35 = (bf16[128,4096]{1,0:T(8,128)(2,1)S(1)}, bf16[128,4096]{1,0:T(8,128)(2,1)}, u32[]{:S(2)}, u32[]{:S(2)}) collective-permute-start(bf16[128,4096]{1,0:T(8,128)(2,1)S(1)} %copy-done.61), channel_id=1, source_target_pairs={{0,24},{4,28},{8,16},{12,20},{16,8},{20,12},{24,0},{28,4},{1,25},{... | collective-permute-start | bytes 3145736 | tf_op jit(solution)/shard_map/ppermute | solution.py:728
  545.1 77.1 %all-gather.23.cloned.1.call-start = ((), (), s32[]{:S(2)}) async-start(), calls=%async_computation.7 | async-start | bytes 4718592 | tf_op jit(solution)/shard_map/all_gather | solution.py:920
  (92 other events, 1055.6 us)
Sparse Core Ops, SparseCore 0:
  39.3 36.9 all-gather.8
  78.7 54.1 all-gather.10
  135.4 73.3 all-gather.12
  255.1 80.8 all-gather.14
  337.4 79.2 all-gather.18
  418.7 99.3 all-gather.16
  545.2 37.6 all-gather.20
  585.4 36.7 all-gather.22

commit v5 on v4

--- a/solution.py
+++ b/solution.py
@@ -1064,13 +1064,12 @@
         ffn_state = ring_start(ffn_slots)
         memory_got = for_other(memory_found)
         memory_got, small, ffn_state, *cross_total = wall(memory_got, small, ffn_state, *cross_total)
-        for k in range(mp_size - 2, 1, -1):
+        for k in range(mp_size - 2, 0, -1):
             ffn_state = ring_next(ffn_slots, k, ffn_state)
         cross_slots = slots_of(cross_total)
         cross_state = ring_start(cross_slots)
         memory_grad = order_rows(info, memory_found, memory_got, rows, group, 1, f32).reshape(memory.shape)
         memory_grad, small, ffn_state, cross_state = wall(memory_grad, small, ffn_state, cross_state)
-        ffn_state = ring_next(ffn_slots, 1, ffn_state)
         for k in range(mp_size - 2, 1, -1):
             cross_state = ring_next(cross_slots, k, cross_state)
         ffn_state, small, cross_state, *self_total = wall(ffn_state, small, cross_state, *self_total)

time: 643 us -> 665 us (1.034)
  waiting for transfers between devices: 184 us -> 207 us
    ppermute x4, waiting for transfers between devices: 2.62 us -> 25.8 us  [ring_next(): return lax.ppermute(add_up([slots[k], state]), 'mp', back_ring)]
    ppermute x27, waiting for transfers between devices: 69.1 us -> 83.5 us  [flip(): lax.ppermute(value, axis, [(i, i ^ bits) for i in range(size)])]
    ppermute x2, waiting for transfers between devices: 20.6 us -> 7.62 us  [ring_start(): return lax.ppermute(slots[mp_size - 1], 'mp', back_ring)]
  transfers between devices with their start and end apart: 53 -> 53, of which waited for: 26 -> 27; matrix products, arithmetic and copies ran while one was open for 9% -> 9% of each run, Pallas kernels for 41% -> 40%
where the time goes in v5:
time: 665 us; the launch traced here: 658 us
  Pallas kernels  312 us (47%)
  waiting for transfers between devices  207 us (31%)
  local copies, waits for them, and re-layouts  49.9 us (8%)
  starting transfers between devices  47 us (7%)
  other arithmetic  26.3 us (4%)
  between operations  15.7 us (2%)
    pallas_call x32, Pallas kernels, call(): pl.pallas_call(kernel, out_shape=tuple((jax.ShapeDtypeStruct(s, t) for s,...  312 us
    ppermute x27, waiting for transfers between devices, flip(): lax.ppermute(value, axis, [(i, i ^ bits) for i in range(size)])  83.5 us
    ppermute x9, waiting for transfers between devices, pass_on(): return lax.ppermute(value, 'mp', ring)  62.6 us
    ppermute x27, starting transfers between devices, flip(): lax.ppermute(value, axis, [(i, i ^ bits) for i in range(size)])  29.1 us
    ppermute x4, waiting for transfers between devices, ring_next(): return lax.ppermute(add_up([slots[k], state]), 'mp', back_ring)  25.8 us
    unnamed x159, local copies, waits for them, and re-layouts  17.9 us
  transfers between devices with their start and end apart: 53, of which 27 were waited for; matrix products, arithmetic and copies ran while one was open for 9% of the time, Pallas kernels for 40%

profile of v5, /device:TPU:0, one launch (start us, length us, event | category | flops | bytes accessed | tf_op | source)
XLA Modules:
  0.0 658.1 jit_solution(15147328115277483918)
XLA Ops:
  52.1 11.9 %collective-permute-done.6 = bf16[144,1280]{1,0:T(8,128)(2,1)S(1)} collective-permute-done((bf16[144,1280]{1,0:T(8,128)(2,1)S(1)}, bf16[144,1280]{1,0:T(8,128)(2,1)S(1)}, u32[]{:S(2)}, u32[]{:S(2)}) %collective-permute-start.6) | collective-permute-done | bytes 368672 | tf_op jit(solution)/shard_map/ppermute | solution.py:799
  65.5 9.5 %collective-permute-done.8 = bf16[144,1280]{1,0:T(8,128)(2,1)S(1)} collective-permute-done((bf16[144,1280]{1,0:T(8,128)(2,1)S(1)}, bf16[144,1280]{1,0:T(8,128)(2,1)S(1)}, u32[]{:S(2)}, u32[]{:S(2)}) %collective-permute-start.8) | collective-permute-done | bytes 368672 | tf_op jit(solution)/shard_map/ppermute | solution.py:799
  77.4 15.2 %collective-permute-done.9 = bf16[144,2048]{1,0:T(8,128)(2,1)} collective-permute-done((bf16[144,2048]{1,0:T(8,128)(2,1)}, bf16[144,2048]{1,0:T(8,128)(2,1)}, u32[]{:S(2)}, u32[]{:S(2)}) %collective-permute-start.9) | collective-permute-done | bytes 589856 | tf_op jit(solution)/shard_map/ppermute | solution.py:799
  136.2 15.1 %shard_map.301 = (bf16[512,1024]{1,0:T(8,128)(2,1)S(1)}, f32[8,8,512]{2,1,0:T(8,128)S(1)}) custom-call(s32[7]{0:T(128)S(1)} %stack.38.info, bf16[512,1024]{1,0:T(8,128)(2,1)} %copy-done.11, bf16[1024,1024]{1,0:T(8,128)(2,1)} %shard_map.298.k_ref, bf16[1024,1024]{1,0:T(8,128)(2,1)} %shard_map.299.v_ref), custom_call_target="tpu_custom_call" | custom-call | flops 160000000 | bytes 1024 | tf_op jit(solution)/shard_map/pallas_call | solution.py:48
  177.4 17.9 %shard_map.306 = (bf16[512,1024]{1,0:T(8,128)(2,1)S(1)}, f32[8,8,512]{2,1,0:T(8,128)S(1)}) custom-call(s32[7]{0:T(128)S(1)} %stack.38.info, bf16[512,1024]{1,0:T(8,128)(2,1)} %copy-done.12, bf16[1024,1024]{1,0:T(8,128)(2,1)} %shard_map.304.k_ref, bf16[1024,1024]{1,0:T(8,128)(2,1)} %shard_map.305.v_ref), custom_call_target="tpu_custom_call" | custom-call | flops 160000000 | bytes 1024 | tf_op jit(solution)/shard_map/pallas_call | solution.py:48
  210.1 32.8 %shard_map.308 = (bf16[512,4096]{1,0:T(8,128)(2,1)}, bf16[512,4096]{1,0:T(8,128)(2,1)}, f32[8,4096]{1,0:T(8,128)S(1)}, bf16[512,1024]{1,0:T(8,128)(2,1)S(1)}, f3...) custom-call(s32[7]{0:T(128)S(1)} %stack.38.info, bf16[512,1024]{1,0:T(8,128)(2,1)} %copy-done.13, ...), custom_call_target="tpu_custom_call" | custom-call | flops 320000000 | bytes 1024 | tf_op jit(solution)/shard_map/pallas_call | solution.py:48
  243.9 10.8 %shard_map.309 = bf16[512,8192]{1,0:T(8,128)(2,1)} custom-call(s32[7]{0:T(128)S(1)} %stack.38.info, bf16[1,512,1024]{2,1,0:T(8,128)(2,1)S(1)} %bitcast.48, bf16[1,512,1024]{2,1,0:T(8,128)(2,1)} %maximum_select_fusion.c0_ref.c1_ref.refs_1_, bf16[512,4096]{1,0:T(8,128)(2,1)} %get-tuple-element.178.refs_2_, bf16[512,4096]{1,0:T(8,128)(2,1)} %get-tuple-element.179.refs_3_), custom_call_target="tpu_custom_call" | custom-call | flops 80000000 | bytes 1024 | tf_op jit(solution)/shard_map/pallas_call | solution.py:48
  260.8 25.8 %shard_map.311 = (bf16[512,1024]{1,0:T(8,128)(2,1)S(1)}, bf16[1024,1024]{1,0:T(8,128)(2,1)}, bf16[1024,1024]{1,0:T(8,128)(2,1)}, f32[8,1024]{1,0:T(8,128)S(1)}, f32[8,1024]{1,0:T(8,128)S(1)}) custom-call(s32[7]{0:T(128)S(1)} %stack.38.info, bf16[512,1024]{1,0:T(8,128)(2,1)} %copy-done.12, bf16[1024,1024]{1,0:T(8,128)(2,1)} %shard_map.304.k_ref, ...), custom_call_target="tpu_custom_call" | custom-call | flops 240000000 | bytes 1024 | tf_op jit(solution)/shard_map/pallas_call | solution.py:48
  286.7 8.9 %shard_map.312 = bf16[1024,1024]{1,0:T(8,128)(2,1)} custom-call(s32[7]{0:T(128)S(1)} %stack.38.info, bf16[1024,1024]{1,0:T(8,128)(2,1)} %get-tuple-element.183.refs_0_.refs_5_, bf16[2,1024,256]{2,1,0:T(8,128)(2,1)S(1)} %copy-done.2, bf16[1024,3840]{1,0:T(8,128)(2,1)} %all-gather.11.cloned.1.call-done.rest_ref.refs_2_.refs_5_, ...), custom_call_target="tpu_custom_call" | custom-call | flops 50000000 | bytes 1024 | tf_op jit(solution)/shard_map/pallas_call | solution.py:48
  298.2 12.7 %shard_map.313 = (bf16[128,8192]{1,0:T(8,128)(2,1)}, bf16[128,8192]{1,0:T(8,128)(2,1)}, bf16[128,8192]{1,0:T(8,128)(2,1)}, bf16[128,8192]{1,0:T(8,128)(2,1)}) custom-call(s32[7]{0:T(128)S(1)} %stack.38.info, bf16[1,512,1024]{2,1,0:T(8,128)(2,1)S(1)} %bitcast.49, bf16[1,512,1024]{2,1,0:T(8,128)(2,1)} %maximum_select_fusion.c0_ref.c1_ref.refs_1_, ...), custom_call_target="tpu_custom_call" | custom-call | flops 80000000 | bytes 1024 | tf_op jit(solution)/shard_map/pallas_call | solution.py:48
  313.7 10.7 %shard_map.315 = bf16[512,4096]{1,0:T(8,128)(2,1)} custom-call(s32[7]{0:T(128)S(1)} %stack.38.info, bf16[1,512,1024]{2,1,0:T(8,128)(2,1)S(1)} %bitcast.44, bf16[1,1024,1024]{2,1,0:T(8,128)(2,1)} %dynamic-slice_select_fusion.x_ref.refs_1_.refs_2_, bf16[1,1024,1024]{2,1,0:T(8,128)(2,1)} %dynamic-slice_select_fusion.x_ref.refs_1_.refs_2_, ...), custom_call_target="tpu_custom_call" | custom-call | flops 80000000 | bytes 1024 | tf_op jit(solution)/shard_map/pallas_call | solution.py:48
  326.7 9.3 %all-gather.15.cloned.1.call-done.same_ref = bf16[2048,1024]{1,0:T(8,128)(2,1)} async-done(((bf16[512,1024]{1,0:T(8,128)(2,1)}), bf16[2048,1024]{1,0:T(8,128)(2,1)}) %all-gather.15.cloned.1.call-update) | async-done | bytes 4194320 | tf_op jit(solution)/shard_map/all_gather | solution.py:923
  350.3 20.6 %shard_map.317 = (bf16[512,1024]{1,0:T(8,128)(2,1)S(1)}, bf16[1024,1024]{1,0:T(8,128)(2,1)}, bf16[1024,1024]{1,0:T(8,128)(2,1)}, f32[8,1024]{1,0:T(8,128)S(1)}, f32[8,1024]{1,0:T(8,128)S(1)}) custom-call(s32[7]{0:T(128)S(1)} %stack.38.info, bf16[512,1024]{1,0:T(8,128)(2,1)} %copy-done.11, bf16[1024,1024]{1,0:T(8,128)(2,1)} %shard_map.298.k_ref, ...), custom_call_target="tpu_custom_call" | custom-call | flops 240000000 | bytes 1024 | tf_op jit(solution)/shard_map/pallas_call | solution.py:48
  370.9 9.3 %shard_map.318 = bf16[1024,1024]{1,0:T(8,128)(2,1)} custom-call(s32[7]{0:T(128)S(1)} %stack.38.info, bf16[1024,1024]{1,0:T(8,128)(2,1)} %get-tuple-element.200.refs_0_.refs_6_, bf16[3,1024,256]{2,1,0:T(8,128)(2,1)S(1)} %copy-done.1, bf16[1024,2304]{1,0:T(8,128)(2,1)} %all-gather.9.cloned.1.call-done.rest_ref.refs_2_.refs_5_, ...), custom_call_target="tpu_custom_call" | custom-call | flops 50000000 | bytes 1024 | tf_op jit(solution)/shard_map/pallas_call | solution.py:48
  385.8 10.7 %shard_map.319 = bf16[512,4096]{1,0:T(8,128)(2,1)} custom-call(s32[7]{0:T(128)S(1)} %stack.38.info, bf16[1,1024,1024]{2,1,0:T(8,128)(2,1)} %bitcast.59, bf16[1,1024,1024]{2,1,0:T(8,128)(2,1)} %bitcast.60, bf16[1,1024,1024]{2,1,0:T(8,128)(2,1)} %bitcast.61, bf16[1,1024,1024]{2,1,0:T(8,128)(2,1)} %bitcast.62, bf16[1,512,1024]{2,1,0:T(8,128)(2,1)S(1)} %bitcast.47, ...), custom_call_target="tpu_custom_call" | custom-call | flops 80000000 | bytes 1024 | tf_op jit(solution)/shard_map/pallas_call | solution.py:48
  396.5 12.0 %shard_map.320 = (bf16[128,4096]{1,0:T(8,128)(2,1)S(1)}, bf16[128,4096]{1,0:T(8,128)(2,1)}, bf16[128,4096]{1,0:T(8,128)(2,1)}, bf16[128,4096]{1,0:T(8,128)(2,1)}) custom-call(s32[7]{0:T(128)S(1)} %stack.38.info, bf16[1,512,1024]{2,1,0:T(8,128)(2,1)} %bitcast.43, bf16[1,1024,1024]{2,1,0:T(8,128)(2,1)} %dynamic-slice_select_fusion.x_ref.refs_1_.refs_2_, ...), custom_call_target="tpu_custom_call" | custom-call | flops 80000000 | bytes 1024 | tf_op jit(solution)/shard_map/pallas_call | solution.py:48
  426.2 7.7 %shard_map.321 = bf16[2048,1024]{1,0:T(8,128)(2,1)} custom-call(s32[7]{0:T(128)S(1)} %stack.38.info, bf16[2048,1024]{1,0:T(8,128)(2,1)} %all-gather.15.cloned.1.call-done.same_ref, bf16[1024,1024]{1,0:T(8,128)(2,1)} %collective-permute-done.19.other_ref), custom_call_target="tpu_custom_call" | custom-call | flops 40000000 | bytes 1024 | tf_op jit(solution)/shard_map/pallas_call | solution.py:48
  436.5 11.9 %shard_map.323 = (bf16[128,4096]{1,0:T(8,128)(2,1)S(1)}, bf16[128,4096]{1,0:T(8,128)(2,1)}, bf16[128,4096]{1,0:T(8,128)(2,1)}, bf16[128,4096]{1,0:T(8,128)(2,1)}) custom-call(s32[7]{0:T(128)S(1)} %stack.38.info, bf16[1,1024,1024]{2,1,0:T(8,128)(2,1)} %bitcast.63, bf16[1,1024,1024]{2,1,0:T(8,128)(2,1)} %bitcast.64, bf16[1,1024,1024]{2,1,0:T(8,128)(2,1)} %bitcast.65, ...), custom_call_target="tpu_custom_call" | custom-call | flops 80000000 | bytes 1024 | tf_op jit(solution)/shard_map/pallas_call | solution.py:48
  454.0 14.7 %collective-permute-done.26 = bf16[128,4096]{1,0:T(8,128)(2,1)S(1)} collective-permute-done((bf16[128,4096]{1,0:T(8,128)(2,1)}, bf16[128,4096]{1,0:T(8,128)(2,1)S(1)}, u32[]{:S(2)}, u32[]{:S(2)}) %collective-permute-start.26) | collective-permute-done | bytes 1048608 | tf_op jit(solution)/shard_map/ppermute | solution.py:728
  468.7 21.9 %collective-permute-done.28 = bf16[128,4096]{1,0:T(8,128)(2,1)S(1)} collective-permute-done((bf16[128,4096]{1,0:T(8,128)(2,1)S(1)}, bf16[128,4096]{1,0:T(8,128)(2,1)S(1)}, u32[]{:S(2)}, u32[]{:S(2)}) %collective-permute-start.28) | collective-permute-done | bytes 1048608 | tf_op jit(solution)/shard_map/ppermute | solution.py:728
  492.3 25.8 %collective-permute-done.29 = bf16[128,2048]{1,0:T(8,128)(2,1)S(1)} collective-permute-done((bf16[128,2048]{1,0:T(8,128)(2,1)S(1)}, bf16[128,2048]{1,0:T(8,128)(2,1)S(1)}, u32[]{:S(2)}, u32[]{:S(2)}) %collective-permute-start.29) | collective-permute-done | bytes 524320 | tf_op jit(solution)/shard_map/ppermute | solution.py:1062
  546.1 19.8 %collective-permute-done.34 = bf16[128,4096]{1,0:T(8,128)(2,1)} collective-permute-done((bf16[128,4096]{1,0:T(8,128)(2,1)S(1)}, bf16[128,4096]{1,0:T(8,128)(2,1)}, u32[]{:S(2)}, u32[]{:S(2)}) %collective-permute-start.34) | collective-permute-done | bytes 1048608 | tf_op jit(solution)/shard_map/ppermute | solution.py:728
  582.4 9.3 %shard_map.324 = f32[2048,1024]{1,0:T(8,128)} custom-call(s32[7]{0:T(128)S(1)} %stack.38.info, bf16[2048,1024]{1,0:T(8,128)(2,1)} %all-gather.17.cloned.1.call-done.same_ref, bf16[1024,1024]{1,0:T(8,128)(2,1)} %copy-done.39), custom_call_target="tpu_custom_call" | custom-call | flops 40000000 | bytes 1024 | tf_op jit(solution)/shard_map/pallas_call | solution.py:48
  591.7 9.2 %collective-permute-done.38 = bf16[128,1024]{1,0:T(8,128)(2,1)S(1)} collective-permute-done((bf16[128,1024]{1,0:T(8,128)(2,1)S(1)}, bf16[128,1024]{1,0:T(8,128)(2,1)S(1)}, u32[]{:S(2)}, u32[]{:S(2)}) %collective-permute-start.38) | collective-permute-done | bytes 262176 | tf_op jit(solution)/shard_map/ppermute | solution.py:912
  (386 shorter events, 288.9 us)
Async XLA Ops:
  7.2 86.2 %all-gather.9.cloned.1.call-start = ((), (), s32[]{:S(2)}) async-start(), calls=%async_computation | async-start | bytes 5308416 | tf_op jit(solution)/shard_map/all_gather | solution.py:809
  39.2 113.8 %all-gather.11.cloned.1.call-start = ((), (), s32[]{:S(2)}) async-start(), calls=%async_computation.1 | async-start | bytes 8847360 | tf_op jit(solution)/shard_map/all_gather | solution.py:809
  77.3 131.4 %all-gather.13.cloned.1.call-start = ((), (), s32[]{:S(2)}) async-start(), calls=%async_computation.2 | async-start | bytes 14155776 | tf_op jit(solution)/shard_map/all_gather | solution.py:809
  124.5 211.5 %all-gather.15.cloned.1.call-start = ((), (), s32[]{:S(2)}) async-start(), calls=%async_computation.3 | async-start | bytes 5242880 | tf_op jit(solution)/shard_map/all_gather | solution.py:923
  254.7 40.9 %collective-permute-start.13 = (bf16[512,8192]{1,0:T(8,128)(2,1)}, bf16[512,8192]{1,0:T(8,128)(2,1)}, u32[]{:S(2)}, u32[]{:S(2)}) collective-permute-start(bf16[512,8192]{1,0:T(8,128)(2,1)} %shard_map.309), channel_id=1, source_target_pairs={{0,4},{4,0},{8,12},{12,8},{16,20},{20,16},{24,28},{28,24},{1,5},{5... | collective-permute-start | bytes 25165832 | tf_op jit(solution)/shard_map/ppermute | solution.py:728
  255.0 166.5 %all-gather.19.cloned.1.call-start = ((), (), s32[]{:S(2)}) async-start(), calls=%async_computation.5 | async-start | bytes 5242880 | tf_op jit(solution)/shard_map/all_gather | solution.py:923
  324.4 57.4 %collective-permute-start.15 = (bf16[512,4096]{1,0:T(8,128)(2,1)}, bf16[512,4096]{1,0:T(8,128)(2,1)}, u32[]{:S(2)}, u32[]{:S(2)}) collective-permute-start(bf16[512,4096]{1,0:T(8,128)(2,1)} %shard_map.315), channel_id=1, source_target_pairs={{0,4},{4,0},{8,12},{12,8},{16,20},{20,16},{24,28},{28,24},{1,5},{5... | collective-permute-start | bytes 12582920 | tf_op jit(solution)/shard_map/ppermute | solution.py:728
  324.6 243.4 %all-gather.17.cloned.1.call-start = ((), (), s32[]{:S(2)}) async-start(), calls=%async_computation.4 | async-start | bytes 5242880 | tf_op jit(solution)/shard_map/all_gather | solution.py:923
  324.7 57.1 %collective-permute-start.16 = (bf16[128,8192]{1,0:T(8,128)(2,1)}, bf16[128,8192]{1,0:T(8,128)(2,1)}, u32[]{:S(2)}, u32[]{:S(2)}) collective-permute-start(bf16[128,8192]{1,0:T(8,128)(2,1)} %get-tuple-element.204), channel_id=1, source_target_pairs={{0,8},{4,12},{8,0},{12,4},{16,24},{20,28},{24,16},{28,20},{1,9},{5... | collective-permute-start | bytes 6291464 | tf_op jit(solution)/shard_map/ppermute | solution.py:728
  326.2 55.6 %collective-permute-start.17 = (bf16[128,8192]{1,0:T(8,128)(2,1)}, bf16[128,8192]{1,0:T(8,128)(2,1)}, u32[]{:S(2)}, u32[]{:S(2)}) collective-permute-start(bf16[128,8192]{1,0:T(8,128)(2,1)} %get-tuple-element.205), channel_id=1, source_target_pairs={{0,16},{4,20},{8,24},{12,28},{16,0},{20,4},{24,8},{28,12},{1,17},{... | collective-permute-start | bytes 6291464 | tf_op jit(solution)/shard_map/ppermute | solution.py:728
  337.7 70.7 %collective-permute-start.19 = (bf16[1024,1024]{1,0:T(8,128)(2,1)S(1)}, bf16[1024,1024]{1,0:T(8,128)(2,1)}, u32[]{:S(2)}, u32[]{:S(2)}) collective-permute-start(bf16[1024,1024]{1,0:T(8,128)(2,1)S(1)} %constant_dynamic-slice_fusion.5), channel_id=1, source_target_pairs={{0,4},{4,0},{8,12},{12,8},{16,20},{20,16},{24,28},{28,24},{1,5},{5... | collective-permute-start | bytes 6291464 | tf_op jit(solution)/shard_map/ppermute | solution.py:728
  383.4 26.3 %collective-permute-start.20 = (bf16[128,4096]{1,0:T(8,128)(2,1)}, bf16[128,4096]{1,0:T(8,128)(2,1)S(1)}, u32[]{:S(2)}, u32[]{:S(2)}) collective-permute-start(bf16[128,4096]{1,0:T(8,128)(2,1)} %get-tuple-element.209), channel_id=1, source_target_pairs={{0,24},{4,28},{8,16},{12,20},{16,8},{20,12},{24,0},{28,4},{1,25},{... | collective-permute-start | bytes 3145736 | tf_op jit(solution)/shard_map/ppermute | solution.py:728
  417.9 213.1 %all-gather.21.cloned.1.call-start = ((), (), s32[]{:S(2)}) async-start(), calls=%async_computation.6 | async-start | bytes 4718592 | tf_op jit(solution)/shard_map/all_gather | solution.py:920
  419.0 29.4 %collective-permute-start.21 = (bf16[128,4096]{1,0:T(8,128)(2,1)}, bf16[128,4096]{1,0:T(8,128)(2,1)}, u32[]{:S(2)}, u32[]{:S(2)}) collective-permute-start(bf16[128,4096]{1,0:T(8,128)(2,1)} %get-tuple-element.229), channel_id=1, source_target_pairs={{0,24},{4,28},{8,16},{12,20},{16,8},{20,12},{24,0},{28,4},{1,25},{... | collective-permute-start | bytes 3145736 | tf_op jit(solution)/shard_map/ppermute | solution.py:728
  424.6 66.1 %collective-permute-start.24 = (bf16[1024,1024]{1,0:T(8,128)(2,1)}, bf16[1024,1024]{1,0:T(8,128)(2,1)}, u32[]{:S(2)}, u32[]{:S(2)}) collective-permute-start(bf16[1024,1024]{1,0:T(8,128)(2,1)} %constant_dynamic-slice_fusion.1), channel_id=1, source_target_pairs={{0,4},{4,0},{8,12},{12,8},{16,20},{20,16},{24,28},{28,24},{1,5},{5... | collective-permute-start | bytes 6291464 | tf_op jit(solution)/shard_map/ppermute | solution.py:728
  425.1 43.6 %collective-permute-start.26 = (bf16[128,4096]{1,0:T(8,128)(2,1)}, bf16[128,4096]{1,0:T(8,128)(2,1)S(1)}, u32[]{:S(2)}, u32[]{:S(2)}) collective-permute-start(bf16[128,4096]{1,0:T(8,128)(2,1)} %get-tuple-element.243), channel_id=1, source_target_pairs={{0,8},{4,12},{8,0},{12,4},{16,24},{20,28},{24,16},{28,20},{1,9},{5... | collective-permute-start | bytes 3145736 | tf_op jit(solution)/shard_map/ppermute | solution.py:728
  425.7 43.0 %collective-permute-start.27 = (bf16[128,4096]{1,0:T(8,128)(2,1)}, bf16[128,4096]{1,0:T(8,128)(2,1)S(1)}, u32[]{:S(2)}, u32[]{:S(2)}) collective-permute-start(bf16[128,4096]{1,0:T(8,128)(2,1)} %get-tuple-element.244), channel_id=1, source_target_pairs={{0,16},{4,20},{8,24},{12,28},{16,0},{20,4},{24,8},{28,12},{1,17},{... | collective-permute-start | bytes 3145736 | tf_op jit(solution)/shard_map/ppermute | solution.py:728
  434.0 56.6 %collective-permute-start.28 = (bf16[128,4096]{1,0:T(8,128)(2,1)S(1)}, bf16[128,4096]{1,0:T(8,128)(2,1)S(1)}, u32[]{:S(2)}, u32[]{:S(2)}) collective-permute-start(bf16[128,4096]{1,0:T(8,128)(2,1)S(1)} %copy-done.60), channel_id=1, source_target_pairs={{0,24},{4,28},{8,16},{12,20},{16,8},{20,12},{24,0},{28,4},{1,25},{... | collective-permute-start | bytes 3145736 | tf_op jit(solution)/shard_map/ppermute | solution.py:728
  453.0 39.2 %collective-permute-start.25 = (bf16[128,2048]{1,0:T(8,128)(2,1)S(1)}, bf16[128,2048]{1,0:T(8,128)(2,1)S(1)}, u32[]{:S(2)}, u32[]{:S(2)}) collective-permute-start(bf16[128,2048]{1,0:T(8,128)(2,1)S(1)} %get-tuple-element.241), channel_id=1, source_target_pairs={{0,3},{1,0},{2,1},{3,2},{4,7},{5,4},{6,5},{7,6},{8,11},{9,8},{10,9... | collective-permute-start | bytes 1572872 | tf_op jit(solution)/shard_map/ppermute | solution.py:1059
  519.7 26.4 %collective-permute-start.33 = (bf16[128,4096]{1,0:T(8,128)(2,1)}, bf16[128,4096]{1,0:T(8,128)(2,1)}, u32[]{:S(2)}, u32[]{:S(2)}) collective-permute-start(bf16[128,4096]{1,0:T(8,128)(2,1)} %get-tuple-element.259), channel_id=1, source_target_pairs={{0,8},{4,12},{8,0},{12,4},{16,24},{20,28},{24,16},{28,20},{1,9},{5... | collective-permute-start | bytes 3145736 | tf_op jit(solution)/shard_map/ppermute | solution.py:728
  520.9 45.0 %collective-permute-start.34 = (bf16[128,4096]{1,0:T(8,128)(2,1)S(1)}, bf16[128,4096]{1,0:T(8,128)(2,1)}, u32[]{:S(2)}, u32[]{:S(2)}) collective-permute-start(bf16[128,4096]{1,0:T(8,128)(2,1)S(1)} %copy-done.62), channel_id=1, source_target_pairs={{0,16},{4,20},{8,24},{12,28},{16,0},{20,4},{24,8},{28,12},{1,17},{... | collective-permute-start | bytes 3145736 | tf_op jit(solution)/shard_map/ppermute | solution.py:728
  522.4 44.6 %collective-permute-start.35 = (bf16[128,4096]{1,0:T(8,128)(2,1)S(1)}, bf16[128,4096]{1,0:T(8,128)(2,1)}, u32[]{:S(2)}, u32[]{:S(2)}) collective-permute-start(bf16[128,4096]{1,0:T(8,128)(2,1)S(1)} %copy-done.61), channel_id=1, source_target_pairs={{0,24},{4,28},{8,16},{12,20},{16,8},{20,12},{24,0},{28,4},{1,25},{... | collective-permute-start | bytes 3145736 | tf_op jit(solution)/shard_map/ppermute | solution.py:728
  538.7 28.3 %collective-permute-start.32 = (bf16[128,1024]{1,0:T(8,128)(2,1)S(1)}, bf16[128,1024]{1,0:T(8,128)(2,1)S(1)}, u32[]{:S(2)}, u32[]{:S(2)}) collective-permute-start(bf16[128,1024]{1,0:T(8,128)(2,1)S(1)} %add_convert_fusion.17), channel_id=1, source_target_pairs={{0,3},{1,0},{2,1},{3,2},{4,7},{5,4},{6,5},{7,6},{8,11},{9,8},{10,9... | collective-permute-start | bytes 786440 | tf_op jit(solution)/shard_map/ppermute | solution.py:1062
  567.9 76.6 %all-gather.23.cloned.1.call-start = ((), (), s32[]{:S(2)}) async-start(), calls=%async_computation.7 | async-start | bytes 4718592 | tf_op jit(solution)/shard_map/all_gather | solution.py:920
  (92 other events, 1148.6 us)
Sparse Core Ops, SparseCore 0:
  39.3 36.9 all-gather.8
  78.7 54.1 all-gather.10
  135.4 73.3 all-gather.12
  255.1 80.8 all-gather.14
  337.4 79.2 all-gather.18
  418.7 97.6 all-gather.16
  568.0 37.1 all-gather.20
  607.7 36.7 all-gather.22
